TPU v7x, 256 devices: a whole 4x4x8 slice. The times are simulated.
256 devices in a mesh: layer: 32 (over z, y_lo, core), rep: 8 (over y_hi, x).
Axes of the slice: x: 4, y: 4 (y_hi: 2, y_lo: 2; y = y_hi * 2 + y_lo), z: 8, core: 2. Of those that a mesh axis runs over, the one named last changes fastest.
Arguments:
- features: bfloat16 [32768, 512], P(('layer', 'rep')), may hold values from -6 to 6
- block_columns: int32 [256, 128], P('layer', 'rep'), may hold values from -1 to 255, as said below
- block_values: int32 [256, 128, 128, 128], P('layer', 'rep'), may hold values from 0 to 3, as said below
- weight: bfloat16 [512, 512], replicated, may hold values from -1.5 to 1.5
- bias_row: float32 [512], replicated, may hold values from -3 to 3
- cotangent: bfloat16 [32768, 512], P(('layer', 'rep')), may hold values from -6 to 6
Outputs:
- activations: bfloat16 [32768, 512], P(('layer', 'rep'))
- weight_grad: float32 [512, 512], replicated
- bias_grad: float32 [512], replicated
- feature_grad: bfloat16 [32768, 512], P(('layer', 'rep'))
Inputs may be any that keep to these rules, and one draw needn't show every extreme that they name: `block_columns`: in row panel p, slots r*16 to (r+1)*16 - 1 name distinct column blocks in rising order, each inside a span of 128 nodes whose span index is r modulo 8; the used slots come first, at least one in each such group, and the others hold -1. Some group of some row panel uses all 16 slots in every draw. `block_values`: zero in every slot whose column is -1.
All inputs are finite; a program needn't handle non-finite values.
Results may differ from a plain program's by a relative error of at most 0.007.
Values may be sent and summed in bfloat16 or wider, within the bound.
No kernel may reach another device: no remote copies, remote signals or barrier semaphores. Data moves between devices by JAX's collectives and lax.ppermute only.
A program may use at most 128 MiB of HBM per device.

v0:
```python
import functools

import jax
import jax.numpy as jnp
from jax import lax
from jax.experimental import pallas as pl
from jax.experimental.pallas import tpu as pltpu
from jax.sharding import PartitionSpec as P

BF = jnp.bfloat16
F32 = jnp.float32
Z, Y, C = 8, 2, 2
REPS = 8
BLK = 128
SLOTS = 16
F = 512
GROUPS = 8
DEG = 16
ROWS = 800
HALF = 144


def layer_perm(dz, dy, dc):
    pairs = []
    for z in range(Z):
        for y in range(Y):
            for c in range(C):
                to = (((z + dz) % Z) * Y + (y + dy) % Y) * C + (c + dc) % C
                pairs.append(((z * Y + y) * C + c, to))
    return pairs


def core_perm(hops):
    pairs = []
    for z in range(Z):
        for y in range(Y):
            for c in range(C):
                step = hops if c == 0 else -hops
                pairs.append(((z * Y + y) * C + c, (((z + step) % Z) * Y + y) * C + c))
    return pairs


OUT1, OUT2 = core_perm(1), core_perm(2)
BACK1, BACK2 = core_perm(-1), core_perm(-2)
SIDE = layer_perm(0, 1, 0)
CORE = layer_perm(0, 0, 1)

def send(value, perm):
    return lax.ppermute(value, "layer", perm)


def after(value, *earlier):
    return lax.optimization_barrier((value,) + earlier)[0]


def spread_kernel(place_ref, values_ref, dense_ref, degree_ref, tiles, sems):
    panel = pl.program_id(0)

    def fetch(p):
        return pltpu.make_async_copy(values_ref.at[p], tiles.at[p], sems.at[p])

    @pl.when(panel == 0)
    def _():
        for p in range(REPS):
            fetch(p).start()

    dense_ref[...] = jnp.zeros_like(dense_ref)
    fetch(panel).wait()
    total = jnp.zeros((BLK, BLK), jnp.int32)
    for slot in range(SLOTS):
        tile = tiles[panel, slot]
        total = total + tile
        place = place_ref[panel * SLOTS + slot]

        @pl.when(place >= 0)
        def _():
            lane = pl.multiple_of((place % 4) * BLK, BLK)
            dense_ref[place // 4, :, pl.ds(lane, BLK)] = tile.astype(F32).astype(BF)

    row = lax.dot_general(
        jnp.ones((DEG, BLK), BF),
        total.astype(F32).astype(BF),
        (((1,), (1,)), ((), ())),
        preferred_element_type=F32,
    )
    high = jnp.floor(row * (1.0 / 128.0)) * 128.0
    degree_ref[...] = jnp.zeros_like(degree_ref)
    degree_ref[0, :, 0:BLK] = high.astype(BF)
    degree_ref[0, :, BLK : 2 * BLK] = (row - high).astype(BF)


def spread_blocks(place, values):
    panels = values.shape[0]
    return pl.pallas_call(
        spread_kernel,
        grid_spec=pltpu.PrefetchScalarGridSpec(
            num_scalar_prefetch=1,
            grid=(panels,),
            in_specs=[pl.BlockSpec(memory_space=pltpu.HBM)],
            out_specs=[
                pl.BlockSpec((GROUPS, BLK, 4 * BLK), lambda p, place: (0, p, 0)),
                pl.BlockSpec((1, DEG, F), lambda p, place: (p, 0, 0)),
            ],
            scratch_shapes=[
                pltpu.VMEM((panels, SLOTS, BLK, BLK), jnp.int32),
                pltpu.SemaphoreType.DMA((panels,)),
            ],
        ),
        out_shape=[
            jax.ShapeDtypeStruct((GROUPS, panels * BLK, 4 * BLK), BF),
            jax.ShapeDtypeStruct((panels, DEG, F), BF),
        ],
        compiler_params=pltpu.CompilerParams(vmem_limit_bytes=16 << 20),
        cost_estimate=pl.CostEstimate(flops=1 << 22, bytes_accessed=16 << 20, transcendentals=0),
    )(place.reshape(-1), pltpu.with_memory_space_constraint(values, pltpu.HBM))


def payload_kernel(total_ref, dense_ref, last_ref, degree_ref, out_ref):
    product = jnp.dot(dense_ref[0], last_ref[...], preferred_element_type=F32)
    out_ref[0, 0:BLK, :] = (total_ref[...] + product).astype(BF)
    out_ref[0, BLK : BLK + DEG, :] = degree_ref[0]


def payload_of(total, dense, group, last, degree_rows):
    return pl.pallas_call(
        payload_kernel,
        grid=(REPS,),
        in_specs=[
            pl.BlockSpec((BLK, F), lambda p: (p, 0)),
            pl.BlockSpec((1, BLK, 4 * BLK), lambda p: (group, p, 0)),
            pl.BlockSpec((4 * BLK, F), lambda p: (0, 0)),
            pl.BlockSpec((1, DEG, F), lambda p: (p, 0, 0)),
        ],
        out_specs=pl.BlockSpec((1, BLK + DEG, F), lambda p: (p, 0, 0)),
        out_shape=jax.ShapeDtypeStruct((REPS, BLK + DEG, F), BF),
        compiler_params=pltpu.CompilerParams(vmem_limit_bytes=8 << 20),
        cost_estimate=pl.CostEstimate(
            flops=2 * REPS * BLK * 4 * BLK * F, bytes_accessed=5 << 20, transcendentals=0
        ),
    )(total, dense, last, degree_rows)


def node_kernel(
    got_ref, features_ref, weight_ref, bias_ref, cotangent_ref, act_ref, out_ref
):
    got = got_ref[...].astype(F32)
    summed = jnp.sum(got, axis=0)
    parts = summed[BLK : BLK + 1, :]
    degree_row = 1.0 + parts[:, 0:BLK] + parts[:, BLK : 2 * BLK]
    degree = jnp.transpose(jnp.broadcast_to(degree_row, (BLK, BLK)))
    degree = jnp.concatenate([degree] * 4, axis=1)
    aggregate = summed[0:BLK] + features_ref[...].astype(F32)
    hidden_wide = (aggregate / degree).astype(BF)
    weight = weight_ref[...]
    preact = jnp.dot(hidden_wide, weight, preferred_element_type=F32) + bias_ref[...]
    gate = jax.nn.sigmoid(preact)
    act_ref[...] = (preact * gate).astype(BF)
    slope = (cotangent_ref[...].astype(F32) * gate * (1.0 + preact * (1.0 - gate))).astype(BF)
    rows = lax.dot_general(slope, weight, (((1,), (1,)), ((), ())), preferred_element_type=F32)
    scaled = (rows / degree).astype(BF)
    scaled_t = jnp.transpose(scaled.astype(F32)).astype(BF)
    hidden_t = jnp.transpose(hidden_wide.astype(F32)).astype(BF)
    grad = jnp.dot(hidden_t, slope, preferred_element_type=F32).astype(BF)
    bias = jnp.sum(slope.astype(F32), axis=0, keepdims=True).astype(BF)
    out_ref[:, 768:ROWS, :] = jnp.zeros((REPS, 32, BLK), BF)
    for peer in range(REPS):
        out_ref[peer, 0:512, :] = scaled_t
        for b in range(4):
            out_ref[peer, 512 + 64 * b : 576 + 64 * b, :] = grad[
                64 * peer : 64 * peer + 64, BLK * b : BLK * (b + 1)
            ]
            out_ref[peer, 768 + b : 769 + b, :] = bias[:, BLK * b : BLK * (b + 1)]


def node_step(got, features, weight, bias_row, cotangent):
    return pl.pallas_call(
        node_kernel,
        out_shape=[
            jax.ShapeDtypeStruct((BLK, F), BF),
            jax.ShapeDtypeStruct((REPS, ROWS, BLK), BF),
        ],
        compiler_params=pltpu.CompilerParams(vmem_limit_bytes=24 << 20),
        cost_estimate=pl.CostEstimate(
            flops=6 * BLK * F * F, bytes_accessed=4 << 20, transcendentals=BLK * F
        ),
    )(got, features, weight, bias_row.reshape(1, F), cotangent)


def sum_round(grads, c, *earlier):
    own = after(grads.astype(BF), *earlier)
    return send(own, OUT1), send(own, OUT2)


def sum_rest(grads, first, second, c, *earlier):
    second = after(second, *earlier)
    third = send(second, OUT1)
    fourth = send(lax.dynamic_slice_in_dim(second, c * HALF, HALF, 0), OUT2)
    line = first.astype(F32) + second.astype(F32) + third.astype(F32)
    fourth = lax.dynamic_update_slice_in_dim(
        jnp.zeros((2 * HALF, BLK), F32), fourth.astype(F32), c * HALF, 0
    )
    line = line + fourth
    return grads + line + send(line, CORE)


def product_kernel(groups, first, left_ref, dense_ref, *rest):
    step = pl.program_id(0)
    if first:
        wide_ref = rest[-1]

        @pl.when(step == 0)
        def _():
            for p in range(REPS):
                wide_ref[:, BLK * p : BLK * (p + 1)] = left_ref[p]
    else:
        wide_ref = left_ref
    whole = jnp.dot(wide_ref[...], dense_ref[0], preferred_element_type=F32)
    outs = list(rest)
    for index, group in enumerate(groups):
        if group in (0, 7):
            mine, away = outs.pop(0), outs.pop(0)

            @pl.when(step == index)
            def _():
                if group == 7:
                    mine[...] = whole[:, : 2 * BLK]
                    away[...] = whole[:, 2 * BLK :].astype(BF)
                else:
                    for part in (0, 1):
                        own = 2 * part * BLK
                        here = slice(part * BLK, (part + 1) * BLK)
                        mine[:, here] = whole[:, own : own + BLK]
                        away[:, here] = whole[:, own + BLK : own + 2 * BLK].astype(BF)
        else:
            out = outs.pop(0)

            @pl.when(step == index)
            def _():
                out[...] = whole.astype(out.dtype)


def products(left, dense, groups, first):
    shapes = []
    for group in groups:
        if group in (0, 7):
            shapes += [((F, 2 * BLK), F32), ((F, 2 * BLK), BF)]
        else:
            shapes.append(((F, 4 * BLK), F32 if group % 2 else BF))
    if first:
        shapes.append(((F, REPS * BLK), BF))
        left_spec = pl.BlockSpec((REPS, F, BLK), lambda i: (0, 0, 0))
    else:
        left_spec = pl.BlockSpec((F, REPS * BLK), lambda i: (0, 0))
    top = groups[0]
    return pl.pallas_call(
        functools.partial(product_kernel, groups, first),
        grid=(len(groups),),
        in_specs=[
            left_spec,
            pl.BlockSpec((1, REPS * BLK, 4 * BLK), lambda i: (top - i, 0, 0)),
        ],
        out_specs=[pl.BlockSpec(shape, lambda i: (0, 0)) for shape, _ in shapes],
        out_shape=[jax.ShapeDtypeStruct(shape, dtype) for shape, dtype in shapes],
        compiler_params=pltpu.CompilerParams(vmem_limit_bytes=20 << 20),
        cost_estimate=pl.CostEstimate(
            flops=len(groups) * 2 * F * REPS * BLK * 4 * BLK,
            bytes_accessed=len(groups) * (5 << 19),
            transcendentals=0,
        ),
    )(left, dense)


def forward(features, dense, degree_rows):
    def dot(g, piece):
        return jnp.dot(dense[g], piece, preferred_element_type=F32)

    beside = send(features, SIDE)
    chain = jnp.concatenate([features, send(features, CORE)], axis=0)
    second = send(chain, OUT2)
    own = jnp.concatenate([chain, beside, send(beside, CORE)], axis=0)
    first = send(own, OUT1)
    third = send(second, OUT1)
    fourth = send(second[:BLK], OUT2)
    both2 = jnp.concatenate([second, send(second, SIDE)], axis=0)
    cross2 = send(both2, CORE)
    cross1 = send(first, CORE)
    both3 = jnp.concatenate([third, send(third, SIDE)], axis=0)
    both4 = jnp.concatenate([fourth, send(fourth, SIDE)], axis=0)
    total = dot(0, own) + dot(1, first) + dot(3, both2)
    both3 = after(both3, total)
    cross3 = send(both3, CORE)
    total = total + dot(4, cross2) + dot(2, cross1) + dot(5, both3)
    both4 = after(both4, total)
    last = jnp.concatenate([both4, send(both4, CORE)], axis=0)
    total = total + dot(6, cross3)
    return payload_of(total, dense, 7, last, degree_rows)


def final_kernel(mine_ref, far_ref, near_ref, other_ref, scaled_ref, out_ref):
    total = (
        mine_ref[...]
        + far_ref[:, :BLK].astype(F32)
        + near_ref[:, :BLK].astype(F32)
        + other_ref[...].astype(F32)
        + scaled_ref[0, :F].astype(F32)
    )
    out_ref[...] = jnp.transpose(total).astype(BF)


def final_step(mine, far, near, other, outgoing):
    return pl.pallas_call(
        final_kernel,
        grid=(1,),
        in_specs=[
            pl.BlockSpec((F, BLK), lambda i: (0, 0)),
            pl.BlockSpec((F, 2 * BLK), lambda i: (0, 0)),
            pl.BlockSpec((F, 2 * BLK), lambda i: (0, 0)),
            pl.BlockSpec((F, BLK), lambda i: (0, 0)),
            pl.BlockSpec((1, F, BLK), lambda i: (0, 0, 0)),
        ],
        out_specs=pl.BlockSpec((BLK, F), lambda i: (0, 0)),
        out_shape=jax.ShapeDtypeStruct((BLK, F), BF),
        compiler_params=pltpu.CompilerParams(vmem_limit_bytes=8 << 20),
        cost_estimate=pl.CostEstimate(flops=1 << 19, bytes_accessed=1 << 20, transcendentals=0),
    )(mine, far, near, other, outgoing)


def gradient_kernel(pieces_ref, out_ref):
    for peer in range(REPS):
        for b in range(4):
            out_ref[64 * peer : 64 * peer + 64, BLK * b : BLK * (b + 1)] = pieces_ref[
                peer, 64 * b : 64 * b + 64
            ].astype(F32)


def gradient_of(pieces):
    return pl.pallas_call(
        gradient_kernel,
        out_shape=jax.ShapeDtypeStruct((F, F), F32),
        compiler_params=pltpu.CompilerParams(vmem_limit_bytes=8 << 20),
        cost_estimate=pl.CostEstimate(flops=1 << 18, bytes_accessed=3 << 19, transcendentals=0),
    )(pieces)


def backward(outgoing, everyone, dense, c):
    def over_core(mine, away):
        return mine + send(away, CORE).astype(F32)

    def cut(line):
        width = line.shape[1] // 2
        return line[:, :width], line[:, width:].astype(BF)

    grads = jnp.sum(everyone[:, F:].astype(F32), axis=0)
    grads = grads + send(grads.astype(BF), CORE).astype(F32)
    mine4, away4, away3, mine3, wide = products(everyone, dense, (7, 6, 5), True)
    grads = grads + send(grads.astype(BF), SIDE).astype(F32)
    line4, side4 = cut(over_core(mine4, away4))
    away2, mine2 = products(wide, dense, (4, 3), False)
    line3, side3 = cut(over_core(mine3, away3))
    wide = after(wide, side3, side4)
    away1, mine1, mine0, away0 = products(wide, dense, (2, 1, 0), False)
    grad1, grad2 = sum_round(grads, c, side3, side4)
    line2, side2 = cut(over_core(mine2, away2))
    quad4 = line4 + send(side4, SIDE).astype(F32)
    quad3 = line3 + send(side3, SIDE).astype(F32)
    line1, side1 = cut(over_core(mine1, away1))
    line0, side0 = cut(over_core(mine0, away0))
    away4 = quad4.astype(BF)
    away3 = quad3.astype(BF)
    grads = sum_rest(grads, grad1, grad2, c, away4, away3)
    came4 = send(away4, BACK2).astype(F32)
    came3 = send(away3, BACK1).astype(F32)
    quad2 = line2 + send(side2, SIDE).astype(F32) + came3
    quad1 = line1 + send(side1, SIDE).astype(F32)
    quad0 = line0 + send(side0, SIDE).astype(F32)
    quad2 = jnp.concatenate([quad2[:, :BLK] + came4, quad2[:, BLK:]], axis=1)
    near = send(quad1.astype(BF), BACK1)
    far = send(quad2.astype(BF), BACK2)
    other = send((near[:, BLK:].astype(F32) + far[:, BLK:].astype(F32)).astype(BF), CORE)
    return final_step(quad0, far, near, other, outgoing), grads


def per_device(features, block_columns, block_values, weight, bias_row, cotangent):
    layer = lax.axis_index("layer")
    z, y, c = layer // 4, (layer // 2) % 2, layer % 2
    owner = jnp.where(block_columns >= 0, block_columns, 0) // REPS
    dz = (owner // 4 - z + Z) % Z
    dy = ((owner // 2) % 2 - y) % 2
    dc = (owner % 2 - c) % 2
    near = jnp.where(dz <= 4, dz, Z - dz)
    other = ((dz > 4) != (c == 0)).astype(jnp.int32)
    ends = (near == 0) | (near == 4)
    group = jnp.where(near == 0, 0, jnp.where(near == 4, 7, 2 * near - 1 + other))
    column = jnp.where(near == 4, 2 * dc + dy, 2 * dy + jnp.where(ends, dc, dc ^ other))
    place = jnp.where(block_columns >= 0, 4 * group + column, -1).astype(jnp.int32)
    dense, degree_rows = spread_blocks(place, block_values)
    payload = forward(features, dense, degree_rows)
    got = lax.all_to_all(payload, "rep", 0, 0, tiled=True)

    activations, outgoing = node_step(got, features, weight, bias_row, cotangent)
    everyone = lax.all_to_all(outgoing, "rep", 0, 0, tiled=True)
    feature_grad, grads = backward(outgoing, everyone, dense, c)
    bias_grad = grads[256:260].reshape(F)
    mine = jnp.broadcast_to(grads[:256].astype(BF)[None], (REPS, 256, BLK))
    pieces = lax.all_to_all(mine, "rep", 0, 0, tiled=True)
    weight_grad = gradient_of(pieces)
    return (activations, weight_grad, bias_grad, feature_grad)


def solution(mesh):
    in_specs = (
        P(("layer", "rep"), None),
        P("layer", "rep"),
        P("layer", "rep", None, None),
        P(),
        P(),
        P(("layer", "rep"), None),
    )
    out_specs = (P(("layer", "rep"), None), P(), P(), P(("layer", "rep"), None))
    return jax.shard_map(
        per_device, mesh=mesh, in_specs=in_specs, out_specs=out_specs, check_vma=False
    )
```

profile of v0, /device:TPU:1, one launch (start us, length us, event | category | flops | bytes accessed | tf_op | source)
XLA Modules:
  0.0 174.0 jit_solution(8027955889115179781)
XLA Ops:
  0.6 3.3 %collective-permute-start = (bf16[128,512]{1,0:T(8,128)(2,1)}, bf16[128,512]{1,0:T(8,128)(2,1)S(1)}, u32[]{:S(2)}, u32[]{:S(2)}) collective-permute-start(bf16[128,512]{1,0:T(8,128)(2,1)} %features_ref.1), channel_id=1, source_target_pairs={{0,8},{8,0},{16,24},{24,16},{32,40},{40,32},{48,56},{56,48},{64,72... | collective-permute-start | bytes 393224 | tf_op jit(solution)/shard_map/ppermute | solution.py:49
  4.0 0.7 compare_select_fusion.1
  4.7 0.9 constant_dynamic-update-slice_fusion.3
  5.7 5.9 %shard_map.93 = (bf16[8,1024,512]{2,1,0:T(8,128)(2,1)S(1)}, bf16[8,16,512]{2,1,0:T(8,128)(2,1)S(1)}) custom-call(s32[128]{0:T(128)S(1)} %reshape.18.place_ref, s32[8,16,128,128]{3,2,1,0:T(8,128)} %values_ref.1), custom_call_target="tpu_custom_call" | custom-call | flops 4194304 | bytes 16777216 | tf_op jit(solution)/shard_map/pallas_call | solution.py:94
  11.7 5.6 %collective-permute-start.4 = (bf16[256,512]{1,0:T(8,128)(2,1)S(1)}, bf16[256,512]{1,0:T(8,128)(2,1)S(1)}, u32[]{:S(2)}, u32[]{:S(2)}) collective-permute-start(bf16[256,512]{1,0:T(8,128)(2,1)S(1)} %pad_maximum_fusion.2), channel_id=1, source_target_pairs={{0,64},{8,200},{16,80},{24,216},{32,96},{40,232},{48,112},{56,248}... | collective-permute-start | bytes 786440 | tf_op jit(solution)/shard_map/ppermute | solution.py:49
  17.3 1.3 collective-permute-done.2
  18.7 1.1 collective-permute-start.3
  19.8 3.6 %collective-permute-done.4 = bf16[256,512]{1,0:T(8,128)(2,1)S(1)} collective-permute-done((bf16[256,512]{1,0:T(8,128)(2,1)S(1)}, bf16[256,512]{1,0:T(8,128)(2,1)S(1)}, u32[]{:S(2)}, u32[]{:S(2)}) %collective-permute-start.4) | collective-permute-done | bytes 262176 | tf_op jit(solution)/shard_map/ppermute | solution.py:49
  23.4 4.2 %collective-permute-start.11 = (bf16[128,512]{1,0:T(8,128)(2,1)S(1)}, bf16[128,512]{1,0:T(8,128)(2,1)S(1)}, u32[]{:S(2)}, u32[]{:S(2)}) collective-permute-start(bf16[128,512]{1,0:T(8,128)(2,1)S(1)} %slice.107), channel_id=1, source_target_pairs={{0,64},{8,200},{16,80},{24,216},{32,96},{40,232},{48,112},{56,248}... | collective-permute-start | bytes 393224 | tf_op jit(solution)/shard_map/ppermute | solution.py:49
  28.9 2.9 %collective-permute-done.11 = bf16[128,512]{1,0:T(8,128)(2,1)S(1)} collective-permute-done((bf16[128,512]{1,0:T(8,128)(2,1)S(1)}, bf16[128,512]{1,0:T(8,128)(2,1)S(1)}, u32[]{:S(2)}, u32[]{:S(2)}) %collective-permute-start.11) | collective-permute-done | bytes 131104 | tf_op jit(solution)/shard_map/ppermute | solution.py:49
  31.9 4.0 %collective-permute-done.5 = bf16[256,512]{1,0:T(8,128)(2,1)S(1)} collective-permute-done((bf16[256,512]{1,0:T(8,128)(2,1)S(1)}, bf16[256,512]{1,0:T(8,128)(2,1)S(1)}, u32[]{:S(2)}, u32[]{:S(2)}) %collective-permute-start.5) | collective-permute-done | bytes 262176 | tf_op jit(solution)/shard_map/ppermute | solution.py:49
  36.4 2.3 %collective-permute-done.12 = bf16[128,512]{1,0:T(8,128)(2,1)S(1)} collective-permute-done((bf16[128,512]{1,0:T(8,128)(2,1)S(1)}, bf16[128,512]{1,0:T(8,128)(2,1)S(1)}, u32[]{:S(2)}, u32[]{:S(2)}) %collective-permute-start.12) | collective-permute-done | bytes 131104 | tf_op jit(solution)/shard_map/ppermute | solution.py:49
  40.7 3.4 %collective-permute-done.9 = bf16[256,512]{1,0:T(8,128)(2,1)S(1)} collective-permute-done((bf16[256,512]{1,0:T(8,128)(2,1)S(1)}, bf16[256,512]{1,0:T(8,128)(2,1)S(1)}, u32[]{:S(2)}, u32[]{:S(2)}) %collective-permute-start.9) | collective-permute-done | bytes 262176 | tf_op jit(solution)/shard_map/ppermute | solution.py:49
  44.1 1.1 collective-permute-start.10
  46.6 0.8 add_add_fusion
  48.4 0.8 collective-permute-done.13
  49.3 1.9 %shard_map.94 = bf16[8,144,512]{2,1,0:T(8,128)(2,1)S(1)} custom-call(f32[1024,512]{1,0:T(8,128)S(1)} %convolution_add_fusion.total_ref, bf16[8,1024,512]{2,1,0:T(8,128)(2,1)S(1)} %get-tuple-element.24.dense_ref, bf16[512,512]{1,0:T(8,128)(2,1)S(1)} %pad_maximum_fusion.1.last_ref, bf16[8,16,512]{2,1,0:T(8,128)(2,1)S(1)} %get-tuple-element.27.degree_ref), custom_call_target="tpu_custom_call" | custom-call | flops 536870912 | bytes 5242880 | tf_op jit(solution)/shard_map/pallas_call | solution.py:125
  51.3 24.9 %all_to_all.15.got_ref = bf16[8,144,512]{2,1,0:T(8,128)(2,1)S(1)} all-to-all(bf16[8,144,512]{2,1,0:T(8,128)(2,1)S(1)} %shard_map.94), channel_id=1, replica_groups=mesh['layer'=32,'rep'=8] {'rep'}, dimensions={0} | all-to-all | bytes 2359296 | tf_op jit(solution)/shard_map/all_to_all | solution.py:398
  76.2 1.9 %shard_map.95 = (bf16[128,512]{1,0:T(8,128)(2,1)}, bf16[8,800,128]{2,1,0:T(8,128)(2,1)}) custom-call(bf16[8,144,512]{2,1,0:T(8,128)(2,1)S(1)} %all_to_all.15.got_ref, bf16[128,512]{1,0:T(8,128)(2,1)S(1)} %copy-done.2, bf16[512,512]{1,0:T(8,128)(2,1)S(1)} %copy-done.3, f32[1,512]{1,0:T(1,128)S(1)} %bitcast.33, bf16[128,512]{1,0:T(8,128)(2,1)S(1)} %copy-done.4), custom_call_target="tpu_custom_call" | custom-call | flops 201326592 | bytes 4194304 | tf_op jit(solution)/shard_map/pallas_call | solution.py:176
  78.0 3.6 %all-to-all-start.1 = ((bf16[8,800,128]{2,1,0:T(8,128)(2,1)}), bf16[8,800,128]{2,1,0:T(8,128)(2,1)S(1)}, u32[]{:S(2)}, u32[]{:S(2)}) async-start(bf16[8,800,128]{2,1,0:T(8,128)(2,1)} %get-tuple-element.29.scaled_ref), calls=%async_computation.1 | async-start | bytes 3276800 | tf_op jit(solution)/shard_map/all_to_all | solution.py:401
  81.6 23.6 %all-to-all-done.1.left_ref = bf16[8,800,128]{2,1,0:T(8,128)(2,1)S(1)} async-done(((bf16[8,800,128]{2,1,0:T(8,128)(2,1)}), bf16[8,800,128]{2,1,0:T(8,128)(2,1)S(1)}, u32[]{:S(2)}, u32[]{:S(2)}) %all-to-all-start.1) | async-done | bytes 1638432 | tf_op jit(solution)/shard_map/all_to_all | solution.py:401
  105.3 0.9 collective-permute-start.14
  106.2 3.4 %copy-done.1 = bf16[8,1024,512]{2,1,0:T(8,128)(2,1)S(1)} copy-done((bf16[8,1024,512]{2,1,0:T(8,128)(2,1)S(1)}, bf16[8,1024,512]{2,1,0:T(8,128)(2,1)}, u32[]{:S(2)}) %copy-start.1) | copy-done | bytes 8388632
  109.6 2.7 %shard_map.96 = (f32[512,256]{1,0:T(8,128)S(1)}, bf16[512,256]{1,0:T(8,128)(2,1)S(1)}, bf16[512,512]{1,0:T(8,128)(2,1)S(1)}, f32[512,512]{1,0:T(8,128)S(1)}, bf16[512,1024]{1,0:T(8,128)(2,1)S(1)}) custom-call(bf16[8,800,128]{2,1,0:T(8,128)(2,1)S(1)} %all-to-all-done.1.left_ref, bf16[8,1024,512]{2,1,0:T(8,128)(2,1)S(1)} %copy-done.1), custom_call_target="tpu_custom_call" | custom-call | flops 1610612736 | bytes 7864320 | tf_op jit(solution)/shard_map/pallas_call | solution.py:255
  112.9 1.6 shard_map.99
  114.9 1.5 collective-permute-start.20
  116.4 1.6 collective-permute-done.15
  118.0 3.0 %collective-permute-done.20 = bf16[512,128]{1,0:T(8,128)(2,1)S(1)} collective-permute-done((bf16[512,128]{1,0:T(8,128)(2,1)S(1)}, bf16[512,128]{1,0:T(8,128)(2,1)S(1)}, u32[]{:S(2)}, u32[]{:S(2)}) %collective-permute-start.20) | collective-permute-done | bytes 131104 | tf_op jit(solution)/shard_map/ppermute | solution.py:49
  121.1 1.6 collective-permute-start.30
  123.0 2.1 %collective-permute-start.19 = (bf16[288,128]{1,0:T(8,128)(2,1)S(1)}, bf16[288,128]{1,0:T(8,128)(2,1)S(1)}, u32[]{:S(2)}, u32[]{:S(2)}) collective-permute-start(bf16[288,128]{1,0:T(8,128)(2,1)S(1)} %fusion.27), channel_id=1, source_target_pairs={{0,64},{8,200},{16,80},{24,216},{32,96},{40,232},{48,112},{56,248}... | collective-permute-start | bytes 221192 | tf_op jit(solution)/shard_map/ppermute | solution.py:49
  125.1 1.8 %collective-permute-start.18 = (bf16[288,128]{1,0:T(8,128)(2,1)S(1)}, bf16[288,128]{1,0:T(8,128)(2,1)S(1)}, u32[]{:S(2)}, u32[]{:S(2)}) collective-permute-start(bf16[288,128]{1,0:T(8,128)(2,1)S(1)} %fusion.27), channel_id=1, source_target_pairs={{0,32},{8,232},{16,48},{24,248},{32,64},{40,8},{48,80},{56,24},{64... | collective-permute-start | bytes 221192 | tf_op jit(solution)/shard_map/ppermute | solution.py:49
  126.9 2.4 %shard_map.98 = (bf16[512,512]{1,0:T(8,128)(2,1)S(1)}, f32[512,512]{1,0:T(8,128)S(1)}, f32[512,256]{1,0:T(8,128)S(1)}, bf16[512,256]{1,0:T(8,128)(2,1)S(1)}) custom-call(bf16[512,1024]{1,0:T(8,128)(2,1)S(1)} %get-tuple-element.37.left_ref, bf16[8,1024,512]{2,1,0:T(8,128)(2,1)S(1)} %copy-done.1), custom_call_target="tpu_custom_call" | custom-call | flops 1610612736 | bytes 7864320 | tf_op jit(solution)/shard_map/pallas_call | solution.py:255
  129.3 2.5 %collective-permute-start.25 = (bf16[512,256]{1,0:T(8,128)(2,1)S(1)}, bf16[512,256]{1,0:T(8,128)(2,1)S(1)}, u32[]{:S(2)}, u32[]{:S(2)}) collective-permute-start(bf16[512,256]{1,0:T(8,128)(2,1)S(1)} %get-tuple-element.39), channel_id=1, source_target_pairs={{0,8},{8,0},{16,24},{24,16},{32,40},{40,32},{48,56},{56,48},{64,72... | collective-permute-start | bytes 786440 | tf_op jit(solution)/shard_map/ppermute | solution.py:49
  132.0 1.3 collective-permute-start.28
  133.8 0.9 collective-permute-start.22
  135.5 1.8 %collective-permute-done.22 = bf16[288,128]{1,0:T(8,128)(2,1)S(1)} collective-permute-done((bf16[288,128]{1,0:T(8,128)(2,1)S(1)}, bf16[288,128]{1,0:T(8,128)(2,1)S(1)}, u32[]{:S(2)}, u32[]{:S(2)}) %collective-permute-start.22) | collective-permute-done | bytes 73760 | tf_op jit(solution)/shard_map/ppermute | solution.py:49
  137.3 0.9 collective-permute-start.23
  138.3 3.6 %collective-permute-done.23 = bf16[144,128]{1,0:T(8,128)(2,1)S(1)} collective-permute-done((bf16[144,128]{1,0:T(8,128)(2,1)S(1)}, bf16[144,128]{1,0:T(8,128)(2,1)S(1)}, u32[]{:S(2)}, u32[]{:S(2)}) %collective-permute-start.23) | collective-permute-done | bytes 36896 | tf_op jit(solution)/shard_map/ppermute | solution.py:49
  141.9 4.7 %collective-permute-start.24 = (f32[288,128]{1,0:T(8,128)S(1)}, f32[288,128]{1,0:T(8,128)S(1)}, u32[]{:S(2)}, u32[]{:S(2)}) collective-permute-start(f32[288,128]{1,0:T(8,128)S(1)} %add_dynamic-update-slice_fusion), channel_id=1, source_target_pairs={{0,8},{8,0},{16,24},{24,16},{32,40},{40,32},{48,56},{56,48},{64,72... | collective-permute-start | bytes 442376 | tf_op jit(solution)/shard_map/ppermute | solution.py:49
  146.8 1.6 collective-permute-start.33
  148.7 6.5 %collective-permute-done.33 = bf16[512,256]{1,0:T(8,128)(2,1)S(1)} collective-permute-done((bf16[512,256]{1,0:T(8,128)(2,1)S(1)}, bf16[512,256]{1,0:T(8,128)(2,1)S(1)}, u32[]{:S(2)}, u32[]{:S(2)}) %collective-permute-start.33) | collective-permute-done | bytes 262176 | tf_op jit(solution)/shard_map/ppermute | solution.py:49
  155.5 0.9 broadcast_in_dim.8
  156.4 3.5 %all-to-all-start.2 = ((bf16[8,256,128]{2,1,0:T(8,128)(2,1)}), bf16[8,256,128]{2,1,0:T(8,128)(2,1)S(1)}, u32[]{:S(2)}, u32[]{:S(2)}) async-start(bf16[8,256,128]{2,1,0:T(8,128)(2,1)} %broadcast_in_dim.8), calls=%async_computation.2 | async-start | bytes 1048576 | tf_op jit(solution)/shard_map/all_to_all | solution.py:405
  159.9 1.9 %collective-permute-done.34.near_ref = bf16[512,256]{1,0:T(8,128)(2,1)S(1)} collective-permute-done((bf16[512,256]{1,0:T(8,128)(2,1)S(1)}, bf16[512,256]{1,0:T(8,128)(2,1)S(1)}, u32[]{:S(2)}, u32[]{:S(2)}) %collective-permute-start.34) | collective-permute-done | bytes 262176 | tf_op jit(solution)/shard_map/ppermute | solution.py:49
  161.9 1.6 collective-permute-start.35
  164.1 7.2 %all-to-all-done.2.pieces_ref = bf16[8,256,128]{2,1,0:T(8,128)(2,1)S(1)} async-done(((bf16[8,256,128]{2,1,0:T(8,128)(2,1)}), bf16[8,256,128]{2,1,0:T(8,128)(2,1)S(1)}, u32[]{:S(2)}, u32[]{:S(2)}) %all-to-all-start.2) | async-done | bytes 524320 | tf_op jit(solution)/shard_map/all_to_all | solution.py:405
  171.3 1.0 shard_map.97
  172.3 1.7 shard_map.100
  (99 shorter events, 10.7 us)
Async XLA Ops:
  0.6 11.0 %collective-permute-start = (bf16[128,512]{1,0:T(8,128)(2,1)}, bf16[128,512]{1,0:T(8,128)(2,1)S(1)}, u32[]{:S(2)}, u32[]{:S(2)}) collective-permute-start(bf16[128,512]{1,0:T(8,128)(2,1)} %features_ref.1), channel_id=1, source_target_pairs={{0,8},{8,0},{16,24},{24,16},{32,40},{40,32},{48,56},{56,48},{64,72... | collective-permute-start | bytes 393224 | tf_op jit(solution)/shard_map/ppermute | solution.py:49
  4.0 13.3 %collective-permute-start.1 = (bf16[128,512]{1,0:T(8,128)(2,1)}, bf16[128,512]{1,0:T(8,128)(2,1)S(1)}, u32[]{:S(2)}, u32[]{:S(2)}) collective-permute-start(bf16[128,512]{1,0:T(8,128)(2,1)} %features_ref.1), channel_id=1, source_target_pairs={{0,16},{8,24},{16,0},{24,8},{32,48},{40,56},{48,32},{56,40},{64,80... | collective-permute-start | bytes 393224 | tf_op jit(solution)/shard_map/ppermute | solution.py:49
  5.7 5.9 %copy-start.2 = (bf16[128,512]{1,0:T(8,128)(2,1)S(1)}, bf16[128,512]{1,0:T(8,128)(2,1)}, u32[]{:S(2)}) copy-start(bf16[128,512]{1,0:T(8,128)(2,1)} %features_ref.1) | copy-start | bytes 393220
  11.6 37.7 %copy-start = (bf16[8,1024,512]{2,1,0:T(8,128)(2,1)}, bf16[8,1024,512]{2,1,0:T(8,128)(2,1)S(1)}, u32[]{:S(2)}) copy-start(bf16[8,1024,512]{2,1,0:T(8,128)(2,1)S(1)} %get-tuple-element.24.dense_ref) | copy-start | bytes 25165828
  11.7 11.8 %collective-permute-start.4 = (bf16[256,512]{1,0:T(8,128)(2,1)S(1)}, bf16[256,512]{1,0:T(8,128)(2,1)S(1)}, u32[]{:S(2)}, u32[]{:S(2)}) collective-permute-start(bf16[256,512]{1,0:T(8,128)(2,1)S(1)} %pad_maximum_fusion.2), channel_id=1, source_target_pairs={{0,64},{8,200},{16,80},{24,216},{32,96},{40,232},{48,112},{56,248}... | collective-permute-start | bytes 786440 | tf_op jit(solution)/shard_map/ppermute | solution.py:49
  17.3 1.3 collective-permute-start.2
  18.7 20.0 %collective-permute-start.3 = (bf16[512,512]{1,0:T(8,128)(2,1)S(1)}, bf16[512,512]{1,0:T(8,128)(2,1)S(1)}, u32[]{:S(2)}, u32[]{:S(2)}) collective-permute-start(bf16[512,512]{1,0:T(8,128)(2,1)S(1)} %constant_dynamic-update-slice_fusion), channel_id=1, source_target_pairs={{0,32},{8,232},{16,48},{24,248},{32,64},{40,8},{48,80},{56,24},{64... | collective-permute-start | bytes 1572872 | tf_op jit(solution)/shard_map/ppermute | solution.py:49
  23.4 8.4 %collective-permute-start.11 = (bf16[128,512]{1,0:T(8,128)(2,1)S(1)}, bf16[128,512]{1,0:T(8,128)(2,1)S(1)}, u32[]{:S(2)}, u32[]{:S(2)}) collective-permute-start(bf16[128,512]{1,0:T(8,128)(2,1)S(1)} %slice.107), channel_id=1, source_target_pairs={{0,64},{8,200},{16,80},{24,216},{32,96},{40,232},{48,112},{56,248}... | collective-permute-start | bytes 393224 | tf_op jit(solution)/shard_map/ppermute | solution.py:49
  27.6 8.7 %collective-permute-start.8 = (bf16[256,512]{1,0:T(8,128)(2,1)S(1)}, bf16[256,512]{1,0:T(8,128)(2,1)S(1)}, u32[]{:S(2)}, u32[]{:S(2)}) collective-permute-start(bf16[256,512]{1,0:T(8,128)(2,1)S(1)} %collective-permute-done.4), channel_id=1, source_target_pairs={{0,32},{8,232},{16,48},{24,248},{32,64},{40,8},{48,80},{56,24},{64... | collective-permute-start | bytes 786440 | tf_op jit(solution)/shard_map/ppermute | solution.py:49
  27.6 8.3 %collective-permute-start.5 = (bf16[256,512]{1,0:T(8,128)(2,1)S(1)}, bf16[256,512]{1,0:T(8,128)(2,1)S(1)}, u32[]{:S(2)}, u32[]{:S(2)}) collective-permute-start(bf16[256,512]{1,0:T(8,128)(2,1)S(1)} %collective-permute-done.4), channel_id=1, source_target_pairs={{0,16},{8,24},{16,0},{24,8},{32,48},{40,56},{48,32},{56,40},{64,80... | collective-permute-start | bytes 786440 | tf_op jit(solution)/shard_map/ppermute | solution.py:49
  31.8 6.8 %collective-permute-start.12 = (bf16[128,512]{1,0:T(8,128)(2,1)S(1)}, bf16[128,512]{1,0:T(8,128)(2,1)S(1)}, u32[]{:S(2)}, u32[]{:S(2)}) collective-permute-start(bf16[128,512]{1,0:T(8,128)(2,1)S(1)} %collective-permute-done.11), channel_id=1, source_target_pairs={{0,16},{8,24},{16,0},{24,8},{32,48},{40,56},{48,32},{56,40},{64,80... | collective-permute-start | bytes 393224 | tf_op jit(solution)/shard_map/ppermute | solution.py:49
  35.9 10.0 %collective-permute-start.6 = (bf16[512,512]{1,0:T(8,128)(2,1)S(1)}, bf16[512,512]{1,0:T(8,128)(2,1)S(1)}, u32[]{:S(2)}, u32[]{:S(2)}) collective-permute-start(bf16[512,512]{1,0:T(8,128)(2,1)S(1)} %constant_dynamic-update-slice_fusion.4), channel_id=1, source_target_pairs={{0,8},{8,0},{16,24},{24,16},{32,40},{40,32},{48,56},{56,48},{64,72... | collective-permute-start | bytes 1572872 | tf_op jit(solution)/shard_map/ppermute | solution.py:49
  36.3 7.7 %collective-permute-start.9 = (bf16[256,512]{1,0:T(8,128)(2,1)S(1)}, bf16[256,512]{1,0:T(8,128)(2,1)S(1)}, u32[]{:S(2)}, u32[]{:S(2)}) collective-permute-start(bf16[256,512]{1,0:T(8,128)(2,1)S(1)} %collective-permute-done.8), channel_id=1, source_target_pairs={{0,16},{8,24},{16,0},{24,8},{32,48},{40,56},{48,32},{56,40},{64,80... | collective-permute-start | bytes 786440 | tf_op jit(solution)/shard_map/ppermute | solution.py:49
  40.1 6.5 %collective-permute-start.7 = (bf16[512,512]{1,0:T(8,128)(2,1)S(1)}, bf16[512,512]{1,0:T(8,128)(2,1)S(1)}, u32[]{:S(2)}, u32[]{:S(2)}) collective-permute-start(bf16[512,512]{1,0:T(8,128)(2,1)S(1)} %collective-permute-done.3), channel_id=1, source_target_pairs={{0,8},{8,0},{16,24},{24,16},{32,40},{40,32},{48,56},{56,48},{64,72... | collective-permute-start | bytes 1572872 | tf_op jit(solution)/shard_map/ppermute | solution.py:49
  44.1 3.6 %collective-permute-start.10 = (bf16[512,512]{1,0:T(8,128)(2,1)S(1)}, bf16[512,512]{1,0:T(8,128)(2,1)S(1)}, u32[]{:S(2)}, u32[]{:S(2)}) collective-permute-start(bf16[512,512]{1,0:T(8,128)(2,1)S(1)} %pad_maximum_fusion), channel_id=1, source_target_pairs={{0,8},{8,0},{16,24},{24,16},{32,40},{40,32},{48,56},{56,48},{64,72... | collective-permute-start | bytes 1572872 | tf_op jit(solution)/shard_map/ppermute | solution.py:49
  47.4 1.8 %collective-permute-start.13 = (bf16[256,512]{1,0:T(8,128)(2,1)S(1)}, bf16[256,512]{1,0:T(8,128)(2,1)S(1)}, u32[]{:S(2)}, u32[]{:S(2)}) collective-permute-start(bf16[256,512]{1,0:T(8,128)(2,1)S(1)} %pad_maximum_fusion.3), channel_id=1, source_target_pairs={{0,8},{8,0},{16,24},{24,16},{32,40},{40,32},{48,56},{56,48},{64,72... | collective-permute-start | bytes 786440 | tf_op jit(solution)/shard_map/ppermute | solution.py:49
  51.2 24.9 %copy-start.3 = (bf16[512,512]{1,0:T(8,128)(2,1)S(1)}, bf16[512,512]{1,0:T(8,128)(2,1)}, u32[]{:S(2)}) copy-start(bf16[512,512]{1,0:T(8,128)(2,1)} %weight_ref.1) | copy-start | bytes 1572868
  51.2 24.9 %copy-start.4 = (bf16[128,512]{1,0:T(8,128)(2,1)S(1)}, bf16[128,512]{1,0:T(8,128)(2,1)}, u32[]{:S(2)}) copy-start(bf16[128,512]{1,0:T(8,128)(2,1)} %cotangent_ref.1) | copy-start | bytes 393220
  51.3 24.9 %copy-start.5 = (f32[512]{0:T(512)S(1)}, f32[512]{0:T(512)}, u32[]{:S(2)}) copy-start(f32[512]{0:T(512)} %param.10) | copy-start | bytes 6148
  78.0 27.2 %all-to-all-start.1 = ((bf16[8,800,128]{2,1,0:T(8,128)(2,1)}), bf16[8,800,128]{2,1,0:T(8,128)(2,1)S(1)}, u32[]{:S(2)}, u32[]{:S(2)}) async-start(bf16[8,800,128]{2,1,0:T(8,128)(2,1)} %get-tuple-element.29.scaled_ref), calls=%async_computation.1 | async-start | bytes 3276800 | tf_op jit(solution)/shard_map/all_to_all | solution.py:401
  105.3 9.4 %collective-permute-start.14 = (bf16[288,128]{1,0:T(8,128)(2,1)S(1)}, bf16[288,128]{1,0:T(8,128)(2,1)S(1)}, u32[]{:S(2)}, u32[]{:S(2)}) collective-permute-start(bf16[288,128]{1,0:T(8,128)(2,1)S(1)} %convert_element_type.96), channel_id=1, source_target_pairs={{0,8},{8,0},{16,24},{24,16},{32,40},{40,32},{48,56},{56,48},{64,72... | collective-permute-start | bytes 221192 | tf_op jit(solution)/shard_map/ppermute | solution.py:49
  106.2 3.4 %copy-start.1 = (bf16[8,1024,512]{2,1,0:T(8,128)(2,1)S(1)}, bf16[8,1024,512]{2,1,0:T(8,128)(2,1)}, u32[]{:S(2)}) copy-start(bf16[8,1024,512]{2,1,0:T(8,128)(2,1)} %copy-done) | copy-start | bytes 25165828
  112.3 10.4 %collective-permute-start.16 = (bf16[512,512]{1,0:T(8,128)(2,1)S(1)}, bf16[512,512]{1,0:T(8,128)(2,1)S(1)}, u32[]{:S(2)}, u32[]{:S(2)}) collective-permute-start(bf16[512,512]{1,0:T(8,128)(2,1)S(1)} %get-tuple-element.31), channel_id=1, source_target_pairs={{0,8},{8,0},{16,24},{24,16},{32,40},{40,32},{48,56},{56,48},{64,72... | collective-permute-start | bytes 1572872 | tf_op jit(solution)/shard_map/ppermute | solution.py:49
  112.4 2.4 %collective-permute-start.17 = (bf16[512,256]{1,0:T(8,128)(2,1)S(1)}, bf16[512,256]{1,0:T(8,128)(2,1)S(1)}, u32[]{:S(2)}, u32[]{:S(2)}) collective-permute-start(bf16[512,256]{1,0:T(8,128)(2,1)S(1)} %get-tuple-element.33), channel_id=1, source_target_pairs={{0,8},{8,0},{16,24},{24,16},{32,40},{40,32},{48,56},{56,48},{64,72... | collective-permute-start | bytes 786440 | tf_op jit(solution)/shard_map/ppermute | solution.py:49
  114.5 14.8 %collective-permute-start.27 = (bf16[512,512]{1,0:T(8,128)(2,1)S(1)}, bf16[512,512]{1,0:T(8,128)(2,1)S(1)}, u32[]{:S(2)}, u32[]{:S(2)}) collective-permute-start(bf16[512,512]{1,0:T(8,128)(2,1)S(1)} %get-tuple-element.41), channel_id=1, source_target_pairs={{0,8},{8,0},{16,24},{24,16},{32,40},{40,32},{48,56},{56,48},{64,72... | collective-permute-start | bytes 1572872 | tf_op jit(solution)/shard_map/ppermute | solution.py:49
  114.7 3.3 %collective-permute-start.15 = (bf16[288,128]{1,0:T(8,128)(2,1)S(1)}, bf16[288,128]{1,0:T(8,128)(2,1)S(1)}, u32[]{:S(2)}, u32[]{:S(2)}) collective-permute-start(bf16[288,128]{1,0:T(8,128)(2,1)S(1)} %fusion.26), channel_id=1, source_target_pairs={{0,16},{8,24},{16,0},{24,8},{32,48},{40,56},{48,32},{56,40},{64,80... | collective-permute-start | bytes 221192 | tf_op jit(solution)/shard_map/ppermute | solution.py:49
  114.9 6.1 %collective-permute-start.20 = (bf16[512,128]{1,0:T(8,128)(2,1)S(1)}, bf16[512,128]{1,0:T(8,128)(2,1)S(1)}, u32[]{:S(2)}, u32[]{:S(2)}) collective-permute-start(bf16[512,128]{1,0:T(8,128)(2,1)S(1)} %slice.185), channel_id=1, source_target_pairs={{0,16},{8,24},{16,0},{24,8},{32,48},{40,56},{48,32},{56,40},{64,80... | collective-permute-start | bytes 393224 | tf_op jit(solution)/shard_map/ppermute | solution.py:49
  121.1 27.5 %collective-permute-start.30 = (bf16[512,128]{1,0:T(8,128)(2,1)S(1)}, bf16[512,128]{1,0:T(8,128)(2,1)S(1)}, u32[]{:S(2)}, u32[]{:S(2)}) collective-permute-start(bf16[512,128]{1,0:T(8,128)(2,1)S(1)} %fusion.25), channel_id=1, source_target_pairs={{0,192},{8,72},{16,208},{24,88},{32,224},{40,104},{48,240},{56,120... | collective-permute-start | bytes 393224 | tf_op jit(solution)/shard_map/ppermute | solution.py:49
  122.9 9.1 %collective-permute-start.21 = (bf16[512,256]{1,0:T(8,128)(2,1)S(1)}, bf16[512,256]{1,0:T(8,128)(2,1)S(1)}, u32[]{:S(2)}, u32[]{:S(2)}) collective-permute-start(bf16[512,256]{1,0:T(8,128)(2,1)S(1)} %slice.182), channel_id=1, source_target_pairs={{0,16},{8,24},{16,0},{24,8},{32,48},{40,56},{48,32},{56,40},{64,80... | collective-permute-start | bytes 786440 | tf_op jit(solution)/shard_map/ppermute | solution.py:49
  123.0 10.4 %collective-permute-start.19 = (bf16[288,128]{1,0:T(8,128)(2,1)S(1)}, bf16[288,128]{1,0:T(8,128)(2,1)S(1)}, u32[]{:S(2)}, u32[]{:S(2)}) collective-permute-start(bf16[288,128]{1,0:T(8,128)(2,1)S(1)} %fusion.27), channel_id=1, source_target_pairs={{0,64},{8,200},{16,80},{24,216},{32,96},{40,232},{48,112},{56,248}... | collective-permute-start | bytes 221192 | tf_op jit(solution)/shard_map/ppermute | solution.py:49
  125.1 9.7 %collective-permute-start.18 = (bf16[288,128]{1,0:T(8,128)(2,1)S(1)}, bf16[288,128]{1,0:T(8,128)(2,1)S(1)}, u32[]{:S(2)}, u32[]{:S(2)}) collective-permute-start(bf16[288,128]{1,0:T(8,128)(2,1)S(1)} %fusion.27), channel_id=1, source_target_pairs={{0,32},{8,232},{16,48},{24,248},{32,64},{40,8},{48,80},{56,24},{64... | collective-permute-start | bytes 221192 | tf_op jit(solution)/shard_map/ppermute | solution.py:49
  129.3 4.5 %collective-permute-start.25 = (bf16[512,256]{1,0:T(8,128)(2,1)S(1)}, bf16[512,256]{1,0:T(8,128)(2,1)S(1)}, u32[]{:S(2)}, u32[]{:S(2)}) collective-permute-start(bf16[512,256]{1,0:T(8,128)(2,1)S(1)} %get-tuple-element.39), channel_id=1, source_target_pairs={{0,8},{8,0},{16,24},{24,16},{32,40},{40,32},{48,56},{56,48},{64,72... | collective-permute-start | bytes 786440 | tf_op jit(solution)/shard_map/ppermute | solution.py:49
  132.0 14.8 %collective-permute-start.28 = (bf16[512,256]{1,0:T(8,128)(2,1)S(1)}, bf16[512,256]{1,0:T(8,128)(2,1)S(1)}, u32[]{:S(2)}, u32[]{:S(2)}) collective-permute-start(bf16[512,256]{1,0:T(8,128)(2,1)S(1)} %slice.181), channel_id=1, source_target_pairs={{0,16},{8,24},{16,0},{24,8},{32,48},{40,56},{48,32},{56,40},{64,80... | collective-permute-start | bytes 786440 | tf_op jit(solution)/shard_map/ppermute | solution.py:49
  133.4 8.5 %collective-permute-start.32 = (bf16[512,512]{1,0:T(8,128)(2,1)S(1)}, bf16[512,512]{1,0:T(8,128)(2,1)S(1)}, u32[]{:S(2)}, u32[]{:S(2)}) collective-permute-start(bf16[512,512]{1,0:T(8,128)(2,1)S(1)} %get-tuple-element.43), channel_id=1, source_target_pairs={{0,8},{8,0},{16,24},{24,16},{32,40},{40,32},{48,56},{56,48},{64,72... | collective-permute-start | bytes 1572872 | tf_op jit(solution)/shard_map/ppermute | solution.py:49
  133.8 3.5 %collective-permute-start.22 = (bf16[288,128]{1,0:T(8,128)(2,1)S(1)}, bf16[288,128]{1,0:T(8,128)(2,1)S(1)}, u32[]{:S(2)}, u32[]{:S(2)}) collective-permute-start(bf16[288,128]{1,0:T(8,128)(2,1)S(1)} %collective-permute-done.19), channel_id=1, source_target_pairs={{0,32},{8,232},{16,48},{24,248},{32,64},{40,8},{48,80},{56,24},{64... | collective-permute-start | bytes 221192 | tf_op jit(solution)/shard_map/ppermute | solution.py:49
  134.9 13.5 %collective-permute-start.29 = (bf16[512,256]{1,0:T(8,128)(2,1)S(1)}, bf16[512,256]{1,0:T(8,128)(2,1)S(1)}, u32[]{:S(2)}, u32[]{:S(2)}) collective-permute-start(bf16[512,256]{1,0:T(8,128)(2,1)S(1)} %fusion.23), channel_id=1, source_target_pairs={{0,224},{8,40},{16,240},{24,56},{32,0},{40,72},{48,16},{56,88},{64... | collective-permute-start | bytes 786440 | tf_op jit(solution)/shard_map/ppermute | solution.py:49
  137.3 4.6 %collective-permute-start.23 = (bf16[144,128]{1,0:T(8,128)(2,1)S(1)}, bf16[144,128]{1,0:T(8,128)(2,1)S(1)}, u32[]{:S(2)}, u32[]{:S(2)}) collective-permute-start(bf16[144,128]{1,0:T(8,128)(2,1)S(1)} %constant_dynamic-slice_fusion), channel_id=1, source_target_pairs={{0,64},{8,200},{16,80},{24,216},{32,96},{40,232},{48,112},{56,248}... | collective-permute-start | bytes 110600 | tf_op jit(solution)/shard_map/ppermute | solution.py:49
  141.9 18.0 %collective-permute-start.26 = (bf16[512,128]{1,0:T(8,128)(2,1)S(1)}, bf16[512,128]{1,0:T(8,128)(2,1)S(1)}, u32[]{:S(2)}, u32[]{:S(2)}) collective-permute-start(bf16[512,128]{1,0:T(8,128)(2,1)S(1)} %slice.184), channel_id=1, source_target_pairs={{0,16},{8,24},{16,0},{24,8},{32,48},{40,56},{48,32},{56,40},{64,80... | collective-permute-start | bytes 393224 | tf_op jit(solution)/shard_map/ppermute | solution.py:49
  141.9 13.5 %collective-permute-start.24 = (f32[288,128]{1,0:T(8,128)S(1)}, f32[288,128]{1,0:T(8,128)S(1)}, u32[]{:S(2)}, u32[]{:S(2)}) collective-permute-start(f32[288,128]{1,0:T(8,128)S(1)} %add_dynamic-update-slice_fusion), channel_id=1, source_target_pairs={{0,8},{8,0},{16,24},{24,16},{32,40},{40,32},{48,56},{56,48},{64,72... | collective-permute-start | bytes 442376 | tf_op jit(solution)/shard_map/ppermute | solution.py:49
  146.8 8.4 %collective-permute-start.33 = (bf16[512,256]{1,0:T(8,128)(2,1)S(1)}, bf16[512,256]{1,0:T(8,128)(2,1)S(1)}, u32[]{:S(2)}, u32[]{:S(2)}) collective-permute-start(bf16[512,256]{1,0:T(8,128)(2,1)S(1)} %slice.180), channel_id=1, source_target_pairs={{0,16},{8,24},{16,0},{24,8},{32,48},{40,56},{48,32},{56,40},{64,80... | collective-permute-start | bytes 786440 | tf_op jit(solution)/shard_map/ppermute | solution.py:49
  148.6 11.3 %collective-permute-start.31 = (bf16[512,256]{1,0:T(8,128)(2,1)S(1)}, bf16[512,256]{1,0:T(8,128)(2,1)S(1)}, u32[]{:S(2)}, u32[]{:S(2)}) collective-permute-start(bf16[512,256]{1,0:T(8,128)(2,1)S(1)} %pad_maximum_fusion.4), channel_id=1, source_target_pairs={{0,192},{8,72},{16,208},{24,88},{32,224},{40,104},{48,240},{56,120... | collective-permute-start | bytes 786440 | tf_op jit(solution)/shard_map/ppermute | solution.py:49
  155.3 6.5 %collective-permute-start.34 = (bf16[512,256]{1,0:T(8,128)(2,1)S(1)}, bf16[512,256]{1,0:T(8,128)(2,1)S(1)}, u32[]{:S(2)}, u32[]{:S(2)}) collective-permute-start(bf16[512,256]{1,0:T(8,128)(2,1)S(1)} %fusion.21), channel_id=1, source_target_pairs={{0,224},{8,40},{16,240},{24,56},{32,0},{40,72},{48,16},{56,88},{64... | collective-permute-start | bytes 786440 | tf_op jit(solution)/shard_map/ppermute | solution.py:49
  156.4 14.9 %all-to-all-start.2 = ((bf16[8,256,128]{2,1,0:T(8,128)(2,1)}), bf16[8,256,128]{2,1,0:T(8,128)(2,1)S(1)}, u32[]{:S(2)}, u32[]{:S(2)}) async-start(bf16[8,256,128]{2,1,0:T(8,128)(2,1)} %broadcast_in_dim.8), calls=%async_computation.2 | async-start | bytes 1048576 | tf_op jit(solution)/shard_map/all_to_all | solution.py:405
  161.9 10.4 %collective-permute-start.35 = (bf16[512,128]{1,0:T(8,128)(2,1)S(1)}, bf16[512,128]{1,0:T(8,128)(2,1)S(1)}, u32[]{:S(2)}, u32[]{:S(2)}) collective-permute-start(bf16[512,128]{1,0:T(8,128)(2,1)S(1)} %add_convert_fusion), channel_id=1, source_target_pairs={{0,8},{8,0},{16,24},{24,16},{32,40},{40,32},{48,56},{56,48},{64,72... | collective-permute-start | bytes 393224 | tf_op jit(solution)/shard_map/ppermute | solution.py:49
where the time goes:
time: 175 us; the launch traced here: 174 us
  waiting for transfers between devices  67.6 us (39%)
  starting transfers between devices  48 us (27%)
  blocking collectives  24.9 us (14%)
  Pallas kernels  19.1 us (11%)
  local copies, waits for them, and re-layouts  6.11 us (3%)
  matrix products  5.05 us (3%)
  other arithmetic  2.11 us (1%)
    ppermute x36, starting transfers between devices, send(): return lax.ppermute(value, 'layer', perm)  40.9 us
    ppermute x36, waiting for transfers between devices, send(): return lax.ppermute(value, 'layer', perm)  36.9 us
    all_to_all x1, blocking collectives, per_device(): got = lax.all_to_all(payload, 'rep', 0, 0, tiled=True)  24.9 us
    all_to_all x1, waiting for transfers between devices, per_device(): everyone = lax.all_to_all(outgoing, 'rep', 0, 0, tiled=True)  23.6 us
    all_to_all x1, waiting for transfers between devices, per_device(): pieces = lax.all_to_all(mine, 'rep', 0, 0, tiled=True)  7.22 us
    pallas_call x3, Pallas kernels, products(): pl.pallas_call(functools.partial(product_kernel, groups, first), grid=(le...  6.63 us
    pallas_call x1, Pallas kernels, spread_blocks(): pl.pallas_call(spread_kernel, grid_spec=pltpu.PrefetchScalarGridSpec(num_...  5.9 us
    dot_general x7, matrix products, dot(): return jnp.dot(dense[g], piece, preferred_element_type=F32)  5.05 us
  transfers between devices with their start and end apart: 38, of which 15 were waited for; matrix products, arithmetic and copies ran while one was open for 6% of the time, Pallas kernels for 8%

commit v1 on v0

v1 whole, which is shorter than its diff:
```python
import functools

import jax
import jax.numpy as jnp
from jax import lax
from jax.experimental import pallas as pl
from jax.experimental.pallas import tpu as pltpu
from jax.sharding import PartitionSpec as P

BF = jnp.bfloat16
F32 = jnp.float32
Z, Y, C = 8, 2, 2
REPS = 8
BLK = 128
SLOTS = 16
F = 512
GROUPS = 8
DEG = 16
ROWS = 800
HALF = 144
PART = 8


def layer_perm(dz, dy, dc):
    pairs = []
    for z in range(Z):
        for y in range(Y):
            for c in range(C):
                to = (((z + dz) % Z) * Y + (y + dy) % Y) * C + (c + dc) % C
                pairs.append(((z * Y + y) * C + c, to))
    return pairs


def core_perm(hops):
    pairs = []
    for z in range(Z):
        for y in range(Y):
            for c in range(C):
                step = hops if c == 0 else -hops
                pairs.append(((z * Y + y) * C + c, (((z + step) % Z) * Y + y) * C + c))
    return pairs


OUT1, OUT2 = core_perm(1), core_perm(2)
BACK1, BACK2 = core_perm(-1), core_perm(-2)
SIDE = layer_perm(0, 1, 0)
CORE = layer_perm(0, 0, 1)

def send(value, perm):
    return lax.ppermute(value, "layer", perm)


def after(value, *earlier):
    return lax.optimization_barrier((value,) + earlier)[0]


def spread_kernel(first, place_ref, values_ref, *rest):
    dense_ref, degree_ref, tiles, sems = rest[-4:]
    step = pl.program_id(0)

    def fetch(p):
        return pltpu.make_async_copy(values_ref.at[first + p], tiles.at[p], sems.at[p])

    @pl.when(step == 0)
    def _():
        for p in range(PART):
            fetch(p).start()

    dense_ref[...] = jnp.zeros_like(dense_ref)
    fetch(step).wait()
    total = jnp.zeros((BLK, BLK), jnp.int32)
    for slot in reversed(range(SLOTS)):
        tile = tiles[step, slot]
        total = total + tile
        place = place_ref[(first + step) * SLOTS + slot]
        lane = pl.multiple_of((place % 4) * BLK, BLK)
        dense_ref[place // 4, :, pl.ds(lane, BLK)] = tile.astype(F32).astype(BF)

    row = lax.dot_general(
        jnp.ones((DEG, BLK), BF),
        total.astype(F32).astype(BF),
        (((1,), (1,)), ((), ())),
        preferred_element_type=F32,
    )
    high = jnp.floor(row * (1.0 / 128.0)) * 128.0
    degree_ref[...] = jnp.zeros_like(degree_ref)
    degree_ref[0, :, 0:BLK] = high.astype(BF)
    degree_ref[0, :, BLK : 2 * BLK] = (row - high).astype(BF)


def spread_part(place, values, first, dense=None):
    panels = values.shape[0]
    given = [] if dense is None else [dense]
    return pl.pallas_call(
        functools.partial(spread_kernel, first),
        grid_spec=pltpu.PrefetchScalarGridSpec(
            num_scalar_prefetch=1,
            grid=(PART,),
            in_specs=[pl.BlockSpec(memory_space=pltpu.HBM)]
            + [pl.BlockSpec(memory_space=pl.ANY)] * len(given),
            out_specs=[
                pl.BlockSpec((GROUPS, BLK, 4 * BLK), lambda p, place: (0, first + p, 0)),
                pl.BlockSpec((1, DEG, F), lambda p, place: (p, 0, 0)),
            ],
            scratch_shapes=[
                pltpu.VMEM((PART, SLOTS, BLK, BLK), jnp.int32),
                pltpu.SemaphoreType.DMA((PART,)),
            ],
        ),
        out_shape=[
            jax.ShapeDtypeStruct((GROUPS, panels * BLK, 4 * BLK), BF),
            jax.ShapeDtypeStruct((PART, DEG, F), BF),
        ],
        input_output_aliases={2: 0} if given else {},
        compiler_params=pltpu.CompilerParams(vmem_limit_bytes=16 << 20),
        cost_estimate=pl.CostEstimate(flops=1 << 21, bytes_accessed=8 << 20, transcendentals=0),
    )(place.reshape(-1), pltpu.with_memory_space_constraint(values, pltpu.HBM), *given)


def payload_kernel(total_ref, dense_ref, last_ref, degree_ref, out_ref):
    product = jnp.dot(dense_ref[0], last_ref[...], preferred_element_type=F32)
    out_ref[0, 0:BLK, :] = (total_ref[...] + product).astype(BF)
    out_ref[0, BLK : BLK + DEG, :] = degree_ref[0]


def payload_of(total, dense, group, last, degree_rows):
    return pl.pallas_call(
        payload_kernel,
        grid=(REPS,),
        in_specs=[
            pl.BlockSpec((BLK, F), lambda p: (p, 0)),
            pl.BlockSpec((1, BLK, 4 * BLK), lambda p: (group, p, 0)),
            pl.BlockSpec((4 * BLK, F), lambda p: (0, 0)),
            pl.BlockSpec((1, DEG, F), lambda p: (p, 0, 0)),
        ],
        out_specs=pl.BlockSpec((1, BLK + DEG, F), lambda p: (p, 0, 0)),
        out_shape=jax.ShapeDtypeStruct((REPS, BLK + DEG, F), BF),
        compiler_params=pltpu.CompilerParams(vmem_limit_bytes=8 << 20),
        cost_estimate=pl.CostEstimate(
            flops=2 * REPS * BLK * 4 * BLK * F, bytes_accessed=5 << 20, transcendentals=0
        ),
    )(total, dense, last, degree_rows)


def node_kernel(
    got_ref, features_ref, weight_ref, bias_ref, cotangent_ref, act_ref, out_ref, scaled_ref
):
    got = got_ref[...].astype(F32)
    summed = jnp.sum(got, axis=0)
    parts = summed[BLK : BLK + 1, :]
    degree_row = 1.0 + parts[:, 0:BLK] + parts[:, BLK : 2 * BLK]
    degree = jnp.transpose(jnp.broadcast_to(degree_row, (BLK, BLK)))
    degree = jnp.concatenate([degree] * 4, axis=1)
    aggregate = summed[0:BLK] + features_ref[...].astype(F32)
    hidden_wide = (aggregate / degree).astype(BF)
    weight = weight_ref[...]
    preact = jnp.dot(hidden_wide, weight, preferred_element_type=F32) + bias_ref[...]
    gate = jax.nn.sigmoid(preact)
    act_ref[...] = (preact * gate).astype(BF)
    slope = (cotangent_ref[...].astype(F32) * gate * (1.0 + preact * (1.0 - gate))).astype(BF)
    rows = lax.dot_general(slope, weight, (((1,), (1,)), ((), ())), preferred_element_type=F32)
    scaled = (rows / degree).astype(BF)
    scaled_t = jnp.transpose(scaled.astype(F32)).astype(BF)
    scaled_ref[...] = scaled_t
    hidden_t = jnp.transpose(hidden_wide.astype(F32)).astype(BF)
    grad = jnp.dot(hidden_t, slope, preferred_element_type=F32).astype(BF)
    bias = jnp.sum(slope.astype(F32), axis=0, keepdims=True).astype(BF)
    out_ref[:, 768:ROWS, :] = jnp.zeros((REPS, 32, BLK), BF)
    for peer in range(REPS):
        out_ref[peer, 0:512, :] = scaled_t
        for b in range(4):
            out_ref[peer, 512 + 64 * b : 576 + 64 * b, :] = grad[
                64 * peer : 64 * peer + 64, BLK * b : BLK * (b + 1)
            ]
            out_ref[peer, 768 + b : 769 + b, :] = bias[:, BLK * b : BLK * (b + 1)]


def node_step(got, features, weight, bias_row, cotangent):
    return pl.pallas_call(
        node_kernel,
        out_shape=[
            jax.ShapeDtypeStruct((BLK, F), BF),
            jax.ShapeDtypeStruct((REPS, ROWS, BLK), BF),
            jax.ShapeDtypeStruct((F, BLK), BF),
        ],
        compiler_params=pltpu.CompilerParams(vmem_limit_bytes=24 << 20),
        cost_estimate=pl.CostEstimate(
            flops=6 * BLK * F * F, bytes_accessed=4 << 20, transcendentals=BLK * F
        ),
    )(got, features, weight, bias_row.reshape(1, F), cotangent)


def product_kernel(groups, first, left_ref, dense_ref, *rest):
    step = pl.program_id(0)
    if first:
        wide_ref = rest[-1]

        @pl.when(step == 0)
        def _():
            for p in range(REPS):
                wide_ref[:, BLK * p : BLK * (p + 1)] = left_ref[p]
    else:
        wide_ref = left_ref
    whole = jnp.dot(wide_ref[...], dense_ref[0], preferred_element_type=F32)
    away_ref, mine_ref = rest[:2]
    for index, group in enumerate(groups):

        @pl.when(step == index)
        def _():
            if group == 7:
                away_ref[:, : 2 * BLK] = whole[:, 2 * BLK :].astype(BF)
                mine_ref[:, : 2 * BLK] = whole[:, : 2 * BLK]
            elif group == 0:
                for part in (0, 1):
                    own = 2 * part * BLK
                    here = slice(part * BLK, (part + 1) * BLK)
                    rest[2][:, here] = whole[:, own + BLK : own + 2 * BLK].astype(BF)
                    rest[3][:, here] = whole[:, own : own + BLK]
            elif group % 2:
                mine_ref[:, mine_ref.shape[1] - 4 * BLK :] = whole
            else:
                away_ref[:, away_ref.shape[1] - 4 * BLK :] = whole.astype(BF)


def products(left, dense, groups, first):
    columns = 6 * BLK if 7 in groups else 4 * BLK
    shapes = [((F, columns), BF), ((F, columns), F32)]
    if 0 in groups:
        shapes += [((F, 2 * BLK), BF), ((F, 2 * BLK), F32)]
    if first:
        shapes.append(((F, REPS * BLK), BF))
        left_spec = pl.BlockSpec((REPS, F, BLK), lambda i: (0, 0, 0))
    else:
        left_spec = pl.BlockSpec((F, REPS * BLK), lambda i: (0, 0))
    top = groups[0]
    return pl.pallas_call(
        functools.partial(product_kernel, groups, first),
        grid=(len(groups),),
        in_specs=[
            left_spec,
            pl.BlockSpec((1, REPS * BLK, 4 * BLK), lambda i: (top - i, 0, 0)),
        ],
        out_specs=[pl.BlockSpec(shape, lambda i: (0, 0)) for shape, _ in shapes],
        out_shape=[jax.ShapeDtypeStruct(shape, dtype) for shape, dtype in shapes],
        compiler_params=pltpu.CompilerParams(vmem_limit_bytes=20 << 20),
        cost_estimate=pl.CostEstimate(
            flops=len(groups) * 2 * F * REPS * BLK * 4 * BLK,
            bytes_accessed=len(groups) * (5 << 19),
            transcendentals=0,
        ),
    )(left, dense)


def forward(features, place, values):
    def dot(g, piece):
        return jnp.dot(dense[g], piece, preferred_element_type=F32)

    chain = jnp.concatenate([features, send(features, CORE)], axis=0)
    beside = send(features, SIDE)
    second = send(chain, OUT2)
    own = jnp.concatenate([chain, beside, send(beside, CORE)], axis=0)
    first = send(own, OUT1)
    dense, degree_rows = spread_part(after(place, own), values, 0)
    third = send(second, OUT1)
    fourth = send(second[:BLK], OUT2)
    both2 = jnp.concatenate([second, send(second, SIDE)], axis=0)
    cross2 = send(both2, CORE)
    cross1 = send(first, CORE)
    both3 = jnp.concatenate([third, send(third, SIDE)], axis=0)
    both4 = jnp.concatenate([fourth, send(fourth, SIDE)], axis=0)
    total = dot(0, own) + dot(1, first) + dot(3, both2)
    both3 = after(both3, total)
    cross3 = send(both3, CORE)
    total = total + dot(4, cross2) + dot(2, cross1) + dot(5, both3)
    both4 = after(both4, total)
    last = jnp.concatenate([both4, send(both4, CORE)], axis=0)
    total = total + dot(6, cross3)
    return payload_of(total, dense, 7, last, degree_rows), dense


def final_kernel(mine_ref, far_ref, near_ref, other_ref, scaled_ref, out_ref):
    total = (
        mine_ref[...]
        + far_ref[:, :BLK].astype(F32)
        + near_ref[:, :BLK].astype(F32)
        + other_ref[...].astype(F32)
        + scaled_ref[...].astype(F32)
    )
    out_ref[...] = jnp.transpose(total).astype(BF)


def final_step(*parts):
    return pl.pallas_call(
        final_kernel,
        out_shape=jax.ShapeDtypeStruct((BLK, F), BF),
        compiler_params=pltpu.CompilerParams(vmem_limit_bytes=8 << 20),
        cost_estimate=pl.CostEstimate(flops=1 << 19, bytes_accessed=1 << 20, transcendentals=0),
    )(*parts)


def gradient_kernel(pieces_ref, out_ref):
    for peer in range(REPS):
        for b in range(4):
            out_ref[64 * peer : 64 * peer + 64, BLK * b : BLK * (b + 1)] = pieces_ref[
                peer, 64 * b : 64 * b + 64
            ].astype(F32)


def gradient_of(pieces):
    return pl.pallas_call(
        gradient_kernel,
        out_shape=jax.ShapeDtypeStruct((F, F), F32),
        compiler_params=pltpu.CompilerParams(vmem_limit_bytes=8 << 20),
        cost_estimate=pl.CostEstimate(flops=1 << 18, bytes_accessed=3 << 19, transcendentals=0),
    )(pieces)


def folded(rows):
    half = rows.shape[0] // 2
    return jnp.concatenate([rows[:half], rows[half:]], axis=1)


def unfolded(rows):
    return jnp.concatenate([rows[:, :BLK], rows[:, BLK:]], axis=0)


def backward(everyone, dense, scaled_t):
    def wide_of(value):
        return value.astype(F32)

    def stacked(*parts):
        return jnp.concatenate([part.astype(BF) for part in parts], axis=0)

    grads = jnp.sum(wide_of(everyone[:, F:]), axis=0)
    grads = folded(grads + wide_of(send(grads.astype(BF), CORE)))
    away, mine, wide = products(everyone, dense, (7, 6, 5), True)
    line = mine + wide_of(send(away, CORE))
    side3 = stacked(line[:, 4 * BLK :], grads)
    got3 = wide_of(send(side3, SIDE))
    side4 = line[:, BLK : 2 * BLK].astype(BF)
    got4 = wide_of(send(side4, SIDE))
    away, mine = products(wide, dense, (4, 3), False)
    line2 = mine + wide_of(after(send(away, CORE), side3, side4))
    side2 = line2[:, 2 * BLK :].astype(BF)
    got2 = wide_of(send(side2, SIDE))
    away1, mine1, away0, mine0 = products(after(wide, side3, side4), dense, (2, 1, 0), False)
    line1 = mine1 + wide_of(send(away1, CORE))
    side1 = after(line1[:, 2 * BLK :].astype(BF), side2)
    got1 = wide_of(send(side1, SIDE))
    line0 = mine0 + wide_of(send(away0, CORE))
    side0 = after(line0[:, BLK:].astype(BF), side1)
    quad0 = line0[:, :BLK] + wide_of(send(side0, SIDE))

    grads = grads + got3[F:]
    quad3 = after(stacked(line[:, 2 * BLK : 4 * BLK] + got3[:F], grads), side1)
    quad4 = after(stacked(line[:, :BLK] + got4, unfolded(grads)), side1)
    came3 = send(quad3, BACK1)
    came4 = send(quad4, BACK2)
    quad2 = line2[:, : 2 * BLK] + got2 + wide_of(came3[:F])
    quad2 = jnp.concatenate([quad2[:, :BLK] + wide_of(came4[:F]), quad2[:, BLK:]], axis=1)
    quad2 = quad2.astype(BF)
    far = send(quad2, BACK2)
    quad1 = (line1[:, : 2 * BLK] + got1).astype(BF)
    near = send(quad1, BACK1)

    both = jnp.concatenate([came3[F:], folded(came4[F:])], axis=0)
    more = wide_of(send(after(both, quad2), BACK2))
    rows = both.shape[0] // 2
    around = wide_of(both[:rows]) + wide_of(both[rows:]) + more[:rows] + 0.5 * more[rows:]
    grads = after(grads + around + send(around, CORE), quad1)

    other = send((wide_of(far[:, BLK:]) + wide_of(near[:, BLK:])).astype(BF), CORE)
    return final_step(quad0, far, near, other, scaled_t), unfolded(grads)


def per_device(features, block_columns, block_values, weight, bias_row, cotangent):
    layer = lax.axis_index("layer")
    z, y, c = layer // 4, (layer // 2) % 2, layer % 2
    owner = jnp.where(block_columns >= 0, block_columns, 0) // REPS
    dz = (owner // 4 - z + Z) % Z
    dy = ((owner // 2) % 2 - y) % 2
    dc = (owner % 2 - c) % 2
    near = jnp.where(dz <= 4, dz, Z - dz)
    other = ((dz > 4) != (c == 0)).astype(jnp.int32)
    ends = (near == 0) | (near == 4)
    group = jnp.where(near == 0, 0, jnp.where(near == 4, 7, 2 * near - 1 + other))
    column = jnp.where(near == 4, 2 * dc + dy, 2 * dy + jnp.where(ends, dc, dc ^ other))
    place = 4 * group + column
    place = jnp.where(block_columns >= 0, place, place[:, 0:1]).astype(jnp.int32)
    payload, dense = forward(features, place, block_values)
    got = lax.all_to_all(payload, "rep", 0, 0, tiled=True)

    activations, outgoing, scaled_t = node_step(got, features, weight, bias_row, cotangent)
    everyone = lax.all_to_all(outgoing, "rep", 0, 0, tiled=True)
    feature_grad, grads = backward(everyone, dense, scaled_t)
    bias_grad = grads[256:260].reshape(F)
    mine = jnp.broadcast_to(grads[:256].astype(BF)[None], (REPS, 256, BLK))
    pieces = lax.all_to_all(mine, "rep", 0, 0, tiled=True)
    weight_grad = gradient_of(pieces)
    return (activations, weight_grad, bias_grad, feature_grad)


def solution(mesh):
    in_specs = (
        P(("layer", "rep"), None),
        P("layer", "rep"),
        P("layer", "rep", None, None),
        P(),
        P(),
        P(("layer", "rep"), None),
    )
    out_specs = (P(("layer", "rep"), None), P(), P(), P(("layer", "rep"), None))
    return jax.shard_map(
        per_device, mesh=mesh, in_specs=in_specs, out_specs=out_specs, check_vma=False
    )
```

time: 175 us -> 161 us (0.920)
  blocking collectives: 24.9 us -> 49.2 us
  waiting for transfers between devices: 67.6 us -> 43.3 us
  starting transfers between devices: 48 us -> 38.5 us
  local copies, waits for them, and re-layouts: 6.11 us -> 2.83 us
  Pallas kernels: 19.1 us -> 16.5 us
    all_to_all x0 -> x1, blocking collectives: none -> 24.4 us  [per_device(): everyone = lax.all_to_all(outgoing, 'rep', 0, 0, tiled=True)]
    all_to_all x1 -> x0, waiting for transfers between devices: 23.6 us -> none  [per_device(): everyone = lax.all_to_all(outgoing, 'rep', 0, 0, tiled=True)]
    ppermute x36 -> x31, starting transfers between devices: 40.9 us -> 35 us  [send(): return lax.ppermute(value, 'layer', perm)]
    all_to_all x1 -> x0, starting transfers between devices: 3.58 us -> none  [per_device(): everyone = lax.all_to_all(outgoing, 'rep', 0, 0, tiled=True)]
    unnamed x16 -> x12, local copies, waits for them, and re-layouts: 4.36 us -> 0.98 us
    ppermute x36 -> x31, waiting for transfers between devices: 36.9 us -> 36.6 us  [send(): return lax.ppermute(value, 'layer', perm)]
  transfers between devices with their start and end apart: 38 -> 32, of which waited for: 15 -> 12; matrix products, arithmetic and copies ran while one was open for 6% -> 7% of each run, Pallas kernels for 8% -> 6%
where the time goes in v1:
time: 161 us; the launch traced here: 160 us
  blocking collectives  49.2 us (31%)
  waiting for transfers between devices  43.3 us (27%)
  starting transfers between devices  38.5 us (24%)
  Pallas kernels  16.5 us (10%)
  matrix products  4.94 us (3%)
  other arithmetic  3.85 us (2%)
  local copies, waits for them, and re-layouts  2.83 us (2%)
    ppermute x31, waiting for transfers between devices, send(): return lax.ppermute(value, 'layer', perm)  36.6 us
    ppermute x31, starting transfers between devices, send(): return lax.ppermute(value, 'layer', perm)  35 us
    all_to_all x1, blocking collectives, per_device(): got = lax.all_to_all(payload, 'rep', 0, 0, tiled=True)  24.7 us
    all_to_all x1, blocking collectives, per_device(): everyone = lax.all_to_all(outgoing, 'rep', 0, 0, tiled=True)  24.4 us
    all_to_all x1, waiting for transfers between devices, per_device(): pieces = lax.all_to_all(mine, 'rep', 0, 0, tiled=True)  6.72 us
    pallas_call x3, Pallas kernels, products(): pl.pallas_call(functools.partial(product_kernel, groups, first), grid=(le...  6.64 us
    pallas_call x1, Pallas kernels, spread_part(): pl.pallas_call(functools.partial(spread_kernel, first), grid_spec=pltpu.P...  5.07 us
    dot_general x7, matrix products, dot(): return jnp.dot(dense[g], piece, preferred_element_type=F32)  4.94 us
  transfers between devices with their start and end apart: 32, of which 12 were waited for; matrix products, arithmetic and copies ran while one was open for 7% of the time, Pallas kernels for 6%

profile of v1, /device:TPU:1, one launch (start us, length us, event | category | flops | bytes accessed | tf_op | source)
XLA Modules:
  0.0 160.3 jit_solution(10081755031389086862)
XLA Ops:
  0.6 3.3 %collective-permute-start = (bf16[128,512]{1,0:T(8,128)(2,1)}, bf16[128,512]{1,0:T(8,128)(2,1)S(1)}, u32[]{:S(2)}, u32[]{:S(2)}) collective-permute-start(bf16[128,512]{1,0:T(8,128)(2,1)} %features_ref.1), channel_id=1, source_target_pairs={{0,8},{8,0},{16,24},{24,16},{32,40},{40,32},{48,56},{56,48},{64,72... | collective-permute-start | bytes 393224 | tf_op jit(solution)/shard_map/ppermute | solution.py:50
  4.0 0.7 fusion.32
  4.8 0.8 compare_select_fusion.1
  5.6 0.9 constant_dynamic-update-slice_fusion.3
  6.5 0.9 pad_maximum_fusion.4
  7.4 5.7 %collective-permute-start.4 = (bf16[256,512]{1,0:T(8,128)(2,1)S(1)}, bf16[256,512]{1,0:T(8,128)(2,1)S(1)}, u32[]{:S(2)}, u32[]{:S(2)}) collective-permute-start(bf16[256,512]{1,0:T(8,128)(2,1)S(1)} %pad_maximum_fusion.4), channel_id=1, source_target_pairs={{0,64},{8,200},{16,80},{24,216},{32,96},{40,232},{48,112},{56,248}... | collective-permute-start | bytes 786440 | tf_op jit(solution)/shard_map/ppermute | solution.py:50
  13.1 1.3 collective-permute-done.2
  14.5 0.8 collective-permute-start.3
  15.3 5.1 %shard_map.93 = (bf16[8,1024,512]{2,1,0:T(8,128)(2,1)S(1)}, bf16[8,16,512]{2,1,0:T(8,128)(2,1)S(1)}) custom-call(s32[128]{0:T(128)S(1)} %reshape.18.place_ref, s32[8,16,128,128]{3,2,1,0:T(8,128)} %values_ref.1), custom_call_target="tpu_custom_call" | custom-call | flops 2097152 | bytes 8388608 | tf_op jit(solution)/shard_map/pallas_call | solution.py:94
  20.4 3.0 %collective-permute-start.11 = (bf16[128,512]{1,0:T(8,128)(2,1)S(1)}, bf16[128,512]{1,0:T(8,128)(2,1)S(1)}, u32[]{:S(2)}, u32[]{:S(2)}) collective-permute-start(bf16[128,512]{1,0:T(8,128)(2,1)S(1)} %slice.179), channel_id=1, source_target_pairs={{0,64},{8,200},{16,80},{24,216},{32,96},{40,232},{48,112},{56,248}... | collective-permute-start | bytes 393224 | tf_op jit(solution)/shard_map/ppermute | solution.py:50
  23.5 0.7 fusion.12
  24.2 3.5 %collective-permute-done.11 = bf16[128,512]{1,0:T(8,128)(2,1)S(1)} collective-permute-done((bf16[128,512]{1,0:T(8,128)(2,1)S(1)}, bf16[128,512]{1,0:T(8,128)(2,1)S(1)}, u32[]{:S(2)}, u32[]{:S(2)}) %collective-permute-start.11) | collective-permute-done | bytes 131104 | tf_op jit(solution)/shard_map/ppermute | solution.py:50
  27.7 3.2 %collective-permute-done.5 = bf16[256,512]{1,0:T(8,128)(2,1)S(1)} collective-permute-done((bf16[256,512]{1,0:T(8,128)(2,1)S(1)}, bf16[256,512]{1,0:T(8,128)(2,1)S(1)}, u32[]{:S(2)}, u32[]{:S(2)}) %collective-permute-start.5) | collective-permute-done | bytes 262176 | tf_op jit(solution)/shard_map/ppermute | solution.py:50
  30.8 2.4 %collective-permute-start.6 = (bf16[512,512]{1,0:T(8,128)(2,1)S(1)}, bf16[512,512]{1,0:T(8,128)(2,1)S(1)}, u32[]{:S(2)}, u32[]{:S(2)}) collective-permute-start(bf16[512,512]{1,0:T(8,128)(2,1)S(1)} %constant_dynamic-update-slice_fusion.4), channel_id=1, source_target_pairs={{0,8},{8,0},{16,24},{24,16},{32,40},{40,32},{48,56},{56,48},{64,72... | collective-permute-start | bytes 1572872 | tf_op jit(solution)/shard_map/ppermute | solution.py:50
  33.7 0.7 fusion.10
  34.5 0.7 add_add_fusion.1
  35.2 1.3 collective-permute-start.7
  36.5 4.6 %collective-permute-done.9 = bf16[256,512]{1,0:T(8,128)(2,1)S(1)} collective-permute-done((bf16[256,512]{1,0:T(8,128)(2,1)S(1)}, bf16[256,512]{1,0:T(8,128)(2,1)S(1)}, u32[]{:S(2)}, u32[]{:S(2)}) %collective-permute-start.9) | collective-permute-done | bytes 262176 | tf_op jit(solution)/shard_map/ppermute | solution.py:50
  41.1 1.0 collective-permute-start.10
  42.1 0.7 fusion.1
  42.8 0.7 fusion.4
  43.5 0.7 add_add_fusion
  44.5 0.7 convolution_add_fusion.total_ref
  45.2 0.8 collective-permute-done.13
  46.1 1.9 %shard_map.94 = bf16[8,144,512]{2,1,0:T(8,128)(2,1)S(1)} custom-call(f32[1024,512]{1,0:T(8,128)S(1)} %convolution_add_fusion.total_ref, bf16[8,1024,512]{2,1,0:T(8,128)(2,1)S(1)} %get-tuple-element.30.dense_ref, bf16[512,512]{1,0:T(8,128)(2,1)S(1)} %pad_maximum_fusion.1.last_ref, bf16[8,16,512]{2,1,0:T(8,128)(2,1)S(1)} %get-tuple-element.33.degree_ref), custom_call_target="tpu_custom_call" | custom-call | flops 536870912 | bytes 5242880 | tf_op jit(solution)/shard_map/pallas_call | solution.py:127
  48.0 24.7 %all_to_all.15.got_ref = bf16[8,144,512]{2,1,0:T(8,128)(2,1)S(1)} all-to-all(bf16[8,144,512]{2,1,0:T(8,128)(2,1)S(1)} %shard_map.94), channel_id=1, replica_groups=mesh['layer'=32,'rep'=8] {'rep'}, dimensions={0} | all-to-all | bytes 2359296 | tf_op jit(solution)/shard_map/all_to_all | solution.py:391
  72.8 1.0 shard_map.95
  73.8 24.4 %all_to_all.16.left_ref = bf16[8,800,128]{2,1,0:T(8,128)(2,1)S(1)} all-to-all(bf16[8,800,128]{2,1,0:T(8,128)(2,1)S(1)} %get-tuple-element.35), channel_id=1, replica_groups=mesh['layer'=32,'rep'=8] {'rep'}, dimensions={0} | all-to-all | bytes 3276800 | tf_op jit(solution)/shard_map/all_to_all | solution.py:394
  98.3 2.7 %shard_map.96 = (bf16[512,768]{1,0:T(8,128)(2,1)S(1)}, f32[512,768]{1,0:T(8,128)S(1)}, bf16[512,1024]{1,0:T(8,128)(2,1)S(1)}) custom-call(bf16[8,800,128]{2,1,0:T(8,128)(2,1)S(1)} %all_to_all.16.left_ref, bf16[8,1024,512]{2,1,0:T(8,128)(2,1)S(1)} %get-tuple-element.30.dense_ref), custom_call_target="tpu_custom_call" | custom-call | flops 1610612736 | bytes 7864320 | tf_op jit(solution)/shard_map/pallas_call | solution.py:236
  101.0 2.6 %collective-permute-start.15 = (bf16[512,768]{1,0:T(8,128)(2,1)S(1)}, bf16[512,768]{1,0:T(8,128)(2,1)S(1)}, u32[]{:S(2)}, u32[]{:S(2)}) collective-permute-start(bf16[512,768]{1,0:T(8,128)(2,1)S(1)} %get-tuple-element.37), channel_id=1, source_target_pairs={{0,8},{8,0},{16,24},{24,16},{32,40},{40,32},{48,56},{56,48},{64,72... | collective-permute-start | bytes 2359304 | tf_op jit(solution)/shard_map/ppermute | solution.py:50
  103.8 1.6 shard_map.98
  106.6 1.3 collective-permute-start.20
  107.9 2.4 %shard_map.97 = (bf16[512,512]{1,0:T(8,128)(2,1)S(1)}, f32[512,512]{1,0:T(8,128)S(1)}, bf16[512,256]{1,0:T(8,128)(2,1)S(1)}, f32[512,256]{1,0:T(8,128)S(1)}) custom-call(bf16[512,1024]{1,0:T(8,128)(2,1)S(1)} %get-tuple-element.39.left_ref, bf16[8,1024,512]{2,1,0:T(8,128)(2,1)S(1)} %get-tuple-element.30.dense_ref), custom_call_target="tpu_custom_call" | custom-call | flops 1610612736 | bytes 7864320 | tf_op jit(solution)/shard_map/pallas_call | solution.py:236
  111.1 7.6 %collective-permute-done.20 = bf16[512,128]{1,0:T(8,128)(2,1)S(1)} collective-permute-done((bf16[512,128]{1,0:T(8,128)(2,1)S(1)}, bf16[512,128]{1,0:T(8,128)(2,1)S(1)}, u32[]{:S(2)}, u32[]{:S(2)}) %collective-permute-start.20) | collective-permute-done | bytes 131104 | tf_op jit(solution)/shard_map/ppermute | solution.py:50
  119.3 2.0 %collective-permute-start.19 = (bf16[656,256]{1,0:T(8,128)(2,1)S(1)}, bf16[656,256]{1,0:T(8,128)(2,1)S(1)}, u32[]{:S(2)}, u32[]{:S(2)}) collective-permute-start(bf16[656,256]{1,0:T(8,128)(2,1)S(1)} %pad_maximum_fusion.3), channel_id=1, source_target_pairs={{0,224},{8,40},{16,240},{24,56},{32,0},{40,72},{48,16},{56,88},{64... | collective-permute-start | bytes 1007624 | tf_op jit(solution)/shard_map/ppermute | solution.py:50
  121.5 1.9 %collective-permute-start.26 = (bf16[512,256]{1,0:T(8,128)(2,1)S(1)}, bf16[512,256]{1,0:T(8,128)(2,1)S(1)}, u32[]{:S(2)}, u32[]{:S(2)}) collective-permute-start(bf16[512,256]{1,0:T(8,128)(2,1)S(1)} %get-tuple-element.51), channel_id=1, source_target_pairs={{0,8},{8,0},{16,24},{24,16},{32,40},{40,32},{48,56},{56,48},{64,72... | collective-permute-start | bytes 786440 | tf_op jit(solution)/shard_map/ppermute | solution.py:50
  123.4 1.5 collective-permute-start.25
  124.9 3.2 %collective-permute-done.21 = bf16[800,128]{1,0:T(8,128)(2,1)S(1)} collective-permute-done((bf16[800,128]{1,0:T(8,128)(2,1)S(1)}, bf16[800,128]{1,0:T(8,128)(2,1)S(1)}, u32[]{:S(2)}, u32[]{:S(2)}) %collective-permute-start.21) | collective-permute-done | bytes 204832 | tf_op jit(solution)/shard_map/ppermute | solution.py:50
  128.0 3.7 %collective-permute-done.19 = bf16[656,256]{1,0:T(8,128)(2,1)S(1)} collective-permute-done((bf16[656,256]{1,0:T(8,128)(2,1)S(1)}, bf16[656,256]{1,0:T(8,128)(2,1)S(1)}, u32[]{:S(2)}, u32[]{:S(2)}) %collective-permute-start.19) | collective-permute-done | bytes 335904 | tf_op jit(solution)/shard_map/ppermute | solution.py:50
  132.7 6.0 %collective-permute-done.23 = bf16[288,256]{1,0:T(8,128)(2,1)S(1)} collective-permute-done((bf16[288,256]{1,0:T(8,128)(2,1)S(1)}, bf16[288,256]{1,0:T(8,128)(2,1)S(1)}, u32[]{:S(2)}, u32[]{:S(2)}) %collective-permute-start.23) | collective-permute-done | bytes 147488 | tf_op jit(solution)/shard_map/ppermute | solution.py:50
  138.7 1.8 %collective-permute-start.24 = (f32[144,256]{1,0:T(8,128)S(1)}, f32[144,256]{1,0:T(8,128)S(1)}, u32[]{:S(2)}, u32[]{:S(2)}) collective-permute-start(f32[144,256]{1,0:T(8,128)S(1)} %fusion.26), channel_id=1, source_target_pairs={{0,8},{8,0},{16,24},{24,16},{32,40},{40,32},{48,56},{56,48},{64,72... | collective-permute-start | bytes 442376 | tf_op jit(solution)/shard_map/ppermute | solution.py:50
  140.7 2.4 %collective-permute-start.28 = (bf16[512,256]{1,0:T(8,128)(2,1)S(1)}, bf16[512,256]{1,0:T(8,128)(2,1)S(1)}, u32[]{:S(2)}, u32[]{:S(2)}) collective-permute-start(bf16[512,256]{1,0:T(8,128)(2,1)S(1)} %pad_maximum_fusion.6), channel_id=1, source_target_pairs={{0,192},{8,72},{16,208},{24,88},{32,224},{40,104},{48,240},{56,120... | collective-permute-start | bytes 786440 | tf_op jit(solution)/shard_map/ppermute | solution.py:50
  143.2 0.9 broadcast_in_dim.23
  144.1 3.5 %all-to-all-start.2 = ((bf16[8,256,128]{2,1,0:T(8,128)(2,1)}), bf16[8,256,128]{2,1,0:T(8,128)(2,1)S(1)}, u32[]{:S(2)}, u32[]{:S(2)}) async-start(bf16[8,256,128]{2,1,0:T(8,128)(2,1)} %broadcast_in_dim.23), calls=%async_computation.2 | async-start | bytes 1048576 | tf_op jit(solution)/shard_map/all_to_all | solution.py:398
  147.6 2.5 %collective-permute-done.29.near_ref = bf16[512,256]{1,0:T(8,128)(2,1)S(1)} collective-permute-done((bf16[512,256]{1,0:T(8,128)(2,1)S(1)}, bf16[512,256]{1,0:T(8,128)(2,1)S(1)}, u32[]{:S(2)}, u32[]{:S(2)}) %collective-permute-start.29) | collective-permute-done | bytes 262176 | tf_op jit(solution)/shard_map/ppermute | solution.py:50
  151.8 0.8 shard_map.100
  152.6 6.7 %all-to-all-done.2.pieces_ref = bf16[8,256,128]{2,1,0:T(8,128)(2,1)S(1)} async-done(((bf16[8,256,128]{2,1,0:T(8,128)(2,1)}), bf16[8,256,128]{2,1,0:T(8,128)(2,1)S(1)}, u32[]{:S(2)}, u32[]{:S(2)}) %all-to-all-start.2) | async-done | bytes 524320 | tf_op jit(solution)/shard_map/all_to_all | solution.py:398
  159.3 1.0 shard_map.99
  (96 shorter events, 7.0 us)
Async XLA Ops:
  0.6 5.8 %collective-permute-start = (bf16[128,512]{1,0:T(8,128)(2,1)}, bf16[128,512]{1,0:T(8,128)(2,1)S(1)}, u32[]{:S(2)}, u32[]{:S(2)}) collective-permute-start(bf16[128,512]{1,0:T(8,128)(2,1)} %features_ref.1), channel_id=1, source_target_pairs={{0,8},{8,0},{16,24},{24,16},{32,40},{40,32},{48,56},{56,48},{64,72... | collective-permute-start | bytes 393224 | tf_op jit(solution)/shard_map/ppermute | solution.py:50
  4.0 9.1 %collective-permute-start.1 = (bf16[128,512]{1,0:T(8,128)(2,1)}, bf16[128,512]{1,0:T(8,128)(2,1)S(1)}, u32[]{:S(2)}, u32[]{:S(2)}) collective-permute-start(bf16[128,512]{1,0:T(8,128)(2,1)} %features_ref.1), channel_id=1, source_target_pairs={{0,16},{8,24},{16,0},{24,8},{32,48},{40,56},{48,32},{56,40},{64,80... | collective-permute-start | bytes 393224 | tf_op jit(solution)/shard_map/ppermute | solution.py:50
  7.4 13.0 %collective-permute-start.4 = (bf16[256,512]{1,0:T(8,128)(2,1)S(1)}, bf16[256,512]{1,0:T(8,128)(2,1)S(1)}, u32[]{:S(2)}, u32[]{:S(2)}) collective-permute-start(bf16[256,512]{1,0:T(8,128)(2,1)S(1)} %pad_maximum_fusion.4), channel_id=1, source_target_pairs={{0,64},{8,200},{16,80},{24,216},{32,96},{40,232},{48,112},{56,248}... | collective-permute-start | bytes 786440 | tf_op jit(solution)/shard_map/ppermute | solution.py:50
  13.1 1.3 collective-permute-start.2
  14.5 19.3 %collective-permute-start.3 = (bf16[512,512]{1,0:T(8,128)(2,1)S(1)}, bf16[512,512]{1,0:T(8,128)(2,1)S(1)}, u32[]{:S(2)}, u32[]{:S(2)}) collective-permute-start(bf16[512,512]{1,0:T(8,128)(2,1)S(1)} %constant_dynamic-update-slice_fusion), channel_id=1, source_target_pairs={{0,32},{8,232},{16,48},{24,248},{32,64},{40,8},{48,80},{56,24},{64... | collective-permute-start | bytes 1572872 | tf_op jit(solution)/shard_map/ppermute | solution.py:50
  20.4 7.2 %collective-permute-start.11 = (bf16[128,512]{1,0:T(8,128)(2,1)S(1)}, bf16[128,512]{1,0:T(8,128)(2,1)S(1)}, u32[]{:S(2)}, u32[]{:S(2)}) collective-permute-start(bf16[128,512]{1,0:T(8,128)(2,1)S(1)} %slice.179), channel_id=1, source_target_pairs={{0,64},{8,200},{16,80},{24,216},{32,96},{40,232},{48,112},{56,248}... | collective-permute-start | bytes 393224 | tf_op jit(solution)/shard_map/ppermute | solution.py:50
  23.4 9.8 %collective-permute-start.8 = (bf16[256,512]{1,0:T(8,128)(2,1)S(1)}, bf16[256,512]{1,0:T(8,128)(2,1)S(1)}, u32[]{:S(2)}, u32[]{:S(2)}) collective-permute-start(bf16[256,512]{1,0:T(8,128)(2,1)S(1)} %collective-permute-done.4), channel_id=1, source_target_pairs={{0,32},{8,232},{16,48},{24,248},{32,64},{40,8},{48,80},{56,24},{64... | collective-permute-start | bytes 786440 | tf_op jit(solution)/shard_map/ppermute | solution.py:50
  23.4 7.4 %collective-permute-start.5 = (bf16[256,512]{1,0:T(8,128)(2,1)S(1)}, bf16[256,512]{1,0:T(8,128)(2,1)S(1)}, u32[]{:S(2)}, u32[]{:S(2)}) collective-permute-start(bf16[256,512]{1,0:T(8,128)(2,1)S(1)} %collective-permute-done.4), channel_id=1, source_target_pairs={{0,16},{8,24},{16,0},{24,8},{32,48},{40,56},{48,32},{56,40},{64,80... | collective-permute-start | bytes 786440 | tf_op jit(solution)/shard_map/ppermute | solution.py:50
  27.6 6.1 %collective-permute-start.12 = (bf16[128,512]{1,0:T(8,128)(2,1)S(1)}, bf16[128,512]{1,0:T(8,128)(2,1)S(1)}, u32[]{:S(2)}, u32[]{:S(2)}) collective-permute-start(bf16[128,512]{1,0:T(8,128)(2,1)S(1)} %collective-permute-done.11), channel_id=1, source_target_pairs={{0,16},{8,24},{16,0},{24,8},{32,48},{40,56},{48,32},{56,40},{64,80... | collective-permute-start | bytes 393224 | tf_op jit(solution)/shard_map/ppermute | solution.py:50
  30.8 11.9 %collective-permute-start.6 = (bf16[512,512]{1,0:T(8,128)(2,1)S(1)}, bf16[512,512]{1,0:T(8,128)(2,1)S(1)}, u32[]{:S(2)}, u32[]{:S(2)}) collective-permute-start(bf16[512,512]{1,0:T(8,128)(2,1)S(1)} %constant_dynamic-update-slice_fusion.4), channel_id=1, source_target_pairs={{0,8},{8,0},{16,24},{24,16},{32,40},{40,32},{48,56},{56,48},{64,72... | collective-permute-start | bytes 1572872 | tf_op jit(solution)/shard_map/ppermute | solution.py:50
  33.2 7.9 %collective-permute-start.9 = (bf16[256,512]{1,0:T(8,128)(2,1)S(1)}, bf16[256,512]{1,0:T(8,128)(2,1)S(1)}, u32[]{:S(2)}, u32[]{:S(2)}) collective-permute-start(bf16[256,512]{1,0:T(8,128)(2,1)S(1)} %collective-permute-done.8), channel_id=1, source_target_pairs={{0,16},{8,24},{16,0},{24,8},{32,48},{40,56},{48,32},{56,40},{64,80... | collective-permute-start | bytes 786440 | tf_op jit(solution)/shard_map/ppermute | solution.py:50
  35.2 8.3 %collective-permute-start.7 = (bf16[512,512]{1,0:T(8,128)(2,1)S(1)}, bf16[512,512]{1,0:T(8,128)(2,1)S(1)}, u32[]{:S(2)}, u32[]{:S(2)}) collective-permute-start(bf16[512,512]{1,0:T(8,128)(2,1)S(1)} %collective-permute-done.3), channel_id=1, source_target_pairs={{0,8},{8,0},{16,24},{24,16},{32,40},{40,32},{48,56},{56,48},{64,72... | collective-permute-start | bytes 1572872 | tf_op jit(solution)/shard_map/ppermute | solution.py:50
  41.1 3.4 %collective-permute-start.10 = (bf16[512,512]{1,0:T(8,128)(2,1)S(1)}, bf16[512,512]{1,0:T(8,128)(2,1)S(1)}, u32[]{:S(2)}, u32[]{:S(2)}) collective-permute-start(bf16[512,512]{1,0:T(8,128)(2,1)S(1)} %pad_maximum_fusion), channel_id=1, source_target_pairs={{0,8},{8,0},{16,24},{24,16},{32,40},{40,32},{48,56},{56,48},{64,72... | collective-permute-start | bytes 1572872 | tf_op jit(solution)/shard_map/ppermute | solution.py:50
  44.2 1.8 %collective-permute-start.13 = (bf16[256,512]{1,0:T(8,128)(2,1)S(1)}, bf16[256,512]{1,0:T(8,128)(2,1)S(1)}, u32[]{:S(2)}, u32[]{:S(2)}) collective-permute-start(bf16[256,512]{1,0:T(8,128)(2,1)S(1)} %pad_maximum_fusion.5), channel_id=1, source_target_pairs={{0,8},{8,0},{16,24},{24,16},{32,40},{40,32},{48,56},{56,48},{64,72... | collective-permute-start | bytes 786440 | tf_op jit(solution)/shard_map/ppermute | solution.py:50
  48.0 24.8 %copy-start = (bf16[128,512]{1,0:T(8,128)(2,1)S(1)}, bf16[128,512]{1,0:T(8,128)(2,1)}, u32[]{:S(2)}) copy-start(bf16[128,512]{1,0:T(8,128)(2,1)} %features_ref.1) | copy-start | bytes 393220
  48.0 24.8 %copy-start.1 = (bf16[512,512]{1,0:T(8,128)(2,1)S(1)}, bf16[512,512]{1,0:T(8,128)(2,1)}, u32[]{:S(2)}) copy-start(bf16[512,512]{1,0:T(8,128)(2,1)} %weight_ref.1) | copy-start | bytes 1572868
  48.0 24.8 %copy-start.2 = (bf16[128,512]{1,0:T(8,128)(2,1)S(1)}, bf16[128,512]{1,0:T(8,128)(2,1)}, u32[]{:S(2)}) copy-start(bf16[128,512]{1,0:T(8,128)(2,1)} %cotangent_ref.1) | copy-start | bytes 393220
  48.0 24.7 %copy-start.3 = (f32[512]{0:T(512)S(1)}, f32[512]{0:T(512)}, u32[]{:S(2)}) copy-start(f32[512]{0:T(512)} %param.10) | copy-start | bytes 6148
  101.0 5.0 %collective-permute-start.15 = (bf16[512,768]{1,0:T(8,128)(2,1)S(1)}, bf16[512,768]{1,0:T(8,128)(2,1)S(1)}, u32[]{:S(2)}, u32[]{:S(2)}) collective-permute-start(bf16[512,768]{1,0:T(8,128)(2,1)S(1)} %get-tuple-element.37), channel_id=1, source_target_pairs={{0,8},{8,0},{16,24},{24,16},{32,40},{40,32},{48,56},{56,48},{64,72... | collective-permute-start | bytes 2359304 | tf_op jit(solution)/shard_map/ppermute | solution.py:50
  103.7 2.3 %collective-permute-start.14 = (bf16[288,128]{1,0:T(8,128)(2,1)S(1)}, bf16[288,128]{1,0:T(8,128)(2,1)S(1)}, u32[]{:S(2)}, u32[]{:S(2)}) collective-permute-start(bf16[288,128]{1,0:T(8,128)(2,1)S(1)} %convert_element_type.88), channel_id=1, source_target_pairs={{0,8},{8,0},{16,24},{24,16},{32,40},{40,32},{48,56},{56,48},{64,72... | collective-permute-start | bytes 221192 | tf_op jit(solution)/shard_map/ppermute | solution.py:50
  105.4 5.5 %collective-permute-start.18 = (bf16[512,512]{1,0:T(8,128)(2,1)S(1)}, bf16[512,512]{1,0:T(8,128)(2,1)S(1)}, u32[]{:S(2)}, u32[]{:S(2)}) collective-permute-start(bf16[512,512]{1,0:T(8,128)(2,1)S(1)} %get-tuple-element.43), channel_id=1, source_target_pairs={{0,8},{8,0},{16,24},{24,16},{32,40},{40,32},{48,56},{56,48},{64,72... | collective-permute-start | bytes 1572872 | tf_op jit(solution)/shard_map/ppermute | solution.py:50
  106.3 12.4 %collective-permute-start.16 = (bf16[656,256]{1,0:T(8,128)(2,1)S(1)}, bf16[656,256]{1,0:T(8,128)(2,1)S(1)}, u32[]{:S(2)}, u32[]{:S(2)}) collective-permute-start(bf16[656,256]{1,0:T(8,128)(2,1)S(1)} %pad_maximum_fusion.2), channel_id=1, source_target_pairs={{0,16},{8,24},{16,0},{24,8},{32,48},{40,56},{48,32},{56,40},{64,80... | collective-permute-start | bytes 1007624 | tf_op jit(solution)/shard_map/ppermute | solution.py:50
  106.6 12.1 %collective-permute-start.20 = (bf16[512,128]{1,0:T(8,128)(2,1)S(1)}, bf16[512,128]{1,0:T(8,128)(2,1)S(1)}, u32[]{:S(2)}, u32[]{:S(2)}) collective-permute-start(bf16[512,128]{1,0:T(8,128)(2,1)S(1)} %slice.187), channel_id=1, source_target_pairs={{0,16},{8,24},{16,0},{24,8},{32,48},{40,56},{48,32},{56,40},{64,80... | collective-permute-start | bytes 393224 | tf_op jit(solution)/shard_map/ppermute | solution.py:50
  110.2 8.7 %collective-permute-start.17 = (bf16[512,512]{1,0:T(8,128)(2,1)S(1)}, bf16[512,512]{1,0:T(8,128)(2,1)S(1)}, u32[]{:S(2)}, u32[]{:S(2)}) collective-permute-start(bf16[512,512]{1,0:T(8,128)(2,1)S(1)} %get-tuple-element.41), channel_id=1, source_target_pairs={{0,8},{8,0},{16,24},{24,16},{32,40},{40,32},{48,56},{56,48},{64,72... | collective-permute-start | bytes 1572872 | tf_op jit(solution)/shard_map/ppermute | solution.py:50
  119.1 8.9 %collective-permute-start.21 = (bf16[800,128]{1,0:T(8,128)(2,1)S(1)}, bf16[800,128]{1,0:T(8,128)(2,1)S(1)}, u32[]{:S(2)}, u32[]{:S(2)}) collective-permute-start(bf16[800,128]{1,0:T(8,128)(2,1)S(1)} %pad_maximum_fusion.7), channel_id=1, source_target_pairs={{0,192},{8,72},{16,208},{24,88},{32,224},{40,104},{48,240},{56,120... | collective-permute-start | bytes 614408 | tf_op jit(solution)/shard_map/ppermute | solution.py:50
  119.3 12.5 %collective-permute-start.19 = (bf16[656,256]{1,0:T(8,128)(2,1)S(1)}, bf16[656,256]{1,0:T(8,128)(2,1)S(1)}, u32[]{:S(2)}, u32[]{:S(2)}) collective-permute-start(bf16[656,256]{1,0:T(8,128)(2,1)S(1)} %pad_maximum_fusion.3), channel_id=1, source_target_pairs={{0,224},{8,40},{16,240},{24,56},{32,0},{40,72},{48,16},{56,88},{64... | collective-permute-start | bytes 1007624 | tf_op jit(solution)/shard_map/ppermute | solution.py:50
  121.3 6.8 %collective-permute-start.22 = (bf16[512,256]{1,0:T(8,128)(2,1)S(1)}, bf16[512,256]{1,0:T(8,128)(2,1)S(1)}, u32[]{:S(2)}, u32[]{:S(2)}) collective-permute-start(bf16[512,256]{1,0:T(8,128)(2,1)S(1)} %slice.278), channel_id=1, source_target_pairs={{0,16},{8,24},{16,0},{24,8},{32,48},{40,56},{48,32},{56,40},{64,80... | collective-permute-start | bytes 786440 | tf_op jit(solution)/shard_map/ppermute | solution.py:50
  121.5 10.6 %collective-permute-start.26 = (bf16[512,256]{1,0:T(8,128)(2,1)S(1)}, bf16[512,256]{1,0:T(8,128)(2,1)S(1)}, u32[]{:S(2)}, u32[]{:S(2)}) collective-permute-start(bf16[512,256]{1,0:T(8,128)(2,1)S(1)} %get-tuple-element.51), channel_id=1, source_target_pairs={{0,8},{8,0},{16,24},{24,16},{32,40},{40,32},{48,56},{56,48},{64,72... | collective-permute-start | bytes 786440 | tf_op jit(solution)/shard_map/ppermute | solution.py:50
  123.4 17.1 %collective-permute-start.25 = (bf16[512,256]{1,0:T(8,128)(2,1)S(1)}, bf16[512,256]{1,0:T(8,128)(2,1)S(1)}, u32[]{:S(2)}, u32[]{:S(2)}) collective-permute-start(bf16[512,256]{1,0:T(8,128)(2,1)S(1)} %slice.279), channel_id=1, source_target_pairs={{0,16},{8,24},{16,0},{24,8},{32,48},{40,56},{48,32},{56,40},{64,80... | collective-permute-start | bytes 786440 | tf_op jit(solution)/shard_map/ppermute | solution.py:50
  132.0 6.7 %collective-permute-start.23 = (bf16[288,256]{1,0:T(8,128)(2,1)S(1)}, bf16[288,256]{1,0:T(8,128)(2,1)S(1)}, u32[]{:S(2)}, u32[]{:S(2)}) collective-permute-start(bf16[288,256]{1,0:T(8,128)(2,1)S(1)} %maximum_maximum_fusion), channel_id=1, source_target_pairs={{0,192},{8,72},{16,208},{24,88},{32,224},{40,104},{48,240},{56,120... | collective-permute-start | bytes 442376 | tf_op jit(solution)/shard_map/ppermute | solution.py:50
  132.2 15.4 %collective-permute-start.27 = (bf16[512,128]{1,0:T(8,128)(2,1)S(1)}, bf16[512,128]{1,0:T(8,128)(2,1)S(1)}, u32[]{:S(2)}, u32[]{:S(2)}) collective-permute-start(bf16[512,128]{1,0:T(8,128)(2,1)S(1)} %slice.280), channel_id=1, source_target_pairs={{0,16},{8,24},{16,0},{24,8},{32,48},{40,56},{48,32},{56,40},{64,80... | collective-permute-start | bytes 393224 | tf_op jit(solution)/shard_map/ppermute | solution.py:50
  138.7 4.4 %collective-permute-start.24 = (f32[144,256]{1,0:T(8,128)S(1)}, f32[144,256]{1,0:T(8,128)S(1)}, u32[]{:S(2)}, u32[]{:S(2)}) collective-permute-start(f32[144,256]{1,0:T(8,128)S(1)} %fusion.26), channel_id=1, source_target_pairs={{0,8},{8,0},{16,24},{24,16},{32,40},{40,32},{48,56},{56,48},{64,72... | collective-permute-start | bytes 442376 | tf_op jit(solution)/shard_map/ppermute | solution.py:50
  140.6 9.5 %collective-permute-start.29 = (bf16[512,256]{1,0:T(8,128)(2,1)S(1)}, bf16[512,256]{1,0:T(8,128)(2,1)S(1)}, u32[]{:S(2)}, u32[]{:S(2)}) collective-permute-start(bf16[512,256]{1,0:T(8,128)(2,1)S(1)} %fusion.21), channel_id=1, source_target_pairs={{0,224},{8,40},{16,240},{24,56},{32,0},{40,72},{48,16},{56,88},{64... | collective-permute-start | bytes 786440 | tf_op jit(solution)/shard_map/ppermute | solution.py:50
  140.7 9.4 %collective-permute-start.28 = (bf16[512,256]{1,0:T(8,128)(2,1)S(1)}, bf16[512,256]{1,0:T(8,128)(2,1)S(1)}, u32[]{:S(2)}, u32[]{:S(2)}) collective-permute-start(bf16[512,256]{1,0:T(8,128)(2,1)S(1)} %pad_maximum_fusion.6), channel_id=1, source_target_pairs={{0,192},{8,72},{16,208},{24,88},{32,224},{40,104},{48,240},{56,120... | collective-permute-start | bytes 786440 | tf_op jit(solution)/shard_map/ppermute | solution.py:50
  144.1 15.2 %all-to-all-start.2 = ((bf16[8,256,128]{2,1,0:T(8,128)(2,1)}), bf16[8,256,128]{2,1,0:T(8,128)(2,1)S(1)}, u32[]{:S(2)}, u32[]{:S(2)}) async-start(bf16[8,256,128]{2,1,0:T(8,128)(2,1)} %broadcast_in_dim.23), calls=%async_computation.2 | async-start | bytes 1048576 | tf_op jit(solution)/shard_map/all_to_all | solution.py:398
  150.1 1.6 %collective-permute-start.30 = (bf16[512,128]{1,0:T(8,128)(2,1)S(1)}, bf16[512,128]{1,0:T(8,128)(2,1)S(1)}, u32[]{:S(2)}, u32[]{:S(2)}) collective-permute-start(bf16[512,128]{1,0:T(8,128)(2,1)S(1)} %add_convert_fusion), channel_id=1, source_target_pairs={{0,8},{8,0},{16,24},{24,16},{32,40},{40,32},{48,56},{56,48},{64,72... | collective-permute-start | bytes 393224 | tf_op jit(solution)/shard_map/ppermute | solution.py:50

commit v2 on v1

--- a/solution.py
+++ b/solution.py
@@ -42,7 +42,7 @@
 
 
 OUT1, OUT2 = core_perm(1), core_perm(2)
-BACK1, BACK2 = core_perm(-1), core_perm(-2)
+BACK1, BACK2, BACK3, BACK4 = (core_perm(-hops) for hops in (1, 2, 3, 4))
 SIDE = layer_perm(0, 1, 0)
 CORE = layer_perm(0, 0, 1)
 
@@ -119,21 +119,23 @@
 
 def payload_kernel(total_ref, dense_ref, last_ref, degree_ref, out_ref):
     product = jnp.dot(dense_ref[0], last_ref[...], preferred_element_type=F32)
-    out_ref[0, 0:BLK, :] = (total_ref[...] + product).astype(BF)
-    out_ref[0, BLK : BLK + DEG, :] = degree_ref[0]
+    whole = (total_ref[...] + product).astype(BF)
+    for p in range(2):
+        out_ref[p, 0:BLK, :] = whole[p * BLK : (p + 1) * BLK]
+        out_ref[p, BLK : BLK + DEG, :] = degree_ref[p]
 
 
 def payload_of(total, dense, group, last, degree_rows):
     return pl.pallas_call(
         payload_kernel,
-        grid=(REPS,),
+        grid=(REPS // 2,),
         in_specs=[
-            pl.BlockSpec((BLK, F), lambda p: (p, 0)),
-            pl.BlockSpec((1, BLK, 4 * BLK), lambda p: (group, p, 0)),
+            pl.BlockSpec((2 * BLK, F), lambda p: (p, 0)),
+            pl.BlockSpec((1, 2 * BLK, 4 * BLK), lambda p: (group, p, 0)),
             pl.BlockSpec((4 * BLK, F), lambda p: (0, 0)),
-            pl.BlockSpec((1, DEG, F), lambda p: (p, 0, 0)),
+            pl.BlockSpec((2, DEG, F), lambda p: (p, 0, 0)),
         ],
-        out_specs=pl.BlockSpec((1, BLK + DEG, F), lambda p: (p, 0, 0)),
+        out_specs=pl.BlockSpec((2, BLK + DEG, F), lambda p: (p, 0, 0)),
         out_shape=jax.ShapeDtypeStruct((REPS, BLK + DEG, F), BF),
         compiler_params=pltpu.CompilerParams(vmem_limit_bytes=8 << 20),
         cost_estimate=pl.CostEstimate(
@@ -251,31 +253,36 @@
     )(left, dense)
 
 
-def forward(features, place, values):
+def forward(features, place_of, values):
     def dot(g, piece):
         return jnp.dot(dense[g], piece, preferred_element_type=F32)
 
     chain = jnp.concatenate([features, send(features, CORE)], axis=0)
     beside = send(features, SIDE)
     second = send(chain, OUT2)
+    place = place_of(chain)
+    early = place
     own = jnp.concatenate([chain, beside, send(beside, CORE)], axis=0)
+    early = after(early, own)
+    dense, degree_rows = spread_part(early, values, 0)
     first = send(own, OUT1)
-    dense, degree_rows = spread_part(after(place, own), values, 0)
     third = send(second, OUT1)
+    total = dot(0, own)
     fourth = send(second[:BLK], OUT2)
     both2 = jnp.concatenate([second, send(second, SIDE)], axis=0)
     cross2 = send(both2, CORE)
     cross1 = send(first, CORE)
     both3 = jnp.concatenate([third, send(third, SIDE)], axis=0)
     both4 = jnp.concatenate([fourth, send(fourth, SIDE)], axis=0)
-    total = dot(0, own) + dot(1, first) + dot(3, both2)
+    total = total + dot(1, first) + dot(3, both2)
+    total = total + dot(4, cross2) + dot(2, cross1)
+    both4 = after(both4, total)
+    last = jnp.concatenate([both4, send(both4, CORE)], axis=0)
+    total = total + dot(7, last)
     both3 = after(both3, total)
     cross3 = send(both3, CORE)
-    total = total + dot(4, cross2) + dot(2, cross1) + dot(5, both3)
-    both4 = after(both4, total)
-    last = jnp.concatenate([both4, send(both4, CORE)], axis=0)
-    total = total + dot(6, cross3)
-    return payload_of(total, dense, 7, last, degree_rows), dense
+    total = total + dot(5, both3)
+    return payload_of(total, dense, 6, cross3, degree_rows), dense
 
 
 def final_kernel(mine_ref, far_ref, near_ref, other_ref, scaled_ref, out_ref):
@@ -338,12 +345,12 @@
     side3 = stacked(line[:, 4 * BLK :], grads)
     got3 = wide_of(send(side3, SIDE))
     side4 = line[:, BLK : 2 * BLK].astype(BF)
+    away, mine = products(wide, dense, (4, 3), False)
+    line2 = mine + wide_of(after(send(away, CORE), side3))
+    side2 = line2[:, 2 * BLK :].astype(BF)
     got4 = wide_of(send(side4, SIDE))
-    away, mine = products(wide, dense, (4, 3), False)
-    line2 = mine + wide_of(after(send(away, CORE), side3, side4))
-    side2 = line2[:, 2 * BLK :].astype(BF)
     got2 = wide_of(send(side2, SIDE))
-    away1, mine1, away0, mine0 = products(after(wide, side3, side4), dense, (2, 1, 0), False)
+    away1, mine1, away0, mine0 = products(after(wide, side3), dense, (2, 1, 0), False)
     line1 = mine1 + wide_of(send(away1, CORE))
     side1 = after(line1[:, 2 * BLK :].astype(BF), side2)
     got1 = wide_of(send(side1, SIDE))
@@ -352,8 +359,10 @@
     quad0 = line0[:, :BLK] + wide_of(send(side0, SIDE))
 
     grads = grads + got3[F:]
-    quad3 = after(stacked(line[:, 2 * BLK : 4 * BLK] + got3[:F], grads), side1)
-    quad4 = after(stacked(line[:, :BLK] + got4, unfolded(grads)), side1)
+    quad3 = stacked(line[:, 2 * BLK : 4 * BLK] + got3[:F], grads)
+    quad4 = stacked(line[:, :BLK] + got4, unfolded(grads))
+    quad3 = after(quad3, side2)
+    quad4 = after(quad4, side2)
     came3 = send(quad3, BACK1)
     came4 = send(quad4, BACK2)
     quad2 = line2[:, : 2 * BLK] + got2 + wide_of(came3[:F])
@@ -363,31 +372,38 @@
     quad1 = (line1[:, : 2 * BLK] + got1).astype(BF)
     near = send(quad1, BACK1)
 
-    both = jnp.concatenate([came3[F:], folded(came4[F:])], axis=0)
-    more = wide_of(send(after(both, quad2), BACK2))
-    rows = both.shape[0] // 2
-    around = wide_of(both[:rows]) + wide_of(both[rows:]) + more[:rows] + 0.5 * more[rows:]
-    grads = after(grads + around + send(around, CORE), quad1)
+    own = grads.astype(BF)
+    own = after(own, quad3, quad4)
+    third = send(own, BACK3)
+    fourth = send(own, BACK4)
+    around = wide_of(came3[F:]) + wide_of(folded(came4[F:]))
+    around = around + wide_of(third) + 0.5 * wide_of(fourth)
+    got = send(around, CORE)
+    got = after(got, quad2)
+    grads = grads + around + got
 
     other = send((wide_of(far[:, BLK:]) + wide_of(near[:, BLK:])).astype(BF), CORE)
     return final_step(quad0, far, near, other, scaled_t), unfolded(grads)
 
 
 def per_device(features, block_columns, block_values, weight, bias_row, cotangent):
-    layer = lax.axis_index("layer")
-    z, y, c = layer // 4, (layer // 2) % 2, layer % 2
-    owner = jnp.where(block_columns >= 0, block_columns, 0) // REPS
-    dz = (owner // 4 - z + Z) % Z
-    dy = ((owner // 2) % 2 - y) % 2
-    dc = (owner % 2 - c) % 2
-    near = jnp.where(dz <= 4, dz, Z - dz)
-    other = ((dz > 4) != (c == 0)).astype(jnp.int32)
-    ends = (near == 0) | (near == 4)
-    group = jnp.where(near == 0, 0, jnp.where(near == 4, 7, 2 * near - 1 + other))
-    column = jnp.where(near == 4, 2 * dc + dy, 2 * dy + jnp.where(ends, dc, dc ^ other))
-    place = 4 * group + column
-    place = jnp.where(block_columns >= 0, place, place[:, 0:1]).astype(jnp.int32)
-    payload, dense = forward(features, place, block_values)
+    def place_of(chain):
+        layer = lax.axis_index("layer")
+        z, y, c = layer // 4, (layer // 2) % 2, layer % 2
+        columns = after(block_columns, chain)
+        owner = jnp.where(columns >= 0, columns, 0) // REPS
+        dz = (owner // 4 - z + Z) % Z
+        dy = ((owner // 2) % 2 - y) % 2
+        dc = (owner % 2 - c) % 2
+        near = jnp.where(dz <= 4, dz, Z - dz)
+        other = ((dz > 4) != (c == 0)).astype(jnp.int32)
+        ends = (near == 0) | (near == 4)
+        group = jnp.where(near == 0, 0, jnp.where(near == 4, 7, 2 * near - 1 + other))
+        column = jnp.where(near == 4, 2 * dc + dy, 2 * dy + jnp.where(ends, dc, dc ^ other))
+        place = 4 * group + column
+        return jnp.where(columns >= 0, place, place[:, 0:1]).astype(jnp.int32)
+
+    payload, dense = forward(features, place_of, block_values)
     got = lax.all_to_all(payload, "rep", 0, 0, tiled=True)
 
     activations, outgoing, scaled_t = node_step(got, features, weight, bias_row, cotangent)

time: 161 us -> 154 us (0.957)
  waiting for transfers between devices: 43.3 us -> 27.2 us
  starting transfers between devices: 38.5 us -> 48.9 us
    ppermute x31 -> x32, waiting for transfers between devices: 36.6 us -> 22.4 us  [send(): return lax.ppermute(value, 'layer', perm)]
    ppermute x31 -> x32, starting transfers between devices: 35 us -> 45.4 us  [send(): return lax.ppermute(value, 'layer', perm)]
    all_to_all x1, waiting for transfers between devices: 6.72 us -> 4.78 us  [per_device(): pieces = lax.all_to_all(mine, 'rep', 0, 0, tiled=True)]
  transfers between devices with their start and end apart: 32 -> 33, of which waited for: 12 -> 15; matrix products, arithmetic and copies ran while one was open for 7% -> 7% of each run, Pallas kernels for 6% -> 6%
where the time goes in v2:
time: 154 us; the launch traced here: 153 us
  blocking collectives  49.2 us (32%)
  starting transfers between devices  48.9 us (32%)
  waiting for transfers between devices  27.2 us (18%)
  Pallas kernels  15.9 us (10%)
  matrix products  5.03 us (3%)
  local copies, waits for them, and re-layouts  2.87 us (2%)
  other arithmetic  2.85 us (2%)
    ppermute x32, starting transfers between devices, send(): return lax.ppermute(value, 'layer', perm)  45.4 us
    all_to_all x1, blocking collectives, per_device(): got = lax.all_to_all(payload, 'rep', 0, 0, tiled=True)  24.8 us
    all_to_all x1, blocking collectives, per_device(): everyone = lax.all_to_all(outgoing, 'rep', 0, 0, tiled=True)  24.5 us
    ppermute x32, waiting for transfers between devices, send(): return lax.ppermute(value, 'layer', perm)  22.4 us
    pallas_call x3, Pallas kernels, products(): pl.pallas_call(functools.partial(product_kernel, groups, first), grid=(le...  6.66 us
    pallas_call x1, Pallas kernels, spread_part(): pl.pallas_call(functools.partial(spread_kernel, first), grid_spec=pltpu.P...  5.07 us
    dot_general x7, matrix products, dot(): return jnp.dot(dense[g], piece, preferred_element_type=F32)  5.03 us
    all_to_all x1, waiting for transfers between devices, per_device(): pieces = lax.all_to_all(mine, 'rep', 0, 0, tiled=True)  4.78 us
  transfers between devices with their start and end apart: 33, of which 15 were waited for; matrix products, arithmetic and copies ran while one was open for 7% of the time, Pallas kernels for 6%

profile of v2, /device:TPU:1, one launch (start us, length us, event | category | flops | bytes accessed | tf_op | source)
XLA Modules:
  0.0 153.1 jit_solution(10379025794340775531)
XLA Ops:
  0.6 3.3 %collective-permute-start = (bf16[128,512]{1,0:T(8,128)(2,1)}, bf16[128,512]{1,0:T(8,128)(2,1)S(1)}, u32[]{:S(2)}, u32[]{:S(2)}) collective-permute-start(bf16[128,512]{1,0:T(8,128)(2,1)} %features_ref.1), channel_id=1, source_target_pairs={{0,8},{8,0},{16,24},{24,16},{32,40},{40,32},{48,56},{56,48},{64,72... | collective-permute-start | bytes 393224 | tf_op jit(solution)/shard_map/ppermute | solution.py:50
  4.0 1.0 constant_dynamic-update-slice_fusion.5
  5.2 5.5 %collective-permute-start.4 = (bf16[256,512]{1,0:T(8,128)(2,1)S(1)}, bf16[256,512]{1,0:T(8,128)(2,1)S(1)}, u32[]{:S(2)}, u32[]{:S(2)}) collective-permute-start(bf16[256,512]{1,0:T(8,128)(2,1)S(1)} %get-tuple-element.65), channel_id=1, source_target_pairs={{0,64},{8,200},{16,80},{24,216},{32,96},{40,232},{48,112},{56,248}... | collective-permute-start | bytes 786440 | tf_op jit(solution)/shard_map/ppermute | solution.py:50
  10.6 0.7 fusion.31
  11.6 0.8 compare_select_fusion.1
  12.9 2.1 %collective-permute-start.3 = (bf16[512,512]{1,0:T(8,128)(2,1)S(1)}, bf16[512,512]{1,0:T(8,128)(2,1)S(1)}, u32[]{:S(2)}, u32[]{:S(2)}) collective-permute-start(bf16[512,512]{1,0:T(8,128)(2,1)S(1)} %constant_dynamic-update-slice_fusion.2), channel_id=1, source_target_pairs={{0,32},{8,232},{16,48},{24,248},{32,64},{40,8},{48,80},{56,24},{64... | collective-permute-start | bytes 1572872 | tf_op jit(solution)/shard_map/ppermute | solution.py:50
  15.1 5.1 %shard_map.93 = (bf16[8,1024,512]{2,1,0:T(8,128)(2,1)S(1)}, bf16[8,16,512]{2,1,0:T(8,128)(2,1)S(1)}) custom-call(s32[128]{0:T(128)S(1)} %reshape.18.place_ref, s32[8,16,128,128]{3,2,1,0:T(8,128)} %values_ref.1), custom_call_target="tpu_custom_call" | custom-call | flops 2097152 | bytes 8388608 | tf_op jit(solution)/shard_map/pallas_call | solution.py:94
  20.2 1.2 collective-permute-start.8
  21.4 1.3 collective-permute-start.5
  23.4 0.8 collective-permute-start.11
  24.3 2.4 %collective-permute-done.8 = bf16[128,512]{1,0:T(8,128)(2,1)S(1)} collective-permute-done((bf16[128,512]{1,0:T(8,128)(2,1)S(1)}, bf16[128,512]{1,0:T(8,128)(2,1)S(1)}, u32[]{:S(2)}, u32[]{:S(2)}) %collective-permute-start.8) | collective-permute-done | bytes 131104 | tf_op jit(solution)/shard_map/ppermute | solution.py:50
  27.2 2.3 %collective-permute-done.5 = bf16[256,512]{1,0:T(8,128)(2,1)S(1)} collective-permute-done((bf16[256,512]{1,0:T(8,128)(2,1)S(1)}, bf16[256,512]{1,0:T(8,128)(2,1)S(1)}, u32[]{:S(2)}, u32[]{:S(2)}) %collective-permute-start.5) | collective-permute-done | bytes 262176 | tf_op jit(solution)/shard_map/ppermute | solution.py:50
  29.5 1.1 collective-permute-start.6
  30.6 0.7 fusion.5
  31.6 1.5 collective-permute-start.7
  33.8 0.7 fusion.3
  34.6 0.8 add_add_fusion
  35.9 3.4 %collective-permute-done.12 = bf16[256,512]{1,0:T(8,128)(2,1)S(1)} collective-permute-done((bf16[256,512]{1,0:T(8,128)(2,1)S(1)}, bf16[256,512]{1,0:T(8,128)(2,1)S(1)}, u32[]{:S(2)}, u32[]{:S(2)}) %collective-permute-start.12) | collective-permute-done | bytes 262176 | tf_op jit(solution)/shard_map/ppermute | solution.py:50
  39.4 0.7 convolution_add_fusion.1
  40.1 1.1 collective-permute-start.13
  41.1 0.7 convolution_add_fusion.total_ref
  41.8 0.8 collective-permute-done.13.last_ref
  42.7 1.3 shard_map.94
  44.0 24.8 %all_to_all.15.got_ref = bf16[8,144,512]{2,1,0:T(8,128)(2,1)S(1)} all-to-all(bf16[8,144,512]{2,1,0:T(8,128)(2,1)S(1)} %shard_map.94), channel_id=1, replica_groups=mesh['layer'=32,'rep'=8] {'rep'}, dimensions={0} | all-to-all | bytes 2359296 | tf_op jit(solution)/shard_map/all_to_all | solution.py:407
  68.8 1.0 shard_map.95
  69.8 24.5 %all_to_all.16.left_ref = bf16[8,800,128]{2,1,0:T(8,128)(2,1)S(1)} all-to-all(bf16[8,800,128]{2,1,0:T(8,128)(2,1)S(1)} %get-tuple-element.37), channel_id=1, replica_groups=mesh['layer'=32,'rep'=8] {'rep'}, dimensions={0} | all-to-all | bytes 3276800 | tf_op jit(solution)/shard_map/all_to_all | solution.py:410
  94.3 2.7 %shard_map.96 = (bf16[512,768]{1,0:T(8,128)(2,1)S(1)}, f32[512,768]{1,0:T(8,128)S(1)}, bf16[512,1024]{1,0:T(8,128)(2,1)S(1)}) custom-call(bf16[8,800,128]{2,1,0:T(8,128)(2,1)S(1)} %all_to_all.16.left_ref, bf16[8,1024,512]{2,1,0:T(8,128)(2,1)S(1)} %get-tuple-element.32.dense_ref), custom_call_target="tpu_custom_call" | custom-call | flops 1610612736 | bytes 7864320 | tf_op jit(solution)/shard_map/pallas_call | solution.py:238
  97.0 2.6 %collective-permute-start.15 = (bf16[512,768]{1,0:T(8,128)(2,1)S(1)}, bf16[512,768]{1,0:T(8,128)(2,1)S(1)}, u32[]{:S(2)}, u32[]{:S(2)}) collective-permute-start(bf16[512,768]{1,0:T(8,128)(2,1)S(1)} %get-tuple-element.39), channel_id=1, source_target_pairs={{0,8},{8,0},{16,24},{24,16},{32,40},{40,32},{48,56},{56,48},{64,72... | collective-permute-start | bytes 2359304 | tf_op jit(solution)/shard_map/ppermute | solution.py:50
  99.8 1.6 %shard_map.97 = (bf16[512,512]{1,0:T(8,128)(2,1)S(1)}, f32[512,512]{1,0:T(8,128)S(1)}) custom-call(bf16[512,1024]{1,0:T(8,128)(2,1)S(1)} %get-tuple-element.48.left_ref, bf16[8,1024,512]{2,1,0:T(8,128)(2,1)S(1)} %get-tuple-element.32.dense_ref), custom_call_target="tpu_custom_call" | custom-call | flops 1073741824 | bytes 5242880 | tf_op jit(solution)/shard_map/pallas_call | solution.py:238
  102.4 2.4 %shard_map.99 = (bf16[512,512]{1,0:T(8,128)(2,1)S(1)}, f32[512,512]{1,0:T(8,128)S(1)}, bf16[512,256]{1,0:T(8,128)(2,1)S(1)}, f32[512,256]{1,0:T(8,128)S(1)}) custom-call(bf16[512,1024]{1,0:T(8,128)(2,1)S(1)} %get-tuple-element.48.left_ref, bf16[8,1024,512]{2,1,0:T(8,128)(2,1)S(1)} %get-tuple-element.32.dense_ref), custom_call_target="tpu_custom_call" | custom-call | flops 1610612736 | bytes 7864320 | tf_op jit(solution)/shard_map/pallas_call | solution.py:238
  104.9 1.7 %collective-permute-start.19 = (bf16[512,128]{1,0:T(8,128)(2,1)S(1)}, bf16[512,128]{1,0:T(8,128)(2,1)S(1)}, u32[]{:S(2)}, u32[]{:S(2)}) collective-permute-start(bf16[512,128]{1,0:T(8,128)(2,1)S(1)} %slice.182), channel_id=1, source_target_pairs={{0,16},{8,24},{16,0},{24,8},{32,48},{40,56},{48,32},{56,40},{64,80... | collective-permute-start | bytes 393224 | tf_op jit(solution)/shard_map/ppermute | solution.py:50
  107.4 7.2 %collective-permute-done.19 = bf16[512,128]{1,0:T(8,128)(2,1)S(1)} collective-permute-done((bf16[512,128]{1,0:T(8,128)(2,1)S(1)}, bf16[512,128]{1,0:T(8,128)(2,1)S(1)}, u32[]{:S(2)}, u32[]{:S(2)}) %collective-permute-start.19) | collective-permute-done | bytes 131104 | tf_op jit(solution)/shard_map/ppermute | solution.py:50
  115.0 2.1 %collective-permute-start.18 = (bf16[656,256]{1,0:T(8,128)(2,1)S(1)}, bf16[656,256]{1,0:T(8,128)(2,1)S(1)}, u32[]{:S(2)}, u32[]{:S(2)}) collective-permute-start(bf16[656,256]{1,0:T(8,128)(2,1)S(1)} %pad_maximum_fusion.2), channel_id=1, source_target_pairs={{0,224},{8,40},{16,240},{24,56},{32,0},{40,72},{48,16},{56,88},{64... | collective-permute-start | bytes 1007624 | tf_op jit(solution)/shard_map/ppermute | solution.py:50
  117.2 1.5 collective-permute-start.21
  118.7 4.2 %collective-permute-start.22 = (bf16[144,256]{1,0:T(8,128)(2,1)S(1)}, bf16[144,256]{1,0:T(8,128)(2,1)S(1)}, u32[]{:S(2)}, u32[]{:S(2)}) collective-permute-start(bf16[144,256]{1,0:T(8,128)(2,1)S(1)} %fusion.27), channel_id=1, source_target_pairs={{0,128},{8,136},{16,144},{24,152},{32,160},{40,168},{48,176},{56,1... | collective-permute-start | bytes 221192 | tf_op jit(solution)/shard_map/ppermute | solution.py:50
  123.1 2.3 %collective-permute-done.20 = bf16[800,128]{1,0:T(8,128)(2,1)S(1)} collective-permute-done((bf16[800,128]{1,0:T(8,128)(2,1)S(1)}, bf16[800,128]{1,0:T(8,128)(2,1)S(1)}, u32[]{:S(2)}, u32[]{:S(2)}) %collective-permute-start.20) | collective-permute-done | bytes 204832 | tf_op jit(solution)/shard_map/ppermute | solution.py:50
  125.3 1.2 collective-permute-start.29
  127.1 2.9 %collective-permute-start.28 = (bf16[512,256]{1,0:T(8,128)(2,1)S(1)}, bf16[512,256]{1,0:T(8,128)(2,1)S(1)}, u32[]{:S(2)}, u32[]{:S(2)}) collective-permute-start(bf16[512,256]{1,0:T(8,128)(2,1)S(1)} %pad_maximum_fusion.4), channel_id=1, source_target_pairs={{0,192},{8,72},{16,208},{24,88},{32,224},{40,104},{48,240},{56,120... | collective-permute-start | bytes 786440 | tf_op jit(solution)/shard_map/ppermute | solution.py:50
  130.0 1.1 collective-permute-done.22
  131.2 4.4 %collective-permute-start.23 = (f32[144,256]{1,0:T(8,128)S(1)}, f32[144,256]{1,0:T(8,128)S(1)}, u32[]{:S(2)}, u32[]{:S(2)}) collective-permute-start(f32[144,256]{1,0:T(8,128)S(1)} %multiply_add_fusion), channel_id=1, source_target_pairs={{0,8},{8,0},{16,24},{24,16},{32,40},{40,32},{48,56},{56,48},{64,72... | collective-permute-start | bytes 442376 | tf_op jit(solution)/shard_map/ppermute | solution.py:50
  135.6 0.7 collective-permute-start.30
  136.6 0.9 broadcast_in_dim.23
  137.5 3.5 %all-to-all-start.2 = ((bf16[8,256,128]{2,1,0:T(8,128)(2,1)}), bf16[8,256,128]{2,1,0:T(8,128)(2,1)S(1)}, u32[]{:S(2)}, u32[]{:S(2)}) async-start(bf16[8,256,128]{2,1,0:T(8,128)(2,1)} %broadcast_in_dim.23), calls=%async_computation.2 | async-start | bytes 1048576 | tf_op jit(solution)/shard_map/all_to_all | solution.py:414
  141.1 1.1 collective-permute-done.30.near_ref
  142.2 3.3 %collective-permute-start.31 = (bf16[512,128]{1,0:T(8,128)(2,1)S(1)}, bf16[512,128]{1,0:T(8,128)(2,1)S(1)}, u32[]{:S(2)}, u32[]{:S(2)}) collective-permute-start(bf16[512,128]{1,0:T(8,128)(2,1)S(1)} %add_convert_fusion), channel_id=1, source_target_pairs={{0,8},{8,0},{16,24},{24,16},{32,40},{40,32},{48,56},{56,48},{64,72... | collective-permute-start | bytes 393224 | tf_op jit(solution)/shard_map/ppermute | solution.py:50
  146.5 0.8 shard_map.100
  147.3 4.8 %all-to-all-done.2.pieces_ref = bf16[8,256,128]{2,1,0:T(8,128)(2,1)S(1)} async-done(((bf16[8,256,128]{2,1,0:T(8,128)(2,1)}), bf16[8,256,128]{2,1,0:T(8,128)(2,1)S(1)}, u32[]{:S(2)}, u32[]{:S(2)}) %all-to-all-start.2) | async-done | bytes 524320 | tf_op jit(solution)/shard_map/all_to_all | solution.py:414
  152.1 1.0 shard_map.98
  (92 shorter events, 8.6 us)
Async XLA Ops:
  0.6 4.5 %collective-permute-start = (bf16[128,512]{1,0:T(8,128)(2,1)}, bf16[128,512]{1,0:T(8,128)(2,1)S(1)}, u32[]{:S(2)}, u32[]{:S(2)}) collective-permute-start(bf16[128,512]{1,0:T(8,128)(2,1)} %features_ref.1), channel_id=1, source_target_pairs={{0,8},{8,0},{16,24},{24,16},{32,40},{40,32},{48,56},{56,48},{64,72... | collective-permute-start | bytes 393224 | tf_op jit(solution)/shard_map/ppermute | solution.py:50
  4.0 7.5 %collective-permute-start.1 = (bf16[128,512]{1,0:T(8,128)(2,1)}, bf16[128,512]{1,0:T(8,128)(2,1)S(1)}, u32[]{:S(2)}, u32[]{:S(2)}) collective-permute-start(bf16[128,512]{1,0:T(8,128)(2,1)} %features_ref.1), channel_id=1, source_target_pairs={{0,16},{8,24},{16,0},{24,8},{32,48},{40,56},{48,32},{56,40},{64,80... | collective-permute-start | bytes 393224 | tf_op jit(solution)/shard_map/ppermute | solution.py:50
  5.2 15.0 %collective-permute-start.4 = (bf16[256,512]{1,0:T(8,128)(2,1)S(1)}, bf16[256,512]{1,0:T(8,128)(2,1)S(1)}, u32[]{:S(2)}, u32[]{:S(2)}) collective-permute-start(bf16[256,512]{1,0:T(8,128)(2,1)S(1)} %get-tuple-element.65), channel_id=1, source_target_pairs={{0,64},{8,200},{16,80},{24,216},{32,96},{40,232},{48,112},{56,248}... | collective-permute-start | bytes 786440 | tf_op jit(solution)/shard_map/ppermute | solution.py:50
  11.5 1.4 collective-permute-start.2
  12.9 18.7 %collective-permute-start.3 = (bf16[512,512]{1,0:T(8,128)(2,1)S(1)}, bf16[512,512]{1,0:T(8,128)(2,1)S(1)}, u32[]{:S(2)}, u32[]{:S(2)}) collective-permute-start(bf16[512,512]{1,0:T(8,128)(2,1)S(1)} %constant_dynamic-update-slice_fusion.2), channel_id=1, source_target_pairs={{0,32},{8,232},{16,48},{24,248},{32,64},{40,8},{48,80},{56,24},{64... | collective-permute-start | bytes 1572872 | tf_op jit(solution)/shard_map/ppermute | solution.py:50
  20.2 6.5 %collective-permute-start.8 = (bf16[128,512]{1,0:T(8,128)(2,1)S(1)}, bf16[128,512]{1,0:T(8,128)(2,1)S(1)}, u32[]{:S(2)}, u32[]{:S(2)}) collective-permute-start(bf16[128,512]{1,0:T(8,128)(2,1)S(1)} %slice.171), channel_id=1, source_target_pairs={{0,64},{8,200},{16,80},{24,216},{32,96},{40,232},{48,112},{56,248}... | collective-permute-start | bytes 393224 | tf_op jit(solution)/shard_map/ppermute | solution.py:50
  21.4 8.0 %collective-permute-start.5 = (bf16[256,512]{1,0:T(8,128)(2,1)S(1)}, bf16[256,512]{1,0:T(8,128)(2,1)S(1)}, u32[]{:S(2)}, u32[]{:S(2)}) collective-permute-start(bf16[256,512]{1,0:T(8,128)(2,1)S(1)} %collective-permute-done.4), channel_id=1, source_target_pairs={{0,16},{8,24},{16,0},{24,8},{32,48},{40,56},{48,32},{56,40},{64,80... | collective-permute-start | bytes 786440 | tf_op jit(solution)/shard_map/ppermute | solution.py:50
  23.4 7.8 %collective-permute-start.11 = (bf16[256,512]{1,0:T(8,128)(2,1)S(1)}, bf16[256,512]{1,0:T(8,128)(2,1)S(1)}, u32[]{:S(2)}, u32[]{:S(2)}) collective-permute-start(bf16[256,512]{1,0:T(8,128)(2,1)S(1)} %collective-permute-done.4), channel_id=1, source_target_pairs={{0,32},{8,232},{16,48},{24,248},{32,64},{40,8},{48,80},{56,24},{64... | collective-permute-start | bytes 786440 | tf_op jit(solution)/shard_map/ppermute | solution.py:50
  26.7 4.9 %collective-permute-start.9 = (bf16[128,512]{1,0:T(8,128)(2,1)S(1)}, bf16[128,512]{1,0:T(8,128)(2,1)S(1)}, u32[]{:S(2)}, u32[]{:S(2)}) collective-permute-start(bf16[128,512]{1,0:T(8,128)(2,1)S(1)} %collective-permute-done.8), channel_id=1, source_target_pairs={{0,16},{8,24},{16,0},{24,8},{32,48},{40,56},{48,32},{56,40},{64,80... | collective-permute-start | bytes 393224 | tf_op jit(solution)/shard_map/ppermute | solution.py:50
  29.5 4.3 %collective-permute-start.6 = (bf16[512,512]{1,0:T(8,128)(2,1)S(1)}, bf16[512,512]{1,0:T(8,128)(2,1)S(1)}, u32[]{:S(2)}, u32[]{:S(2)}) collective-permute-start(bf16[512,512]{1,0:T(8,128)(2,1)S(1)} %constant_dynamic-update-slice_fusion.6), channel_id=1, source_target_pairs={{0,8},{8,0},{16,24},{24,16},{32,40},{40,32},{48,56},{56,48},{64,72... | collective-permute-start | bytes 1572872 | tf_op jit(solution)/shard_map/ppermute | solution.py:50
  31.3 8.0 %collective-permute-start.12 = (bf16[256,512]{1,0:T(8,128)(2,1)S(1)}, bf16[256,512]{1,0:T(8,128)(2,1)S(1)}, u32[]{:S(2)}, u32[]{:S(2)}) collective-permute-start(bf16[256,512]{1,0:T(8,128)(2,1)S(1)} %collective-permute-done.11), channel_id=1, source_target_pairs={{0,16},{8,24},{16,0},{24,8},{32,48},{40,56},{48,32},{56,40},{64,80... | collective-permute-start | bytes 786440 | tf_op jit(solution)/shard_map/ppermute | solution.py:50
  31.6 3.0 %collective-permute-start.7 = (bf16[512,512]{1,0:T(8,128)(2,1)S(1)}, bf16[512,512]{1,0:T(8,128)(2,1)S(1)}, u32[]{:S(2)}, u32[]{:S(2)}) collective-permute-start(bf16[512,512]{1,0:T(8,128)(2,1)S(1)} %collective-permute-done.3), channel_id=1, source_target_pairs={{0,8},{8,0},{16,24},{24,16},{32,40},{40,32},{48,56},{56,48},{64,72... | collective-permute-start | bytes 1572872 | tf_op jit(solution)/shard_map/ppermute | solution.py:50
  35.5 3.9 %collective-permute-start.10 = (bf16[256,512]{1,0:T(8,128)(2,1)S(1)}, bf16[256,512]{1,0:T(8,128)(2,1)S(1)}, u32[]{:S(2)}, u32[]{:S(2)}) collective-permute-start(bf16[256,512]{1,0:T(8,128)(2,1)S(1)} %pad_maximum_fusion.3), channel_id=1, source_target_pairs={{0,8},{8,0},{16,24},{24,16},{32,40},{40,32},{48,56},{56,48},{64,72... | collective-permute-start | bytes 786440 | tf_op jit(solution)/shard_map/ppermute | solution.py:50
  40.1 2.6 %collective-permute-start.13 = (bf16[512,512]{1,0:T(8,128)(2,1)S(1)}, bf16[512,512]{1,0:T(8,128)(2,1)S(1)}, u32[]{:S(2)}, u32[]{:S(2)}) collective-permute-start(bf16[512,512]{1,0:T(8,128)(2,1)S(1)} %pad_maximum_fusion), channel_id=1, source_target_pairs={{0,8},{8,0},{16,24},{24,16},{32,40},{40,32},{48,56},{56,48},{64,72... | collective-permute-start | bytes 1572872 | tf_op jit(solution)/shard_map/ppermute | solution.py:50
  43.9 24.8 %copy-start = (bf16[512,512]{1,0:T(8,128)(2,1)S(1)}, bf16[512,512]{1,0:T(8,128)(2,1)}, u32[]{:S(2)}) copy-start(bf16[512,512]{1,0:T(8,128)(2,1)} %weight_ref.1) | copy-start | bytes 1572868
  43.9 24.8 %copy-start.1 = (bf16[128,512]{1,0:T(8,128)(2,1)S(1)}, bf16[128,512]{1,0:T(8,128)(2,1)}, u32[]{:S(2)}) copy-start(bf16[128,512]{1,0:T(8,128)(2,1)} %features_ref.1) | copy-start | bytes 393220
  43.9 24.8 %copy-start.2 = (bf16[128,512]{1,0:T(8,128)(2,1)S(1)}, bf16[128,512]{1,0:T(8,128)(2,1)}, u32[]{:S(2)}) copy-start(bf16[128,512]{1,0:T(8,128)(2,1)} %cotangent_ref.1) | copy-start | bytes 393220
  44.0 24.8 %copy-start.3 = (f32[512]{0:T(512)S(1)}, f32[512]{0:T(512)}, u32[]{:S(2)}) copy-start(f32[512]{0:T(512)} %param.10) | copy-start | bytes 6148
  97.0 5.0 %collective-permute-start.15 = (bf16[512,768]{1,0:T(8,128)(2,1)S(1)}, bf16[512,768]{1,0:T(8,128)(2,1)S(1)}, u32[]{:S(2)}, u32[]{:S(2)}) collective-permute-start(bf16[512,768]{1,0:T(8,128)(2,1)S(1)} %get-tuple-element.39), channel_id=1, source_target_pairs={{0,8},{8,0},{16,24},{24,16},{32,40},{40,32},{48,56},{56,48},{64,72... | collective-permute-start | bytes 2359304 | tf_op jit(solution)/shard_map/ppermute | solution.py:50
  99.7 2.3 %collective-permute-start.14 = (bf16[288,128]{1,0:T(8,128)(2,1)S(1)}, bf16[288,128]{1,0:T(8,128)(2,1)S(1)}, u32[]{:S(2)}, u32[]{:S(2)}) collective-permute-start(bf16[288,128]{1,0:T(8,128)(2,1)S(1)} %convert_element_type.92), channel_id=1, source_target_pairs={{0,8},{8,0},{16,24},{24,16},{32,40},{40,32},{48,56},{56,48},{64,72... | collective-permute-start | bytes 221192 | tf_op jit(solution)/shard_map/ppermute | solution.py:50
  101.4 3.5 %collective-permute-start.17 = (bf16[512,512]{1,0:T(8,128)(2,1)S(1)}, bf16[512,512]{1,0:T(8,128)(2,1)S(1)}, u32[]{:S(2)}, u32[]{:S(2)}) collective-permute-start(bf16[512,512]{1,0:T(8,128)(2,1)S(1)} %get-tuple-element.42), channel_id=1, source_target_pairs={{0,8},{8,0},{16,24},{24,16},{32,40},{40,32},{48,56},{56,48},{64,72... | collective-permute-start | bytes 1572872 | tf_op jit(solution)/shard_map/ppermute | solution.py:50
  102.3 12.5 %collective-permute-start.16 = (bf16[656,256]{1,0:T(8,128)(2,1)S(1)}, bf16[656,256]{1,0:T(8,128)(2,1)S(1)}, u32[]{:S(2)}, u32[]{:S(2)}) collective-permute-start(bf16[656,256]{1,0:T(8,128)(2,1)S(1)} %pad_maximum_fusion.1), channel_id=1, source_target_pairs={{0,16},{8,24},{16,0},{24,8},{32,48},{40,56},{48,32},{56,40},{64,80... | collective-permute-start | bytes 1007624 | tf_op jit(solution)/shard_map/ppermute | solution.py:50
  104.8 13.9 %collective-permute-start.26 = (bf16[512,512]{1,0:T(8,128)(2,1)S(1)}, bf16[512,512]{1,0:T(8,128)(2,1)S(1)}, u32[]{:S(2)}, u32[]{:S(2)}) collective-permute-start(bf16[512,512]{1,0:T(8,128)(2,1)S(1)} %get-tuple-element.52), channel_id=1, source_target_pairs={{0,8},{8,0},{16,24},{24,16},{32,40},{40,32},{48,56},{56,48},{64,72... | collective-permute-start | bytes 1572872 | tf_op jit(solution)/shard_map/ppermute | solution.py:50
  104.9 9.7 %collective-permute-start.19 = (bf16[512,128]{1,0:T(8,128)(2,1)S(1)}, bf16[512,128]{1,0:T(8,128)(2,1)S(1)}, u32[]{:S(2)}, u32[]{:S(2)}) collective-permute-start(bf16[512,128]{1,0:T(8,128)(2,1)S(1)} %slice.182), channel_id=1, source_target_pairs={{0,16},{8,24},{16,0},{24,8},{32,48},{40,56},{48,32},{56,40},{64,80... | collective-permute-start | bytes 393224 | tf_op jit(solution)/shard_map/ppermute | solution.py:50
  106.6 8.0 %collective-permute-start.25 = (bf16[512,256]{1,0:T(8,128)(2,1)S(1)}, bf16[512,256]{1,0:T(8,128)(2,1)S(1)}, u32[]{:S(2)}, u32[]{:S(2)}) collective-permute-start(bf16[512,256]{1,0:T(8,128)(2,1)S(1)} %get-tuple-element.50), channel_id=1, source_target_pairs={{0,8},{8,0},{16,24},{24,16},{32,40},{40,32},{48,56},{56,48},{64,72... | collective-permute-start | bytes 786440 | tf_op jit(solution)/shard_map/ppermute | solution.py:50
  107.3 19.2 %collective-permute-start.24 = (bf16[512,256]{1,0:T(8,128)(2,1)S(1)}, bf16[512,256]{1,0:T(8,128)(2,1)S(1)}, u32[]{:S(2)}, u32[]{:S(2)}) collective-permute-start(bf16[512,256]{1,0:T(8,128)(2,1)S(1)} %slice.264), channel_id=1, source_target_pairs={{0,16},{8,24},{16,0},{24,8},{32,48},{40,56},{48,32},{56,40},{64,80... | collective-permute-start | bytes 786440 | tf_op jit(solution)/shard_map/ppermute | solution.py:50
  115.0 11.9 %collective-permute-start.18 = (bf16[656,256]{1,0:T(8,128)(2,1)S(1)}, bf16[656,256]{1,0:T(8,128)(2,1)S(1)}, u32[]{:S(2)}, u32[]{:S(2)}) collective-permute-start(bf16[656,256]{1,0:T(8,128)(2,1)S(1)} %pad_maximum_fusion.2), channel_id=1, source_target_pairs={{0,224},{8,40},{16,240},{24,56},{32,0},{40,72},{48,16},{56,88},{64... | collective-permute-start | bytes 1007624 | tf_op jit(solution)/shard_map/ppermute | solution.py:50
  117.1 8.2 %collective-permute-start.20 = (bf16[800,128]{1,0:T(8,128)(2,1)S(1)}, bf16[800,128]{1,0:T(8,128)(2,1)S(1)}, u32[]{:S(2)}, u32[]{:S(2)}) collective-permute-start(bf16[800,128]{1,0:T(8,128)(2,1)S(1)} %pad_maximum_fusion.5), channel_id=1, source_target_pairs={{0,192},{8,72},{16,208},{24,88},{32,224},{40,104},{48,240},{56,120... | collective-permute-start | bytes 614408 | tf_op jit(solution)/shard_map/ppermute | solution.py:50
  117.2 12.8 %collective-permute-start.21 = (bf16[144,256]{1,0:T(8,128)(2,1)S(1)}, bf16[144,256]{1,0:T(8,128)(2,1)S(1)}, u32[]{:S(2)}, u32[]{:S(2)}) collective-permute-start(bf16[144,256]{1,0:T(8,128)(2,1)S(1)} %fusion.27), channel_id=1, source_target_pairs={{0,160},{8,104},{16,176},{24,120},{32,192},{40,136},{48,208},{56,1... | collective-permute-start | bytes 221192 | tf_op jit(solution)/shard_map/ppermute | solution.py:50
  118.7 12.4 %collective-permute-start.22 = (bf16[144,256]{1,0:T(8,128)(2,1)S(1)}, bf16[144,256]{1,0:T(8,128)(2,1)S(1)}, u32[]{:S(2)}, u32[]{:S(2)}) collective-permute-start(bf16[144,256]{1,0:T(8,128)(2,1)S(1)} %fusion.27), channel_id=1, source_target_pairs={{0,128},{8,136},{16,144},{24,152},{32,160},{40,168},{48,176},{56,1... | collective-permute-start | bytes 221192 | tf_op jit(solution)/shard_map/ppermute | solution.py:50
  125.3 10.2 %collective-permute-start.29 = (bf16[512,256]{1,0:T(8,128)(2,1)S(1)}, bf16[512,256]{1,0:T(8,128)(2,1)S(1)}, u32[]{:S(2)}, u32[]{:S(2)}) collective-permute-start(bf16[512,256]{1,0:T(8,128)(2,1)S(1)} %slice.263), channel_id=1, source_target_pairs={{0,16},{8,24},{16,0},{24,8},{32,48},{40,56},{48,32},{56,40},{64,80... | collective-permute-start | bytes 786440 | tf_op jit(solution)/shard_map/ppermute | solution.py:50
  126.5 14.5 %collective-permute-start.27 = (bf16[512,128]{1,0:T(8,128)(2,1)S(1)}, bf16[512,128]{1,0:T(8,128)(2,1)S(1)}, u32[]{:S(2)}, u32[]{:S(2)}) collective-permute-start(bf16[512,128]{1,0:T(8,128)(2,1)S(1)} %slice.265), channel_id=1, source_target_pairs={{0,16},{8,24},{16,0},{24,8},{32,48},{40,56},{48,32},{56,40},{64,80... | collective-permute-start | bytes 393224 | tf_op jit(solution)/shard_map/ppermute | solution.py:50
  127.1 13.9 %collective-permute-start.28 = (bf16[512,256]{1,0:T(8,128)(2,1)S(1)}, bf16[512,256]{1,0:T(8,128)(2,1)S(1)}, u32[]{:S(2)}, u32[]{:S(2)}) collective-permute-start(bf16[512,256]{1,0:T(8,128)(2,1)S(1)} %pad_maximum_fusion.4), channel_id=1, source_target_pairs={{0,192},{8,72},{16,208},{24,88},{32,224},{40,104},{48,240},{56,120... | collective-permute-start | bytes 786440 | tf_op jit(solution)/shard_map/ppermute | solution.py:50
  131.2 5.4 %collective-permute-start.23 = (f32[144,256]{1,0:T(8,128)S(1)}, f32[144,256]{1,0:T(8,128)S(1)}, u32[]{:S(2)}, u32[]{:S(2)}) collective-permute-start(f32[144,256]{1,0:T(8,128)S(1)} %multiply_add_fusion), channel_id=1, source_target_pairs={{0,8},{8,0},{16,24},{24,16},{32,40},{40,32},{48,56},{56,48},{64,72... | collective-permute-start | bytes 442376 | tf_op jit(solution)/shard_map/ppermute | solution.py:50
  135.6 6.5 %collective-permute-start.30 = (bf16[512,256]{1,0:T(8,128)(2,1)S(1)}, bf16[512,256]{1,0:T(8,128)(2,1)S(1)}, u32[]{:S(2)}, u32[]{:S(2)}) collective-permute-start(bf16[512,256]{1,0:T(8,128)(2,1)S(1)} %fusion.18), channel_id=1, source_target_pairs={{0,224},{8,40},{16,240},{24,56},{32,0},{40,72},{48,16},{56,88},{64... | collective-permute-start | bytes 786440 | tf_op jit(solution)/shard_map/ppermute | solution.py:50
  137.5 14.6 %all-to-all-start.2 = ((bf16[8,256,128]{2,1,0:T(8,128)(2,1)}), bf16[8,256,128]{2,1,0:T(8,128)(2,1)S(1)}, u32[]{:S(2)}, u32[]{:S(2)}) async-start(bf16[8,256,128]{2,1,0:T(8,128)(2,1)} %broadcast_in_dim.23), calls=%async_computation.2 | async-start | bytes 1048576 | tf_op jit(solution)/shard_map/all_to_all | solution.py:414
  142.2 4.3 %collective-permute-start.31 = (bf16[512,128]{1,0:T(8,128)(2,1)S(1)}, bf16[512,128]{1,0:T(8,128)(2,1)S(1)}, u32[]{:S(2)}, u32[]{:S(2)}) collective-permute-start(bf16[512,128]{1,0:T(8,128)(2,1)S(1)} %add_convert_fusion), channel_id=1, source_target_pairs={{0,8},{8,0},{16,24},{24,16},{32,40},{40,32},{48,56},{56,48},{64,72... | collective-permute-start | bytes 393224 | tf_op jit(solution)/shard_map/ppermute | solution.py:50

commit v3 on v2

--- a/solution.py
+++ b/solution.py
@@ -370,7 +370,6 @@
     quad2 = quad2.astype(BF)
     far = send(quad2, BACK2)
     quad1 = (line1[:, : 2 * BLK] + got1).astype(BF)
-    near = send(quad1, BACK1)
 
     own = grads.astype(BF)
     own = after(own, quad3, quad4)
@@ -382,6 +381,8 @@
     got = after(got, quad2)
     grads = grads + around + got
 
+    quad1 = after(quad1, grads)
+    near = send(quad1, BACK1)
     other = send((wide_of(far[:, BLK:]) + wide_of(near[:, BLK:])).astype(BF), CORE)
     return final_step(quad0, far, near, other, scaled_t), unfolded(grads)
 

time: 154 us -> 155 us (level)
  waiting for transfers between devices: 27.2 us -> 33.7 us
  starting transfers between devices: 48.9 us -> 43.6 us
    ppermute x32, waiting for transfers between devices: 22.4 us -> 29.1 us  [send(): return lax.ppermute(value, 'layer', perm)]
    ppermute x32, starting transfers between devices: 45.4 us -> 40.1 us  [send(): return lax.ppermute(value, 'layer', perm)]
where the time goes in v3:
time: 155 us; the launch traced here: 154 us
  blocking collectives  49.2 us (32%)
  starting transfers between devices  43.6 us (28%)
  waiting for transfers between devices  33.7 us (22%)
  Pallas kernels  15.9 us (10%)
  matrix products  5.03 us (3%)
  local copies, waits for them, and re-layouts  2.87 us (2%)
  other arithmetic  2.86 us (2%)
    ppermute x32, starting transfers between devices, send(): return lax.ppermute(value, 'layer', perm)  40.1 us
    ppermute x32, waiting for transfers between devices, send(): return lax.ppermute(value, 'layer', perm)  29.1 us
    all_to_all x1, blocking collectives, per_device(): got = lax.all_to_all(payload, 'rep', 0, 0, tiled=True)  24.8 us
    all_to_all x1, blocking collectives, per_device(): everyone = lax.all_to_all(outgoing, 'rep', 0, 0, tiled=True)  24.5 us
    pallas_call x3, Pallas kernels, products(): pl.pallas_call(functools.partial(product_kernel, groups, first), grid=(le...  6.66 us
    pallas_call x1, Pallas kernels, spread_part(): pl.pallas_call(functools.partial(spread_kernel, first), grid_spec=pltpu.P...  5.07 us
    dot_general x7, matrix products, dot(): return jnp.dot(dense[g], piece, preferred_element_type=F32)  5.03 us
    all_to_all x1, waiting for transfers between devices, per_device(): pieces = lax.all_to_all(mine, 'rep', 0, 0, tiled=True)  4.59 us
  transfers between devices with their start and end apart: 33, of which 15 were waited for; matrix products, arithmetic and copies ran while one was open for 7% of the time, Pallas kernels for 6%

profile of v3, /device:TPU:1, one launch (start us, length us, event | category | flops | bytes accessed | tf_op | source)
XLA Modules:
  0.0 154.3 jit_solution(8882106957930607737)
XLA Ops:
  0.6 3.3 %collective-permute-start = (bf16[128,512]{1,0:T(8,128)(2,1)}, bf16[128,512]{1,0:T(8,128)(2,1)S(1)}, u32[]{:S(2)}, u32[]{:S(2)}) collective-permute-start(bf16[128,512]{1,0:T(8,128)(2,1)} %features_ref.1), channel_id=1, source_target_pairs={{0,8},{8,0},{16,24},{24,16},{32,40},{40,32},{48,56},{56,48},{64,72... | collective-permute-start | bytes 393224 | tf_op jit(solution)/shard_map/ppermute | solution.py:50
  4.0 1.0 constant_dynamic-update-slice_fusion.5
  5.2 5.5 %collective-permute-start.4 = (bf16[256,512]{1,0:T(8,128)(2,1)S(1)}, bf16[256,512]{1,0:T(8,128)(2,1)S(1)}, u32[]{:S(2)}, u32[]{:S(2)}) collective-permute-start(bf16[256,512]{1,0:T(8,128)(2,1)S(1)} %get-tuple-element.67), channel_id=1, source_target_pairs={{0,64},{8,200},{16,80},{24,216},{32,96},{40,232},{48,112},{56,248}... | collective-permute-start | bytes 786440 | tf_op jit(solution)/shard_map/ppermute | solution.py:50
  10.6 0.7 fusion.31
  11.6 0.8 compare_select_fusion.1
  12.9 2.1 %collective-permute-start.3 = (bf16[512,512]{1,0:T(8,128)(2,1)S(1)}, bf16[512,512]{1,0:T(8,128)(2,1)S(1)}, u32[]{:S(2)}, u32[]{:S(2)}) collective-permute-start(bf16[512,512]{1,0:T(8,128)(2,1)S(1)} %constant_dynamic-update-slice_fusion.2), channel_id=1, source_target_pairs={{0,32},{8,232},{16,48},{24,248},{32,64},{40,8},{48,80},{56,24},{64... | collective-permute-start | bytes 1572872 | tf_op jit(solution)/shard_map/ppermute | solution.py:50
  15.1 5.1 %shard_map.93 = (bf16[8,1024,512]{2,1,0:T(8,128)(2,1)S(1)}, bf16[8,16,512]{2,1,0:T(8,128)(2,1)S(1)}) custom-call(s32[128]{0:T(128)S(1)} %reshape.18.place_ref, s32[8,16,128,128]{3,2,1,0:T(8,128)} %values_ref.1), custom_call_target="tpu_custom_call" | custom-call | flops 2097152 | bytes 8388608 | tf_op jit(solution)/shard_map/pallas_call | solution.py:94
  20.2 1.2 collective-permute-start.8
  21.4 1.3 collective-permute-start.5
  23.4 0.8 collective-permute-start.11
  24.3 2.4 %collective-permute-done.8 = bf16[128,512]{1,0:T(8,128)(2,1)S(1)} collective-permute-done((bf16[128,512]{1,0:T(8,128)(2,1)S(1)}, bf16[128,512]{1,0:T(8,128)(2,1)S(1)}, u32[]{:S(2)}, u32[]{:S(2)}) %collective-permute-start.8) | collective-permute-done | bytes 131104 | tf_op jit(solution)/shard_map/ppermute | solution.py:50
  27.2 2.3 %collective-permute-done.5 = bf16[256,512]{1,0:T(8,128)(2,1)S(1)} collective-permute-done((bf16[256,512]{1,0:T(8,128)(2,1)S(1)}, bf16[256,512]{1,0:T(8,128)(2,1)S(1)}, u32[]{:S(2)}, u32[]{:S(2)}) %collective-permute-start.5) | collective-permute-done | bytes 262176 | tf_op jit(solution)/shard_map/ppermute | solution.py:50
  29.5 1.1 collective-permute-start.6
  30.6 0.7 fusion.5
  31.6 1.5 collective-permute-start.7
  33.8 0.7 fusion.3
  34.6 0.8 add_add_fusion
  35.9 3.4 %collective-permute-done.12 = bf16[256,512]{1,0:T(8,128)(2,1)S(1)} collective-permute-done((bf16[256,512]{1,0:T(8,128)(2,1)S(1)}, bf16[256,512]{1,0:T(8,128)(2,1)S(1)}, u32[]{:S(2)}, u32[]{:S(2)}) %collective-permute-start.12) | collective-permute-done | bytes 262176 | tf_op jit(solution)/shard_map/ppermute | solution.py:50
  40.1 1.1 collective-permute-start.13
  41.1 0.7 convolution_add_fusion.total_ref
  41.8 0.8 collective-permute-done.13.last_ref
  42.7 1.3 shard_map.94
  44.0 24.8 %all_to_all.15.got_ref = bf16[8,144,512]{2,1,0:T(8,128)(2,1)S(1)} all-to-all(bf16[8,144,512]{2,1,0:T(8,128)(2,1)S(1)} %shard_map.94), channel_id=1, replica_groups=mesh['layer'=32,'rep'=8] {'rep'}, dimensions={0} | all-to-all | bytes 2359296 | tf_op jit(solution)/shard_map/all_to_all | solution.py:408
  68.8 1.0 shard_map.95
  69.8 24.5 %all_to_all.16.left_ref = bf16[8,800,128]{2,1,0:T(8,128)(2,1)S(1)} all-to-all(bf16[8,800,128]{2,1,0:T(8,128)(2,1)S(1)} %get-tuple-element.38), channel_id=1, replica_groups=mesh['layer'=32,'rep'=8] {'rep'}, dimensions={0} | all-to-all | bytes 3276800 | tf_op jit(solution)/shard_map/all_to_all | solution.py:411
  94.3 2.7 %shard_map.96 = (bf16[512,768]{1,0:T(8,128)(2,1)S(1)}, f32[512,768]{1,0:T(8,128)S(1)}, bf16[512,1024]{1,0:T(8,128)(2,1)S(1)}) custom-call(bf16[8,800,128]{2,1,0:T(8,128)(2,1)S(1)} %all_to_all.16.left_ref, bf16[8,1024,512]{2,1,0:T(8,128)(2,1)S(1)} %get-tuple-element.33.dense_ref), custom_call_target="tpu_custom_call" | custom-call | flops 1610612736 | bytes 7864320 | tf_op jit(solution)/shard_map/pallas_call | solution.py:238
  97.0 2.6 %collective-permute-start.15 = (bf16[512,768]{1,0:T(8,128)(2,1)S(1)}, bf16[512,768]{1,0:T(8,128)(2,1)S(1)}, u32[]{:S(2)}, u32[]{:S(2)}) collective-permute-start(bf16[512,768]{1,0:T(8,128)(2,1)S(1)} %get-tuple-element.40), channel_id=1, source_target_pairs={{0,8},{8,0},{16,24},{24,16},{32,40},{40,32},{48,56},{56,48},{64,72... | collective-permute-start | bytes 2359304 | tf_op jit(solution)/shard_map/ppermute | solution.py:50
  99.8 1.6 %shard_map.97 = (bf16[512,512]{1,0:T(8,128)(2,1)S(1)}, f32[512,512]{1,0:T(8,128)S(1)}) custom-call(bf16[512,1024]{1,0:T(8,128)(2,1)S(1)} %get-tuple-element.49.left_ref, bf16[8,1024,512]{2,1,0:T(8,128)(2,1)S(1)} %get-tuple-element.33.dense_ref), custom_call_target="tpu_custom_call" | custom-call | flops 1073741824 | bytes 5242880 | tf_op jit(solution)/shard_map/pallas_call | solution.py:238
  102.4 2.4 %shard_map.99 = (bf16[512,512]{1,0:T(8,128)(2,1)S(1)}, f32[512,512]{1,0:T(8,128)S(1)}, bf16[512,256]{1,0:T(8,128)(2,1)S(1)}, f32[512,256]{1,0:T(8,128)S(1)}) custom-call(bf16[512,1024]{1,0:T(8,128)(2,1)S(1)} %get-tuple-element.49.left_ref, bf16[8,1024,512]{2,1,0:T(8,128)(2,1)S(1)} %get-tuple-element.33.dense_ref), custom_call_target="tpu_custom_call" | custom-call | flops 1610612736 | bytes 7864320 | tf_op jit(solution)/shard_map/pallas_call | solution.py:238
  104.9 1.7 %collective-permute-start.19 = (bf16[512,128]{1,0:T(8,128)(2,1)S(1)}, bf16[512,128]{1,0:T(8,128)(2,1)S(1)}, u32[]{:S(2)}, u32[]{:S(2)}) collective-permute-start(bf16[512,128]{1,0:T(8,128)(2,1)S(1)} %slice.182), channel_id=1, source_target_pairs={{0,16},{8,24},{16,0},{24,8},{32,48},{40,56},{48,32},{56,40},{64,80... | collective-permute-start | bytes 393224 | tf_op jit(solution)/shard_map/ppermute | solution.py:50
  107.4 7.2 %collective-permute-done.19 = bf16[512,128]{1,0:T(8,128)(2,1)S(1)} collective-permute-done((bf16[512,128]{1,0:T(8,128)(2,1)S(1)}, bf16[512,128]{1,0:T(8,128)(2,1)S(1)}, u32[]{:S(2)}, u32[]{:S(2)}) %collective-permute-start.19) | collective-permute-done | bytes 131104 | tf_op jit(solution)/shard_map/ppermute | solution.py:50
  115.0 2.1 %collective-permute-start.18 = (bf16[656,256]{1,0:T(8,128)(2,1)S(1)}, bf16[656,256]{1,0:T(8,128)(2,1)S(1)}, u32[]{:S(2)}, u32[]{:S(2)}) collective-permute-start(bf16[656,256]{1,0:T(8,128)(2,1)S(1)} %pad_maximum_fusion.2), channel_id=1, source_target_pairs={{0,224},{8,40},{16,240},{24,56},{32,0},{40,72},{48,16},{56,88},{64... | collective-permute-start | bytes 1007624 | tf_op jit(solution)/shard_map/ppermute | solution.py:50
  117.2 1.5 collective-permute-start.21
  118.7 4.2 %collective-permute-start.22 = (bf16[144,256]{1,0:T(8,128)(2,1)S(1)}, bf16[144,256]{1,0:T(8,128)(2,1)S(1)}, u32[]{:S(2)}, u32[]{:S(2)}) collective-permute-start(bf16[144,256]{1,0:T(8,128)(2,1)S(1)} %fusion.27), channel_id=1, source_target_pairs={{0,128},{8,136},{16,144},{24,152},{32,160},{40,168},{48,176},{56,1... | collective-permute-start | bytes 221192 | tf_op jit(solution)/shard_map/ppermute | solution.py:50
  123.1 2.3 %collective-permute-done.20 = bf16[800,128]{1,0:T(8,128)(2,1)S(1)} collective-permute-done((bf16[800,128]{1,0:T(8,128)(2,1)S(1)}, bf16[800,128]{1,0:T(8,128)(2,1)S(1)}, u32[]{:S(2)}, u32[]{:S(2)}) %collective-permute-start.20) | collective-permute-done | bytes 204832 | tf_op jit(solution)/shard_map/ppermute | solution.py:50
  125.3 1.2 collective-permute-start.29
  127.1 1.4 collective-permute-done.21
  128.5 2.7 %collective-permute-done.22 = bf16[144,256]{1,0:T(8,128)(2,1)S(1)} collective-permute-done((bf16[144,256]{1,0:T(8,128)(2,1)S(1)}, bf16[144,256]{1,0:T(8,128)(2,1)S(1)}, u32[]{:S(2)}, u32[]{:S(2)}) %collective-permute-start.22) | collective-permute-done | bytes 73760 | tf_op jit(solution)/shard_map/ppermute | solution.py:50
  131.2 2.1 %collective-permute-start.23 = (f32[144,256]{1,0:T(8,128)S(1)}, f32[144,256]{1,0:T(8,128)S(1)}, u32[]{:S(2)}, u32[]{:S(2)}) collective-permute-start(f32[144,256]{1,0:T(8,128)S(1)} %multiply_add_fusion), channel_id=1, source_target_pairs={{0,8},{8,0},{16,24},{24,16},{32,40},{40,32},{48,56},{56,48},{64,72... | collective-permute-start | bytes 442376 | tf_op jit(solution)/shard_map/ppermute | solution.py:50
  133.3 1.8 %collective-permute-start.28 = (bf16[512,256]{1,0:T(8,128)(2,1)S(1)}, bf16[512,256]{1,0:T(8,128)(2,1)S(1)}, u32[]{:S(2)}, u32[]{:S(2)}) collective-permute-start(bf16[512,256]{1,0:T(8,128)(2,1)S(1)} %pad_maximum_fusion.4), channel_id=1, source_target_pairs={{0,192},{8,72},{16,208},{24,88},{32,224},{40,104},{48,240},{56,120... | collective-permute-start | bytes 786440 | tf_op jit(solution)/shard_map/ppermute | solution.py:50
  135.2 2.1 %collective-permute-start.30 = (bf16[512,256]{1,0:T(8,128)(2,1)S(1)}, bf16[512,256]{1,0:T(8,128)(2,1)S(1)}, u32[]{:S(2)}, u32[]{:S(2)}) collective-permute-start(bf16[512,256]{1,0:T(8,128)(2,1)S(1)} %fusion.18), channel_id=1, source_target_pairs={{0,224},{8,40},{16,240},{24,56},{32,0},{40,72},{48,16},{56,88},{64... | collective-permute-start | bytes 786440 | tf_op jit(solution)/shard_map/ppermute | solution.py:50
  137.3 0.9 broadcast_in_dim.23
  138.2 3.5 %all-to-all-start.2 = ((bf16[8,256,128]{2,1,0:T(8,128)(2,1)}), bf16[8,256,128]{2,1,0:T(8,128)(2,1)S(1)}, u32[]{:S(2)}, u32[]{:S(2)}) async-start(bf16[8,256,128]{2,1,0:T(8,128)(2,1)} %broadcast_in_dim.23), calls=%async_computation.2 | async-start | bytes 1048576 | tf_op jit(solution)/shard_map/all_to_all | solution.py:415
  141.7 4.7 %collective-permute-done.30.near_ref = bf16[512,256]{1,0:T(8,128)(2,1)S(1)} collective-permute-done((bf16[512,256]{1,0:T(8,128)(2,1)S(1)}, bf16[512,256]{1,0:T(8,128)(2,1)S(1)}, u32[]{:S(2)}, u32[]{:S(2)}) %collective-permute-start.30) | collective-permute-done | bytes 262176 | tf_op jit(solution)/shard_map/ppermute | solution.py:50
  147.1 0.8 collective-permute-done.31.other_ref
  147.9 0.8 shard_map.100
  148.7 4.6 %all-to-all-done.2.pieces_ref = bf16[8,256,128]{2,1,0:T(8,128)(2,1)S(1)} async-done(((bf16[8,256,128]{2,1,0:T(8,128)(2,1)}), bf16[8,256,128]{2,1,0:T(8,128)(2,1)S(1)}, u32[]{:S(2)}, u32[]{:S(2)}) %all-to-all-start.2) | async-done | bytes 524320 | tf_op jit(solution)/shard_map/all_to_all | solution.py:415
  153.3 1.0 shard_map.98
  (92 shorter events, 8.9 us)
Async XLA Ops:
  0.6 4.5 %collective-permute-start = (bf16[128,512]{1,0:T(8,128)(2,1)}, bf16[128,512]{1,0:T(8,128)(2,1)S(1)}, u32[]{:S(2)}, u32[]{:S(2)}) collective-permute-start(bf16[128,512]{1,0:T(8,128)(2,1)} %features_ref.1), channel_id=1, source_target_pairs={{0,8},{8,0},{16,24},{24,16},{32,40},{40,32},{48,56},{56,48},{64,72... | collective-permute-start | bytes 393224 | tf_op jit(solution)/shard_map/ppermute | solution.py:50
  4.0 7.5 %collective-permute-start.1 = (bf16[128,512]{1,0:T(8,128)(2,1)}, bf16[128,512]{1,0:T(8,128)(2,1)S(1)}, u32[]{:S(2)}, u32[]{:S(2)}) collective-permute-start(bf16[128,512]{1,0:T(8,128)(2,1)} %features_ref.1), channel_id=1, source_target_pairs={{0,16},{8,24},{16,0},{24,8},{32,48},{40,56},{48,32},{56,40},{64,80... | collective-permute-start | bytes 393224 | tf_op jit(solution)/shard_map/ppermute | solution.py:50
  5.2 15.0 %collective-permute-start.4 = (bf16[256,512]{1,0:T(8,128)(2,1)S(1)}, bf16[256,512]{1,0:T(8,128)(2,1)S(1)}, u32[]{:S(2)}, u32[]{:S(2)}) collective-permute-start(bf16[256,512]{1,0:T(8,128)(2,1)S(1)} %get-tuple-element.67), channel_id=1, source_target_pairs={{0,64},{8,200},{16,80},{24,216},{32,96},{40,232},{48,112},{56,248}... | collective-permute-start | bytes 786440 | tf_op jit(solution)/shard_map/ppermute | solution.py:50
  11.5 1.4 collective-permute-start.2
  12.9 18.7 %collective-permute-start.3 = (bf16[512,512]{1,0:T(8,128)(2,1)S(1)}, bf16[512,512]{1,0:T(8,128)(2,1)S(1)}, u32[]{:S(2)}, u32[]{:S(2)}) collective-permute-start(bf16[512,512]{1,0:T(8,128)(2,1)S(1)} %constant_dynamic-update-slice_fusion.2), channel_id=1, source_target_pairs={{0,32},{8,232},{16,48},{24,248},{32,64},{40,8},{48,80},{56,24},{64... | collective-permute-start | bytes 1572872 | tf_op jit(solution)/shard_map/ppermute | solution.py:50
  20.2 6.5 %collective-permute-start.8 = (bf16[128,512]{1,0:T(8,128)(2,1)S(1)}, bf16[128,512]{1,0:T(8,128)(2,1)S(1)}, u32[]{:S(2)}, u32[]{:S(2)}) collective-permute-start(bf16[128,512]{1,0:T(8,128)(2,1)S(1)} %slice.171), channel_id=1, source_target_pairs={{0,64},{8,200},{16,80},{24,216},{32,96},{40,232},{48,112},{56,248}... | collective-permute-start | bytes 393224 | tf_op jit(solution)/shard_map/ppermute | solution.py:50
  21.4 8.0 %collective-permute-start.5 = (bf16[256,512]{1,0:T(8,128)(2,1)S(1)}, bf16[256,512]{1,0:T(8,128)(2,1)S(1)}, u32[]{:S(2)}, u32[]{:S(2)}) collective-permute-start(bf16[256,512]{1,0:T(8,128)(2,1)S(1)} %collective-permute-done.4), channel_id=1, source_target_pairs={{0,16},{8,24},{16,0},{24,8},{32,48},{40,56},{48,32},{56,40},{64,80... | collective-permute-start | bytes 786440 | tf_op jit(solution)/shard_map/ppermute | solution.py:50
  23.4 7.8 %collective-permute-start.11 = (bf16[256,512]{1,0:T(8,128)(2,1)S(1)}, bf16[256,512]{1,0:T(8,128)(2,1)S(1)}, u32[]{:S(2)}, u32[]{:S(2)}) collective-permute-start(bf16[256,512]{1,0:T(8,128)(2,1)S(1)} %collective-permute-done.4), channel_id=1, source_target_pairs={{0,32},{8,232},{16,48},{24,248},{32,64},{40,8},{48,80},{56,24},{64... | collective-permute-start | bytes 786440 | tf_op jit(solution)/shard_map/ppermute | solution.py:50
  26.7 4.9 %collective-permute-start.9 = (bf16[128,512]{1,0:T(8,128)(2,1)S(1)}, bf16[128,512]{1,0:T(8,128)(2,1)S(1)}, u32[]{:S(2)}, u32[]{:S(2)}) collective-permute-start(bf16[128,512]{1,0:T(8,128)(2,1)S(1)} %collective-permute-done.8), channel_id=1, source_target_pairs={{0,16},{8,24},{16,0},{24,8},{32,48},{40,56},{48,32},{56,40},{64,80... | collective-permute-start | bytes 393224 | tf_op jit(solution)/shard_map/ppermute | solution.py:50
  29.5 4.3 %collective-permute-start.6 = (bf16[512,512]{1,0:T(8,128)(2,1)S(1)}, bf16[512,512]{1,0:T(8,128)(2,1)S(1)}, u32[]{:S(2)}, u32[]{:S(2)}) collective-permute-start(bf16[512,512]{1,0:T(8,128)(2,1)S(1)} %constant_dynamic-update-slice_fusion.6), channel_id=1, source_target_pairs={{0,8},{8,0},{16,24},{24,16},{32,40},{40,32},{48,56},{56,48},{64,72... | collective-permute-start | bytes 1572872 | tf_op jit(solution)/shard_map/ppermute | solution.py:50
  31.3 8.0 %collective-permute-start.12 = (bf16[256,512]{1,0:T(8,128)(2,1)S(1)}, bf16[256,512]{1,0:T(8,128)(2,1)S(1)}, u32[]{:S(2)}, u32[]{:S(2)}) collective-permute-start(bf16[256,512]{1,0:T(8,128)(2,1)S(1)} %collective-permute-done.11), channel_id=1, source_target_pairs={{0,16},{8,24},{16,0},{24,8},{32,48},{40,56},{48,32},{56,40},{64,80... | collective-permute-start | bytes 786440 | tf_op jit(solution)/shard_map/ppermute | solution.py:50
  31.6 3.0 %collective-permute-start.7 = (bf16[512,512]{1,0:T(8,128)(2,1)S(1)}, bf16[512,512]{1,0:T(8,128)(2,1)S(1)}, u32[]{:S(2)}, u32[]{:S(2)}) collective-permute-start(bf16[512,512]{1,0:T(8,128)(2,1)S(1)} %collective-permute-done.3), channel_id=1, source_target_pairs={{0,8},{8,0},{16,24},{24,16},{32,40},{40,32},{48,56},{56,48},{64,72... | collective-permute-start | bytes 1572872 | tf_op jit(solution)/shard_map/ppermute | solution.py:50
  35.5 3.9 %collective-permute-start.10 = (bf16[256,512]{1,0:T(8,128)(2,1)S(1)}, bf16[256,512]{1,0:T(8,128)(2,1)S(1)}, u32[]{:S(2)}, u32[]{:S(2)}) collective-permute-start(bf16[256,512]{1,0:T(8,128)(2,1)S(1)} %pad_maximum_fusion.3), channel_id=1, source_target_pairs={{0,8},{8,0},{16,24},{24,16},{32,40},{40,32},{48,56},{56,48},{64,72... | collective-permute-start | bytes 786440 | tf_op jit(solution)/shard_map/ppermute | solution.py:50
  40.1 2.6 %collective-permute-start.13 = (bf16[512,512]{1,0:T(8,128)(2,1)S(1)}, bf16[512,512]{1,0:T(8,128)(2,1)S(1)}, u32[]{:S(2)}, u32[]{:S(2)}) collective-permute-start(bf16[512,512]{1,0:T(8,128)(2,1)S(1)} %pad_maximum_fusion), channel_id=1, source_target_pairs={{0,8},{8,0},{16,24},{24,16},{32,40},{40,32},{48,56},{56,48},{64,72... | collective-permute-start | bytes 1572872 | tf_op jit(solution)/shard_map/ppermute | solution.py:50
  43.9 24.8 %copy-start = (bf16[512,512]{1,0:T(8,128)(2,1)S(1)}, bf16[512,512]{1,0:T(8,128)(2,1)}, u32[]{:S(2)}) copy-start(bf16[512,512]{1,0:T(8,128)(2,1)} %weight_ref.1) | copy-start | bytes 1572868
  43.9 24.8 %copy-start.1 = (bf16[128,512]{1,0:T(8,128)(2,1)S(1)}, bf16[128,512]{1,0:T(8,128)(2,1)}, u32[]{:S(2)}) copy-start(bf16[128,512]{1,0:T(8,128)(2,1)} %features_ref.1) | copy-start | bytes 393220
  43.9 24.8 %copy-start.2 = (bf16[128,512]{1,0:T(8,128)(2,1)S(1)}, bf16[128,512]{1,0:T(8,128)(2,1)}, u32[]{:S(2)}) copy-start(bf16[128,512]{1,0:T(8,128)(2,1)} %cotangent_ref.1) | copy-start | bytes 393220
  44.0 24.8 %copy-start.3 = (f32[512]{0:T(512)S(1)}, f32[512]{0:T(512)}, u32[]{:S(2)}) copy-start(f32[512]{0:T(512)} %param.10) | copy-start | bytes 6148
  97.0 5.0 %collective-permute-start.15 = (bf16[512,768]{1,0:T(8,128)(2,1)S(1)}, bf16[512,768]{1,0:T(8,128)(2,1)S(1)}, u32[]{:S(2)}, u32[]{:S(2)}) collective-permute-start(bf16[512,768]{1,0:T(8,128)(2,1)S(1)} %get-tuple-element.40), channel_id=1, source_target_pairs={{0,8},{8,0},{16,24},{24,16},{32,40},{40,32},{48,56},{56,48},{64,72... | collective-permute-start | bytes 2359304 | tf_op jit(solution)/shard_map/ppermute | solution.py:50
  99.7 2.3 %collective-permute-start.14 = (bf16[288,128]{1,0:T(8,128)(2,1)S(1)}, bf16[288,128]{1,0:T(8,128)(2,1)S(1)}, u32[]{:S(2)}, u32[]{:S(2)}) collective-permute-start(bf16[288,128]{1,0:T(8,128)(2,1)S(1)} %convert_element_type.92), channel_id=1, source_target_pairs={{0,8},{8,0},{16,24},{24,16},{32,40},{40,32},{48,56},{56,48},{64,72... | collective-permute-start | bytes 221192 | tf_op jit(solution)/shard_map/ppermute | solution.py:50
  101.4 3.5 %collective-permute-start.17 = (bf16[512,512]{1,0:T(8,128)(2,1)S(1)}, bf16[512,512]{1,0:T(8,128)(2,1)S(1)}, u32[]{:S(2)}, u32[]{:S(2)}) collective-permute-start(bf16[512,512]{1,0:T(8,128)(2,1)S(1)} %get-tuple-element.43), channel_id=1, source_target_pairs={{0,8},{8,0},{16,24},{24,16},{32,40},{40,32},{48,56},{56,48},{64,72... | collective-permute-start | bytes 1572872 | tf_op jit(solution)/shard_map/ppermute | solution.py:50
  102.3 12.5 %collective-permute-start.16 = (bf16[656,256]{1,0:T(8,128)(2,1)S(1)}, bf16[656,256]{1,0:T(8,128)(2,1)S(1)}, u32[]{:S(2)}, u32[]{:S(2)}) collective-permute-start(bf16[656,256]{1,0:T(8,128)(2,1)S(1)} %pad_maximum_fusion.1), channel_id=1, source_target_pairs={{0,16},{8,24},{16,0},{24,8},{32,48},{40,56},{48,32},{56,40},{64,80... | collective-permute-start | bytes 1007624 | tf_op jit(solution)/shard_map/ppermute | solution.py:50
  104.8 13.9 %collective-permute-start.26 = (bf16[512,512]{1,0:T(8,128)(2,1)S(1)}, bf16[512,512]{1,0:T(8,128)(2,1)S(1)}, u32[]{:S(2)}, u32[]{:S(2)}) collective-permute-start(bf16[512,512]{1,0:T(8,128)(2,1)S(1)} %get-tuple-element.53), channel_id=1, source_target_pairs={{0,8},{8,0},{16,24},{24,16},{32,40},{40,32},{48,56},{56,48},{64,72... | collective-permute-start | bytes 1572872 | tf_op jit(solution)/shard_map/ppermute | solution.py:50
  104.9 9.7 %collective-permute-start.19 = (bf16[512,128]{1,0:T(8,128)(2,1)S(1)}, bf16[512,128]{1,0:T(8,128)(2,1)S(1)}, u32[]{:S(2)}, u32[]{:S(2)}) collective-permute-start(bf16[512,128]{1,0:T(8,128)(2,1)S(1)} %slice.182), channel_id=1, source_target_pairs={{0,16},{8,24},{16,0},{24,8},{32,48},{40,56},{48,32},{56,40},{64,80... | collective-permute-start | bytes 393224 | tf_op jit(solution)/shard_map/ppermute | solution.py:50
  106.6 8.0 %collective-permute-start.25 = (bf16[512,256]{1,0:T(8,128)(2,1)S(1)}, bf16[512,256]{1,0:T(8,128)(2,1)S(1)}, u32[]{:S(2)}, u32[]{:S(2)}) collective-permute-start(bf16[512,256]{1,0:T(8,128)(2,1)S(1)} %get-tuple-element.51), channel_id=1, source_target_pairs={{0,8},{8,0},{16,24},{24,16},{32,40},{40,32},{48,56},{56,48},{64,72... | collective-permute-start | bytes 786440 | tf_op jit(solution)/shard_map/ppermute | solution.py:50
  107.3 19.2 %collective-permute-start.24 = (bf16[512,256]{1,0:T(8,128)(2,1)S(1)}, bf16[512,256]{1,0:T(8,128)(2,1)S(1)}, u32[]{:S(2)}, u32[]{:S(2)}) collective-permute-start(bf16[512,256]{1,0:T(8,128)(2,1)S(1)} %slice.264), channel_id=1, source_target_pairs={{0,16},{8,24},{16,0},{24,8},{32,48},{40,56},{48,32},{56,40},{64,80... | collective-permute-start | bytes 786440 | tf_op jit(solution)/shard_map/ppermute | solution.py:50
  115.0 11.9 %collective-permute-start.18 = (bf16[656,256]{1,0:T(8,128)(2,1)S(1)}, bf16[656,256]{1,0:T(8,128)(2,1)S(1)}, u32[]{:S(2)}, u32[]{:S(2)}) collective-permute-start(bf16[656,256]{1,0:T(8,128)(2,1)S(1)} %pad_maximum_fusion.2), channel_id=1, source_target_pairs={{0,224},{8,40},{16,240},{24,56},{32,0},{40,72},{48,16},{56,88},{64... | collective-permute-start | bytes 1007624 | tf_op jit(solution)/shard_map/ppermute | solution.py:50
  117.1 8.2 %collective-permute-start.20 = (bf16[800,128]{1,0:T(8,128)(2,1)S(1)}, bf16[800,128]{1,0:T(8,128)(2,1)S(1)}, u32[]{:S(2)}, u32[]{:S(2)}) collective-permute-start(bf16[800,128]{1,0:T(8,128)(2,1)S(1)} %pad_maximum_fusion.5), channel_id=1, source_target_pairs={{0,192},{8,72},{16,208},{24,88},{32,224},{40,104},{48,240},{56,120... | collective-permute-start | bytes 614408 | tf_op jit(solution)/shard_map/ppermute | solution.py:50
  117.2 11.2 %collective-permute-start.21 = (bf16[144,256]{1,0:T(8,128)(2,1)S(1)}, bf16[144,256]{1,0:T(8,128)(2,1)S(1)}, u32[]{:S(2)}, u32[]{:S(2)}) collective-permute-start(bf16[144,256]{1,0:T(8,128)(2,1)S(1)} %fusion.27), channel_id=1, source_target_pairs={{0,160},{8,104},{16,176},{24,120},{32,192},{40,136},{48,208},{56,1... | collective-permute-start | bytes 221192 | tf_op jit(solution)/shard_map/ppermute | solution.py:50
  118.7 12.4 %collective-permute-start.22 = (bf16[144,256]{1,0:T(8,128)(2,1)S(1)}, bf16[144,256]{1,0:T(8,128)(2,1)S(1)}, u32[]{:S(2)}, u32[]{:S(2)}) collective-permute-start(bf16[144,256]{1,0:T(8,128)(2,1)S(1)} %fusion.27), channel_id=1, source_target_pairs={{0,128},{8,136},{16,144},{24,152},{32,160},{40,168},{48,176},{56,1... | collective-permute-start | bytes 221192 | tf_op jit(solution)/shard_map/ppermute | solution.py:50
  125.3 9.8 %collective-permute-start.29 = (bf16[512,256]{1,0:T(8,128)(2,1)S(1)}, bf16[512,256]{1,0:T(8,128)(2,1)S(1)}, u32[]{:S(2)}, u32[]{:S(2)}) collective-permute-start(bf16[512,256]{1,0:T(8,128)(2,1)S(1)} %slice.263), channel_id=1, source_target_pairs={{0,16},{8,24},{16,0},{24,8},{32,48},{40,56},{48,32},{56,40},{64,80... | collective-permute-start | bytes 786440 | tf_op jit(solution)/shard_map/ppermute | solution.py:50
  126.5 15.2 %collective-permute-start.27 = (bf16[512,128]{1,0:T(8,128)(2,1)S(1)}, bf16[512,128]{1,0:T(8,128)(2,1)S(1)}, u32[]{:S(2)}, u32[]{:S(2)}) collective-permute-start(bf16[512,128]{1,0:T(8,128)(2,1)S(1)} %slice.265), channel_id=1, source_target_pairs={{0,16},{8,24},{16,0},{24,8},{32,48},{40,56},{48,32},{56,40},{64,80... | collective-permute-start | bytes 393224 | tf_op jit(solution)/shard_map/ppermute | solution.py:50
  131.2 4.0 %collective-permute-start.23 = (f32[144,256]{1,0:T(8,128)S(1)}, f32[144,256]{1,0:T(8,128)S(1)}, u32[]{:S(2)}, u32[]{:S(2)}) collective-permute-start(f32[144,256]{1,0:T(8,128)S(1)} %multiply_add_fusion), channel_id=1, source_target_pairs={{0,8},{8,0},{16,24},{24,16},{32,40},{40,32},{48,56},{56,48},{64,72... | collective-permute-start | bytes 442376 | tf_op jit(solution)/shard_map/ppermute | solution.py:50
  133.3 8.4 %collective-permute-start.28 = (bf16[512,256]{1,0:T(8,128)(2,1)S(1)}, bf16[512,256]{1,0:T(8,128)(2,1)S(1)}, u32[]{:S(2)}, u32[]{:S(2)}) collective-permute-start(bf16[512,256]{1,0:T(8,128)(2,1)S(1)} %pad_maximum_fusion.4), channel_id=1, source_target_pairs={{0,192},{8,72},{16,208},{24,88},{32,224},{40,104},{48,240},{56,120... | collective-permute-start | bytes 786440 | tf_op jit(solution)/shard_map/ppermute | solution.py:50
  135.2 11.2 %collective-permute-start.30 = (bf16[512,256]{1,0:T(8,128)(2,1)S(1)}, bf16[512,256]{1,0:T(8,128)(2,1)S(1)}, u32[]{:S(2)}, u32[]{:S(2)}) collective-permute-start(bf16[512,256]{1,0:T(8,128)(2,1)S(1)} %fusion.18), channel_id=1, source_target_pairs={{0,224},{8,40},{16,240},{24,56},{32,0},{40,72},{48,16},{56,88},{64... | collective-permute-start | bytes 786440 | tf_op jit(solution)/shard_map/ppermute | solution.py:50
  138.2 15.1 %all-to-all-start.2 = ((bf16[8,256,128]{2,1,0:T(8,128)(2,1)}), bf16[8,256,128]{2,1,0:T(8,128)(2,1)S(1)}, u32[]{:S(2)}, u32[]{:S(2)}) async-start(bf16[8,256,128]{2,1,0:T(8,128)(2,1)} %broadcast_in_dim.23), calls=%async_computation.2 | async-start | bytes 1048576 | tf_op jit(solution)/shard_map/all_to_all | solution.py:415
  146.4 1.4 collective-permute-start.31
